TPU v7x, 256 devices: a whole 4x4x8 slice. The times are simulated.
256 devices in a mesh: rows: 64 (over z, y, x_hi), feat: 4 (over x_lo, core).
Axes of the slice: x: 4 (x_hi: 2, x_lo: 2; x = x_hi * 2 + x_lo), y: 4, z: 8, core: 2. Of those that a mesh axis runs over, the one named last changes fastest.
Arguments:
- query_grads: bfloat16 [1024, 8192], P('rows', 'feat'), may hold values from -300 to 300
- train_grads: bfloat16 [65536, 8192], P('rows', 'feat'), may hold values from -300 to 300
- precond: bfloat16 [32, 256, 256], P('feat'), may hold values from -1.1 to 4.1, as said below
Outputs:
- scores: float32 [1024, 65536], P(None, ('rows', 'feat'))
Inputs may be any that keep to these rules, and one draw needn't show every extreme that they name: `precond`: each block is symmetric.
All inputs are finite; a program needn't handle non-finite values.
Results may differ from a plain program's by a relative error of at most 0.003.
Values may be sent and summed in bfloat16 or wider, within the bound.
No kernel may reach another device: no remote copies, remote signals or barrier semaphores. Data moves between devices by JAX's collectives and lax.ppermute only.
A program may use at most 64 MiB of HBM per device.

v0:
```python
import math

import jax
import jax.numpy as jnp
from jax import lax
from jax.sharding import PartitionSpec as P

F = 8192


eps = 1e-06


def from_behind(value, axis, steps):
    count = lax.axis_size(axis)
    pairs = [(source, (source + steps) % count) for source in range(count)]
    return lax.ppermute(value, axis, pairs)


def on_device(query_grads, train_grads, precond):
    total_rows = lax.axis_size("rows")
    feat_count = lax.axis_size("feat")
    blocks_here = precond.shape[0]
    block_size = precond.shape[1]
    query_rows = query_grads.shape[0]
    train_rows = train_grads.shape[0]
    factor = math.sqrt(F)
    shaped = query_grads.reshape(query_rows, blocks_here, block_size)
    conditioned = jnp.einsum("qkb,kbc->qkc", shaped, precond, preferred_element_type=jnp.float32)
    conditioned = conditioned.reshape(query_rows, blocks_here * block_size)
    query_sums = lax.psum(jnp.sum(conditioned * conditioned, axis=1), "feat")
    query_scale = lax.all_gather(1.0 / jnp.sqrt(query_sums + eps), "rows", axis=0, tiled=True)
    rounded = conditioned.astype(jnp.bfloat16)
    train_squares = jnp.sum(jnp.square(train_grads.astype(jnp.float32)), axis=1)
    train_sums = lax.psum_scatter(train_squares, "feat", scatter_dimension=0, tiled=True)
    train_scale = 1.0 / jnp.sqrt(train_sums + eps)

    def contract(left):
        return lax.dot_general(
            left, train_grads, (((1,), (1,)), ((), ())), preferred_element_type=jnp.float32
        )

    def finish(reduced, scale):
        return reduced * scale[:, None] * train_scale[None, :] * factor

    position = lax.axis_index("rows")

    def one_block(scores, current, stride):
        source = (position - stride) % total_rows
        reduced = lax.psum_scatter(contract(current), "feat", scatter_dimension=1, tiled=True)
        scale = lax.dynamic_slice_in_dim(query_scale, source * query_rows, query_rows)
        return lax.dynamic_update_slice_in_dim(
            scores, finish(reduced, scale), source * query_rows, 0
        )

    scores = jnp.zeros((query_rows * total_rows, train_rows // feat_count), jnp.float32)
    scores = one_block(scores, rounded, 0)

    def advance(stride, state):
        scores, current = state
        current = from_behind(current, "rows", 1)
        return (one_block(scores, current, stride), current)

    scores, current = lax.fori_loop(1, total_rows, advance, (scores, rounded))
    return scores


def solution(mesh):
    in_specs = (P("rows", "feat"), P("rows", "feat"), P("feat", None, None))
    out_specs = P(None, ("rows", "feat"))
    return jax.shard_map(
        on_device, mesh=mesh, in_specs=in_specs, out_specs=out_specs, check_vma=False
    )
```

profile of v0, /device:TPU:8, one launch (start us, length us, event | category | flops | bytes accessed | tf_op | source)
XLA Modules:
  0.0 2172.0 jit_solution(9639153628882512126)
XLA Ops:
  25.8 182.5 %all-reduce = f32[1024]{0:T(1024)S(1)} all-reduce(f32[1024]{0:T(1024)S(1)} %rsqrt_dynamic-update-slice_fusion), channel_id=1, replica_groups=mesh['rows'=64,'feat'=4] {'rows'}, use_global_device_ids=true, to_apply=%add | all-reduce | flops 1024 | bytes 8192
  209.3 1954.9 %while.17 = (s32[]{:T(128)}, f32[1024,256]{1,0:T(8,128)S(1)}, bf16[16,2048]{1,0:T(8,128)(2,1)S(1)}, bf16[1024,2048]{1,0:T(8,128)(2,1)}, s32[]{:T(128)}, /*index=...) while((s32[]{:T(128)}, f32[1024,256]{1,0:T(8,128)S(1)}, ...), condition=%wide.region_7.8_spmd, body=%wide.region_5.7_spmd.sunk | while | flops 67121168 | bytes 4999164 | solution.py:64
  250.8 19.3 reduce-scatter.5.cloned.1.call-done
  281.9 19.3 reduce-scatter.5.cloned.1.call-done
  312.9 19.3 reduce-scatter.5.cloned.1.call-done
  344.0 19.3 reduce-scatter.5.cloned.1.call-done
  406.0 19.3 reduce-scatter.5.cloned.1.call-done
  437.1 19.3 reduce-scatter.5.cloned.1.call-done
  499.2 19.3 reduce-scatter.5.cloned.1.call-done
  530.2 19.3 reduce-scatter.5.cloned.1.call-done
  592.3 19.3 reduce-scatter.5.cloned.1.call-done
  623.4 19.3 reduce-scatter.5.cloned.1.call-done
  654.4 19.3 reduce-scatter.5.cloned.1.call-done
  685.5 19.3 reduce-scatter.5.cloned.1.call-done
  716.5 19.3 reduce-scatter.5.cloned.1.call-done
  747.6 19.3 reduce-scatter.5.cloned.1.call-done
  809.6 19.3 reduce-scatter.5.cloned.1.call-done
  840.7 19.3 reduce-scatter.5.cloned.1.call-done
  871.7 19.3 reduce-scatter.5.cloned.1.call-done
  902.8 19.4 reduce-scatter.5.cloned.1.call-done
  933.9 19.3 reduce-scatter.5.cloned.1.call-done
  964.9 19.3 reduce-scatter.5.cloned.1.call-done
  995.9 19.3 reduce-scatter.5.cloned.1.call-done
  1027.0 19.3 reduce-scatter.5.cloned.1.call-done
  1058.0 19.3 reduce-scatter.5.cloned.1.call-done
  1089.0 19.3 reduce-scatter.5.cloned.1.call-done
  1120.1 19.3 reduce-scatter.5.cloned.1.call-done
  1151.1 19.3 reduce-scatter.5.cloned.1.call-done
  1213.2 19.3 reduce-scatter.5.cloned.1.call-done
  1306.2 19.3 reduce-scatter.5.cloned.1.call-done
  1337.3 19.3 reduce-scatter.5.cloned.1.call-done
  1399.3 19.3 reduce-scatter.5.cloned.1.call-done
  1430.4 19.3 reduce-scatter.5.cloned.1.call-done
  1492.4 19.3 reduce-scatter.5.cloned.1.call-done
  1554.5 19.3 reduce-scatter.5.cloned.1.call-done
  1616.5 19.3 reduce-scatter.5.cloned.1.call-done
  1678.6 19.3 reduce-scatter.5.cloned.1.call-done
  1709.6 19.3 reduce-scatter.5.cloned.1.call-done
  1740.7 19.3 reduce-scatter.5.cloned.1.call-done
  1771.7 19.3 reduce-scatter.5.cloned.1.call-done
  1833.8 19.3 reduce-scatter.5.cloned.1.call-done
  1864.8 19.3 reduce-scatter.5.cloned.1.call-done
  1895.8 19.3 reduce-scatter.5.cloned.1.call-done
  1926.9 19.3 reduce-scatter.5.cloned.1.call-done
  1957.9 19.3 reduce-scatter.5.cloned.1.call-done
  2019.9 19.3 reduce-scatter.5.cloned.1.call-done
  2051.0 19.3 reduce-scatter.5.cloned.1.call-done
  2144.1 19.3 reduce-scatter.5.cloned.1.call-done
  (545 shorter events, 1083.5 us)
Async XLA Ops:
  6.5 201.9 %reduce-scatter.3.cloned.1.call-start = ((), (), s32[]{:S(2)}) async-start(), calls=%async_computation.2 | async-start | bytes 81920 | tf_op jit(solution)/shard_map/reduce_scatter | solution.py:50
  239.9 30.3 %reduce-scatter.5.cloned.1.call-start = ((), (), s32[]{:S(2)}) async-start(), calls=%async_computation.3 | async-start | bytes 81920 | tf_op jit(solution)/shard_map/while/body/eval_jaxpr/reduce_scatter | solution.py:50
  271.0 30.3 %reduce-scatter.5.cloned.1.call-start = ((), (), s32[]{:S(2)}) async-start(), calls=%async_computation.3 | async-start | bytes 81920 | tf_op jit(solution)/shard_map/while/body/eval_jaxpr/reduce_scatter | solution.py:50
  302.0 30.2 %reduce-scatter.5.cloned.1.call-start = ((), (), s32[]{:S(2)}) async-start(), calls=%async_computation.3 | async-start | bytes 81920 | tf_op jit(solution)/shard_map/while/body/eval_jaxpr/reduce_scatter | solution.py:50
  333.1 30.2 %reduce-scatter.5.cloned.1.call-start = ((), (), s32[]{:S(2)}) async-start(), calls=%async_computation.3 | async-start | bytes 81920 | tf_op jit(solution)/shard_map/while/body/eval_jaxpr/reduce_scatter | solution.py:50
  395.1 30.3 %reduce-scatter.5.cloned.1.call-start = ((), (), s32[]{:S(2)}) async-start(), calls=%async_computation.3 | async-start | bytes 81920 | tf_op jit(solution)/shard_map/while/body/eval_jaxpr/reduce_scatter | solution.py:50
  426.1 30.3 %reduce-scatter.5.cloned.1.call-start = ((), (), s32[]{:S(2)}) async-start(), calls=%async_computation.3 | async-start | bytes 81920 | tf_op jit(solution)/shard_map/while/body/eval_jaxpr/reduce_scatter | solution.py:50
  457.2 30.2 %reduce-scatter.5.cloned.1.call-start = ((), (), s32[]{:S(2)}) async-start(), calls=%async_computation.3 | async-start | bytes 81920 | tf_op jit(solution)/shard_map/while/body/eval_jaxpr/reduce_scatter | solution.py:50
  488.2 30.3 %reduce-scatter.5.cloned.1.call-start = ((), (), s32[]{:S(2)}) async-start(), calls=%async_computation.3 | async-start | bytes 81920 | tf_op jit(solution)/shard_map/while/body/eval_jaxpr/reduce_scatter | solution.py:50
  519.3 30.3 %reduce-scatter.5.cloned.1.call-start = ((), (), s32[]{:S(2)}) async-start(), calls=%async_computation.3 | async-start | bytes 81920 | tf_op jit(solution)/shard_map/while/body/eval_jaxpr/reduce_scatter | solution.py:50
  550.3 30.2 %reduce-scatter.5.cloned.1.call-start = ((), (), s32[]{:S(2)}) async-start(), calls=%async_computation.3 | async-start | bytes 81920 | tf_op jit(solution)/shard_map/while/body/eval_jaxpr/reduce_scatter | solution.py:50
  581.4 30.3 %reduce-scatter.5.cloned.1.call-start = ((), (), s32[]{:S(2)}) async-start(), calls=%async_computation.3 | async-start | bytes 81920 | tf_op jit(solution)/shard_map/while/body/eval_jaxpr/reduce_scatter | solution.py:50
  612.4 30.3 %reduce-scatter.5.cloned.1.call-start = ((), (), s32[]{:S(2)}) async-start(), calls=%async_computation.3 | async-start | bytes 81920 | tf_op jit(solution)/shard_map/while/body/eval_jaxpr/reduce_scatter | solution.py:50
  674.5 30.3 %reduce-scatter.5.cloned.1.call-start = ((), (), s32[]{:S(2)}) async-start(), calls=%async_computation.3 | async-start | bytes 81920 | tf_op jit(solution)/shard_map/while/body/eval_jaxpr/reduce_scatter | solution.py:50
  705.6 30.3 %reduce-scatter.5.cloned.1.call-start = ((), (), s32[]{:S(2)}) async-start(), calls=%async_computation.3 | async-start | bytes 81920 | tf_op jit(solution)/shard_map/while/body/eval_jaxpr/reduce_scatter | solution.py:50
  736.6 30.2 %reduce-scatter.5.cloned.1.call-start = ((), (), s32[]{:S(2)}) async-start(), calls=%async_computation.3 | async-start | bytes 81920 | tf_op jit(solution)/shard_map/while/body/eval_jaxpr/reduce_scatter | solution.py:50
  798.7 30.3 %reduce-scatter.5.cloned.1.call-start = ((), (), s32[]{:S(2)}) async-start(), calls=%async_computation.3 | async-start | bytes 81920 | tf_op jit(solution)/shard_map/while/body/eval_jaxpr/reduce_scatter | solution.py:50
  829.7 30.3 %reduce-scatter.5.cloned.1.call-start = ((), (), s32[]{:S(2)}) async-start(), calls=%async_computation.3 | async-start | bytes 81920 | tf_op jit(solution)/shard_map/while/body/eval_jaxpr/reduce_scatter | solution.py:50
  860.8 30.2 %reduce-scatter.5.cloned.1.call-start = ((), (), s32[]{:S(2)}) async-start(), calls=%async_computation.3 | async-start | bytes 81920 | tf_op jit(solution)/shard_map/while/body/eval_jaxpr/reduce_scatter | solution.py:50
  891.8 30.3 %reduce-scatter.5.cloned.1.call-start = ((), (), s32[]{:S(2)}) async-start(), calls=%async_computation.3 | async-start | bytes 81920 | tf_op jit(solution)/shard_map/while/body/eval_jaxpr/reduce_scatter | solution.py:50
  953.9 30.2 %reduce-scatter.5.cloned.1.call-start = ((), (), s32[]{:S(2)}) async-start(), calls=%async_computation.3 | async-start | bytes 81920 | tf_op jit(solution)/shard_map/while/body/eval_jaxpr/reduce_scatter | solution.py:50
  985.0 30.2 %reduce-scatter.5.cloned.1.call-start = ((), (), s32[]{:S(2)}) async-start(), calls=%async_computation.3 | async-start | bytes 81920 | tf_op jit(solution)/shard_map/while/body/eval_jaxpr/reduce_scatter | solution.py:50
  1016.0 30.3 %reduce-scatter.5.cloned.1.call-start = ((), (), s32[]{:S(2)}) async-start(), calls=%async_computation.3 | async-start | bytes 81920 | tf_op jit(solution)/shard_map/while/body/eval_jaxpr/reduce_scatter | solution.py:50
  1078.1 30.3 %reduce-scatter.5.cloned.1.call-start = ((), (), s32[]{:S(2)}) async-start(), calls=%async_computation.3 | async-start | bytes 81920 | tf_op jit(solution)/shard_map/while/body/eval_jaxpr/reduce_scatter | solution.py:50
  1109.1 30.2 %reduce-scatter.5.cloned.1.call-start = ((), (), s32[]{:S(2)}) async-start(), calls=%async_computation.3 | async-start | bytes 81920 | tf_op jit(solution)/shard_map/while/body/eval_jaxpr/reduce_scatter | solution.py:50
  1140.2 30.2 %reduce-scatter.5.cloned.1.call-start = ((), (), s32[]{:S(2)}) async-start(), calls=%async_computation.3 | async-start | bytes 81920 | tf_op jit(solution)/shard_map/while/body/eval_jaxpr/reduce_scatter | solution.py:50
  1171.2 30.2 %reduce-scatter.5.cloned.1.call-start = ((), (), s32[]{:S(2)}) async-start(), calls=%async_computation.3 | async-start | bytes 81920 | tf_op jit(solution)/shard_map/while/body/eval_jaxpr/reduce_scatter | solution.py:50
  1202.2 30.3 %reduce-scatter.5.cloned.1.call-start = ((), (), s32[]{:S(2)}) async-start(), calls=%async_computation.3 | async-start | bytes 81920 | tf_op jit(solution)/shard_map/while/body/eval_jaxpr/reduce_scatter | solution.py:50
  1264.3 30.2 %reduce-scatter.5.cloned.1.call-start = ((), (), s32[]{:S(2)}) async-start(), calls=%async_computation.3 | async-start | bytes 81920 | tf_op jit(solution)/shard_map/while/body/eval_jaxpr/reduce_scatter | solution.py:50
  1295.3 30.2 %reduce-scatter.5.cloned.1.call-start = ((), (), s32[]{:S(2)}) async-start(), calls=%async_computation.3 | async-start | bytes 81920 | tf_op jit(solution)/shard_map/while/body/eval_jaxpr/reduce_scatter | solution.py:50
  1326.3 30.3 %reduce-scatter.5.cloned.1.call-start = ((), (), s32[]{:S(2)}) async-start(), calls=%async_computation.3 | async-start | bytes 81920 | tf_op jit(solution)/shard_map/while/body/eval_jaxpr/reduce_scatter | solution.py:50
  1388.4 30.2 %reduce-scatter.5.cloned.1.call-start = ((), (), s32[]{:S(2)}) async-start(), calls=%async_computation.3 | async-start | bytes 81920 | tf_op jit(solution)/shard_map/while/body/eval_jaxpr/reduce_scatter | solution.py:50
  1419.4 30.3 %reduce-scatter.5.cloned.1.call-start = ((), (), s32[]{:S(2)}) async-start(), calls=%async_computation.3 | async-start | bytes 81920 | tf_op jit(solution)/shard_map/while/body/eval_jaxpr/reduce_scatter | solution.py:50
  1450.5 30.2 %reduce-scatter.5.cloned.1.call-start = ((), (), s32[]{:S(2)}) async-start(), calls=%async_computation.3 | async-start | bytes 81920 | tf_op jit(solution)/shard_map/while/body/eval_jaxpr/reduce_scatter | solution.py:50
  1481.5 30.2 %reduce-scatter.5.cloned.1.call-start = ((), (), s32[]{:S(2)}) async-start(), calls=%async_computation.3 | async-start | bytes 81920 | tf_op jit(solution)/shard_map/while/body/eval_jaxpr/reduce_scatter | solution.py:50
  1543.5 30.3 %reduce-scatter.5.cloned.1.call-start = ((), (), s32[]{:S(2)}) async-start(), calls=%async_computation.3 | async-start | bytes 81920 | tf_op jit(solution)/shard_map/while/body/eval_jaxpr/reduce_scatter | solution.py:50
  1605.6 30.3 %reduce-scatter.5.cloned.1.call-start = ((), (), s32[]{:S(2)}) async-start(), calls=%async_computation.3 | async-start | bytes 81920 | tf_op jit(solution)/shard_map/while/body/eval_jaxpr/reduce_scatter | solution.py:50
  1667.7 30.2 %reduce-scatter.5.cloned.1.call-start = ((), (), s32[]{:S(2)}) async-start(), calls=%async_computation.3 | async-start | bytes 81920 | tf_op jit(solution)/shard_map/while/body/eval_jaxpr/reduce_scatter | solution.py:50
  1698.7 30.2 %reduce-scatter.5.cloned.1.call-start = ((), (), s32[]{:S(2)}) async-start(), calls=%async_computation.3 | async-start | bytes 81920 | tf_op jit(solution)/shard_map/while/body/eval_jaxpr/reduce_scatter | solution.py:50
  1760.8 30.3 %reduce-scatter.5.cloned.1.call-start = ((), (), s32[]{:S(2)}) async-start(), calls=%async_computation.3 | async-start | bytes 81920 | tf_op jit(solution)/shard_map/while/body/eval_jaxpr/reduce_scatter | solution.py:50
  1822.8 30.2 %reduce-scatter.5.cloned.1.call-start = ((), (), s32[]{:S(2)}) async-start(), calls=%async_computation.3 | async-start | bytes 81920 | tf_op jit(solution)/shard_map/while/body/eval_jaxpr/reduce_scatter | solution.py:50
  1853.9 30.2 %reduce-scatter.5.cloned.1.call-start = ((), (), s32[]{:S(2)}) async-start(), calls=%async_computation.3 | async-start | bytes 81920 | tf_op jit(solution)/shard_map/while/body/eval_jaxpr/reduce_scatter | solution.py:50
  1884.9 30.3 %reduce-scatter.5.cloned.1.call-start = ((), (), s32[]{:S(2)}) async-start(), calls=%async_computation.3 | async-start | bytes 81920 | tf_op jit(solution)/shard_map/while/body/eval_jaxpr/reduce_scatter | solution.py:50
  1916.0 30.2 %reduce-scatter.5.cloned.1.call-start = ((), (), s32[]{:S(2)}) async-start(), calls=%async_computation.3 | async-start | bytes 81920 | tf_op jit(solution)/shard_map/while/body/eval_jaxpr/reduce_scatter | solution.py:50
  1947.0 30.3 %reduce-scatter.5.cloned.1.call-start = ((), (), s32[]{:S(2)}) async-start(), calls=%async_computation.3 | async-start | bytes 81920 | tf_op jit(solution)/shard_map/while/body/eval_jaxpr/reduce_scatter | solution.py:50
  2009.0 30.2 %reduce-scatter.5.cloned.1.call-start = ((), (), s32[]{:S(2)}) async-start(), calls=%async_computation.3 | async-start | bytes 81920 | tf_op jit(solution)/shard_map/while/body/eval_jaxpr/reduce_scatter | solution.py:50
  2040.1 30.3 %reduce-scatter.5.cloned.1.call-start = ((), (), s32[]{:S(2)}) async-start(), calls=%async_computation.3 | async-start | bytes 81920 | tf_op jit(solution)/shard_map/while/body/eval_jaxpr/reduce_scatter | solution.py:50
  2133.1 30.3 %reduce-scatter.5.cloned.1.call-start = ((), (), s32[]{:S(2)}) async-start(), calls=%async_computation.3 | async-start | bytes 81920 | tf_op jit(solution)/shard_map/while/body/eval_jaxpr/reduce_scatter | solution.py:50
  (83 other events, 934.9 us)
Sparse Core Ops, SparseCore 0:
  13.2 22.1 reduce-scatter.2
  250.8 19.2 reduce-scatter.4
  281.9 19.2 reduce-scatter.4
  313.0 19.2 reduce-scatter.4
  344.0 19.2 reduce-scatter.4
  406.0 19.2 reduce-scatter.4
  437.1 19.2 reduce-scatter.4
  499.2 19.2 reduce-scatter.4
  530.2 19.2 reduce-scatter.4
  592.3 19.2 reduce-scatter.4
  623.4 19.2 reduce-scatter.4
  654.4 19.2 reduce-scatter.4
  685.5 19.2 reduce-scatter.4
  716.5 19.2 reduce-scatter.4
  747.6 19.2 reduce-scatter.4
  809.6 19.2 reduce-scatter.4
  840.7 19.2 reduce-scatter.4
  871.7 19.2 reduce-scatter.4
  902.8 19.3 reduce-scatter.4
  933.9 19.2 reduce-scatter.4
  964.9 19.2 reduce-scatter.4
  995.9 19.2 reduce-scatter.4
  1027.0 19.2 reduce-scatter.4
  1058.0 19.2 reduce-scatter.4
  1089.0 19.2 reduce-scatter.4
  1120.1 19.2 reduce-scatter.4
  1151.1 19.2 reduce-scatter.4
  1213.2 19.2 reduce-scatter.4
  1306.2 19.2 reduce-scatter.4
  1337.3 19.2 reduce-scatter.4
  1399.3 19.2 reduce-scatter.4
  1430.4 19.2 reduce-scatter.4
  1492.4 19.2 reduce-scatter.4
  1523.5 19.2 reduce-scatter.4
  1554.5 19.2 reduce-scatter.4
  1616.6 19.2 reduce-scatter.4
  1678.6 19.2 reduce-scatter.4
  1709.7 19.2 reduce-scatter.4
  1740.7 19.2 reduce-scatter.4
  1771.7 19.2 reduce-scatter.4
  1833.8 19.2 reduce-scatter.4
  1864.8 19.2 reduce-scatter.4
  1895.9 19.2 reduce-scatter.4
  1926.9 19.2 reduce-scatter.4
  1957.9 19.2 reduce-scatter.4
  2020.0 19.2 reduce-scatter.4
  2051.0 19.2 reduce-scatter.4
  2144.1 19.2 reduce-scatter.4
  (16 shorter events, 306.4 us)
where the time goes:
time: 2180 us; the launch traced here: 2170 us
  waiting for transfers between devices  1480 us (68%)
  matrix products  258 us (12%)
  blocking collectives  190 us (9%)
  starting transfers between devices  168 us (8%)
  other arithmetic  53.8 us (2%)
    reduce_scatter x64, waiting for transfers between devices, one_block(): lax.psum_scatter(contract(current), 'feat', scatter_dimension=1, tiled=True)  1220 us
    ppermute x63, waiting for transfers between devices, from_behind(): return lax.ppermute(value, axis, pairs)  259 us
    dot_general x64, matrix products, contract(): lax.dot_general(left, train_grads, (((1,), (1,)), ((), ())), preferred_el...  257 us
    unnamed x2, blocking collectives  190 us
    ppermute x63, starting transfers between devices, from_behind(): return lax.ppermute(value, axis, pairs)  168 us
    dynamic_update_slice x64, other arithmetic, one_block(): lax.dynamic_update_slice_in_dim(scores, finish(reduced, scale), source *...  50.6 us
  transfers between devices with their start and end apart: 127, of which 126 were waited for; matrix products, arithmetic and copies ran while one was open for 0% of the time, Pallas kernels for 0%

commit v1 on v0

v1 whole, which is shorter than its diff:
```python
import math

import jax
import jax.numpy as jnp
from jax import lax
from jax.experimental import pallas as pl
from jax.experimental.pallas import tpu as pltpu
from jax.sharding import PartitionSpec as P

F = 8192
EPS = 1e-06
NZ, NY, NX = 8, 4, 2
SHARD = 16
BLOCK = 4 * SHARD
NEAR = (0, -1, 1, -2)
VMEM = pl.BlockSpec(memory_space=pltpu.VMEM)
SMEM = pl.BlockSpec(memory_space=pltpu.SMEM)
MIB = 1 << 20


def row_index(z, y, x):
    return (z % NZ) * (NY * NX) + (y % NY) * NX + x % NX


def shift(value, even, odd=None):
    odd = even if odd is None else odd
    pairs = []
    for z in range(NZ):
        for y in range(NY):
            for x in range(NX):
                for f in range(4):
                    dz, dy, dx = odd if f % 2 else even
                    there = row_index(z + dz, y + dy, x + dx)
                    pairs.append((row_index(z, y, x) * 4 + f, there * 4 + f))
    return lax.ppermute(value, ("rows", "feat"), pairs)


def across(value, mask):
    return lax.ppermute(value, "feat", [(f, f ^ mask) for f in range(4)])


def join(*parts):
    return jnp.concatenate(parts, axis=0)


def gather(own):
    pair = join(own, shift(own, (4, 0, 0)))
    four = join(pair, shift(pair, (0, 0, 1)))
    first = [
        shift(four, (0, 1, 0), (1, 0, 0)),
        shift(four, (0, -1, 0), (-1, 0, 0)),
        shift(four, (0, 2, 0), (2, 0, 0)),
    ]
    held = join(four, *first)
    before = shift(held, (1, 0, 0), (0, 1, 0))
    after = shift(held, (-1, 0, 0), (0, -1, 0))
    low = shift(held[: 2 * BLOCK], (2, 0, 0), (0, 2, 0))
    high = shift(held[2 * BLOCK :], (-2, 0, 0), (0, -2, 0))
    return held, before, after, low, high


PIECES = (
    tuple((a, 0) for a in NEAR),
    tuple((a, -1) for a in NEAR),
    tuple((a, 1) for a in NEAR),
    tuple((a, -2) for a in NEAR[:2]),
    tuple((a, 2) for a in NEAR[2:]),
)


def first_row(place, core, first, last, part):
    z, y, x = place[0], place[1], place[2]
    dz = jnp.where(core == 0, last, first)
    dy = jnp.where(core == 0, first, last)
    zz = lax.rem(z + dz + (4 * (part % 2) + NZ), NZ)
    yy = lax.rem(y + dy + NY, NY)
    xx = lax.rem(x + part // 2, NX)
    return pl.multiple_of((zz * (NY * NX) + yy * NX + xx) * SHARD, SHARD)


def split3(value):
    high = value.astype(jnp.bfloat16)
    rest = value - high.astype(jnp.float32)
    middle = rest.astype(jnp.bfloat16)
    low = (rest - middle.astype(jnp.float32)).astype(jnp.bfloat16)
    return [high, middle, low]


def prepare_kernel(place, train_ref, turned_ref, sums_ref):
    me = place[3]
    for k, mask in enumerate((0, 2, 1, 3)):
        start = pl.multiple_of((me ^ mask) * 256, 256)
        for j in range(0, 2048, 512):
            block = train_ref[pl.ds(start, 256), j : j + 512].T
            turned_ref[k, j : j + 512, :] = block
            wide = block.astype(jnp.float32)
            part = jnp.sum(wide * wide, axis=0, keepdims=True)
            if j == 0:
                sums_ref[k : k + 1, :] = part
            else:
                sums_ref[k : k + 1, :] += part


def products_kernel(place, turned_ref, precond_ref, *refs):
    pieces = refs[: len(PIECES)]
    keep_ref, send_ref, sums_ref, rounded_ref = refs[len(PIECES) :]
    core = place[3] % 2
    for piece, blocks in zip(pieces, PIECES):
        rows = piece.shape[0]
        squares = jnp.zeros((rows, 128), jnp.float32)
        for k in range(8):
            columns = slice(k * 256, (k + 1) * 256)
            value = jnp.dot(piece[:, columns], precond_ref[k], preferred_element_type=jnp.float32)
            rounded_ref[:rows, columns] = value.astype(jnp.bfloat16)
            value = value * value
            squares += value[:, :128] + value[:, 128:]
        starts = [first_row(place, core, *block, part) for block in blocks for part in range(4)]
        for n, start in enumerate(starts):
            sums_ref[pl.ds(start, SHARD), :] = squares[n * SHARD : (n + 1) * SHARD]
        for k in range(4):
            value = jnp.dot(rounded_ref[:rows, :], turned_ref[k], preferred_element_type=jnp.float32)
            columns = slice((k % 2) * 256, (k % 2 + 1) * 256)
            for n, start in enumerate(starts):
                part = value[n * SHARD : (n + 1) * SHARD]
                if k < 2:
                    keep_ref[pl.ds(start, SHARD), columns] = part
                else:
                    send_ref[pl.ds(start, SHARD), columns] = part.astype(jnp.bfloat16)


def pack_kernel(sums_ref, train_ref, lanes_ref, rows_ref):
    lanes_ref[...] = jnp.sum(sums_ref[...].T, axis=0, keepdims=True)
    rows = []
    for j in range(2):
        rows += split3(lanes_ref[:, j * 512 : (j + 1) * 512])
    rows += split3(jnp.concatenate([train_ref[2:3, :], train_ref[3:4, :]], axis=1))
    rows.append(jnp.zeros((SHARD - len(rows), 512), jnp.bfloat16))
    rows_ref[...] = jnp.concatenate(rows, axis=0)


def join3(ref, base, row):
    return sum(ref[base + row + i : base + row + i + 1, :].astype(jnp.float32) for i in range(3))


def chip_kernel(keep_ref, got_ref, lanes_ref, train_ref, mine_ref, send_ref, lanes2_ref, train2_ref):
    rows = keep_ref.shape[0]
    mine_ref[...] = keep_ref[:, :256] + got_ref[:rows, :256].astype(jnp.float32)
    theirs = keep_ref[:, 256:] + got_ref[:rows, 256:].astype(jnp.float32)
    send_ref[:rows, :] = theirs.astype(jnp.bfloat16)
    got = got_ref[rows:, :].astype(jnp.float32)
    extra = []
    for j in range(2):
        total = lanes_ref[:, j * 512 : (j + 1) * 512] + (got[3 * j : 3 * j + 1] + got[3 * j + 1 : 3 * j + 2] + got[3 * j + 2 : 3 * j + 3])
        lanes2_ref[:, j * 512 : (j + 1) * 512] = total
        extra += split3(total[:, :256]) + split3(total[:, 256:])
    train = got[6:7] + got[7:8] + got[8:9]
    train2_ref[...] = train_ref[0:1, :] + train[:, :256]
    extra += split3(train_ref[1:2, :] + train[:, 256:])
    extra.append(jnp.zeros((SHARD - len(extra), 256), jnp.bfloat16))
    send_ref[rows:, :] = jnp.concatenate(extra, axis=0)


def finish_kernel(mine_ref, got_ref, lanes_ref, train_ref, out_ref):
    rows = mine_ref.shape[0]
    got = got_ref[rows:, :].astype(jnp.float32)
    sums = [got[3 * j : 3 * j + 1] + got[3 * j + 1 : 3 * j + 2] + got[3 * j + 2 : 3 * j + 3] for j in range(5)]
    query = lanes_ref[...] + jnp.concatenate(sums[:4], axis=1)
    query = 1.0 / jnp.sqrt(query + EPS)
    query = jnp.broadcast_to(query, (128, rows)).T
    train = (1.0 / jnp.sqrt(train_ref[...] + sums[4] + EPS)) * math.sqrt(F)
    for j in range(2):
        columns = slice(j * 128, (j + 1) * 128)
        total = mine_ref[:, columns] + got_ref[:rows, columns].astype(jnp.float32)
        out_ref[:, columns] = total * query * train[:, columns]


def call(kernel, outs, inputs, scratch=(), flops=0, moved=0, smem=0):
    return pl.pallas_call(
        kernel,
        out_shape=[jax.ShapeDtypeStruct(s, d) for s, d in outs],
        in_specs=[SMEM] * smem + [VMEM] * (len(inputs) - smem),
        out_specs=[VMEM] * len(outs),
        scratch_shapes=list(scratch),
        compiler_params=pltpu.CompilerParams(vmem_limit_bytes=24 * MIB),
        cost_estimate=pl.CostEstimate(flops=flops, bytes_accessed=moved, transcendentals=0),
    )(*inputs)


def on_device(query_grads, train_grads, precond):
    f32, bf16 = jnp.float32, jnp.bfloat16
    row = lax.axis_index("rows")
    place = jnp.stack([row // (NY * NX), row // NX % NY, row % NX, lax.axis_index("feat")]).astype(jnp.int32)
    turned, train_sums = call(
        prepare_kernel,
        [((4, 2048, 256), bf16), ((4, 256), f32)],
        [place, train_grads],
        moved=8 * MIB,
        smem=1,
    )
    pieces = gather(query_grads)
    keep, send, squares = call(
        products_kernel,
        [((1024, 512), f32), ((1024, 512), bf16), ((1024, 128), f32)],
        [place, turned, precond, *pieces],
        scratch=[pltpu.VMEM((256, 2048), bf16)],
        flops=5 << 30,
        smem=1,
    )
    lanes, extra = call(pack_kernel, [((1, 1024), f32), ((SHARD, 512), bf16)], [squares, train_sums])
    got = across(join(send, extra), 1)
    mine, send, lanes, train = call(
        chip_kernel,
        [((1024, 256), f32), ((1024 + SHARD, 256), bf16), ((1, 1024), f32), ((1, 256), f32)],
        [keep, got, lanes, train_sums],
    )
    got = across(send, 2)
    return call(finish_kernel, [((1024, 256), f32)], [mine, got, lanes, train])[0]


def solution(mesh):
    in_specs = (P("rows", "feat"), P("rows", "feat"), P("feat", None, None))
    out_specs = P(None, ("rows", "feat"))
    return jax.shard_map(
        on_device, mesh=mesh, in_specs=in_specs, out_specs=out_specs, check_vma=False
    )
```

time: 2180 us -> 86.5 us (0.04)
  waiting for transfers between devices: 1480 us -> 43 us
  matrix products: 258 us -> 0 us
  blocking collectives: 190 us -> 0 us
  starting transfers between devices: 168 us -> 25.5 us
  other arithmetic: 53.8 us -> 2.7 us
    reduce_scatter x64 -> x0, waiting for transfers between devices: 1220 us -> none  [one_block(): lax.psum_scatter(contract(current), 'feat', scatter_dimension=1, tiled=True)]
    dot_general x65 -> x0, matrix products: 258 us -> none  [the longest x64 257 us: contract(): lax.dot_general(left, train_grads, (((1,), (1,)), ((), ())), preferred_el...]
    ppermute x63 -> x11, waiting for transfers between devices: 259 us -> 43 us  [the longest x9 27.7 us: shift(): return lax.ppermute(value, ('rows', 'feat'), pairs)]
    unnamed x2 -> x0, blocking collectives: 190 us -> none
    ppermute x63 -> x11, starting transfers between devices: 168 us -> 25.5 us  [the longest x9 23.8 us: shift(): return lax.ppermute(value, ('rows', 'feat'), pairs)]
    dynamic_update_slice x64 -> x0, other arithmetic: 50.6 us -> none  [one_block(): lax.dynamic_update_slice_in_dim(scores, finish(reduced, scale), source *...]
  transfers between devices with their start and end apart: 127 -> 11, of which waited for: 126 -> 8; matrix products, arithmetic and copies ran while one was open for 0% -> 3% of each run, Pallas kernels for 0% -> 2%
where the time goes in v1:
time: 86.5 us; the launch traced here: 84.9 us
  waiting for transfers between devices  43 us (50%)
  starting transfers between devices  25.5 us (29%)
  Pallas kernels  10.4 us (12%)
  local copies, waits for them, and re-layouts  3.16 us (4%)
  other arithmetic  2.7 us (3%)
    ppermute x9, waiting for transfers between devices, shift(): return lax.ppermute(value, ('rows', 'feat'), pairs)  27.7 us
    ppermute x9, starting transfers between devices, shift(): return lax.ppermute(value, ('rows', 'feat'), pairs)  23.8 us
    ppermute x2, waiting for transfers between devices, across(): return lax.ppermute(value, 'feat', [(f, f ^ mask) for f in range(4)])  15.3 us
    pallas_call x5, Pallas kernels, call(): pl.pallas_call(kernel, out_shape=[jax.ShapeDtypeStruct(s, d) for s, d in...  10.4 us
    unnamed x10, local copies, waits for them, and re-layouts  3.12 us
    concatenate x4, other arithmetic, join(): return jnp.concatenate(parts, axis=0)  2.62 us
  transfers between devices with their start and end apart: 11, of which 8 were waited for; matrix products, arithmetic and copies ran while one was open for 3% of the time, Pallas kernels for 2%

profile of v1, /device:TPU:8, one launch (start us, length us, event | category | flops | bytes accessed | tf_op | source)
XLA Modules:
  0.0 84.9 jit_solution(3761640691141128657)
XLA Ops:
  0.0 0.0 copy-start.2
  0.0 7.2 %collective-permute-start = (bf16[16,2048]{1,0:T(8,128)(2,1)}, bf16[16,2048]{1,0:T(8,128)(2,1)S(1)}, u32[]{:S(2)}, u32[]{:S(2)}) collective-permute-start(bf16[16,2048]{1,0:T(8,128)(2,1)} %param.3), channel_id=1, source_target_pairs={{0,128},{1,129},{2,130},{3,131},{4,132},{5,133},{6,134},{7,135},{8... | collective-permute-start | bytes 196616 | tf_op jit(solution)/shard_map/ppermute | solution.py:35
  7.2 0.9 %constant_dynamic-update-slice_fusion.2 = (bf16[64,2048]{1,0:T(8,128)(2,1)S(1)}, bf16[256,2048]{1,0:T(8,128)(2,1)S(1)}) fusion(bf16[16,2048]{1,0:T(8,128)(2,1)} %param.3), kind=kLoop, calls=%fused_computation.6 | loop fusion | bytes 196608
  8.1 1.8 %collective-permute-done = bf16[16,2048]{1,0:T(8,128)(2,1)S(1)} collective-permute-done((bf16[16,2048]{1,0:T(8,128)(2,1)}, bf16[16,2048]{1,0:T(8,128)(2,1)S(1)}, u32[]{:S(2)}, u32[]{:S(2)}) %collective-permute-start) | collective-permute-done | bytes 65568 | tf_op jit(solution)/shard_map/ppermute | solution.py:35
  9.9 0.8 pad_maximum_fusion.3
  10.7 3.1 %collective-permute-start.1 = (bf16[32,2048]{1,0:T(8,128)(2,1)S(1)}, bf16[32,2048]{1,0:T(8,128)(2,1)S(1)}, u32[]{:S(2)}, u32[]{:S(2)}) collective-permute-start(bf16[32,2048]{1,0:T(8,128)(2,1)S(1)} %pad_maximum_fusion.3), channel_id=1, source_target_pairs={{0,4},{1,5},{2,6},{3,7},{4,0},{5,1},{6,2},{7,3},{8,12},{9,13},{10,... | collective-permute-start | bytes 393224 | tf_op jit(solution)/shard_map/ppermute | solution.py:35
  13.8 3.4 %collective-permute-done.1 = bf16[32,2048]{1,0:T(8,128)(2,1)S(1)} collective-permute-done((bf16[32,2048]{1,0:T(8,128)(2,1)S(1)}, bf16[32,2048]{1,0:T(8,128)(2,1)S(1)}, u32[]{:S(2)}, u32[]{:S(2)}) %collective-permute-start.1) | collective-permute-done | bytes 131104 | tf_op jit(solution)/shard_map/ppermute | solution.py:35
  17.3 1.7 %collective-permute-start.2 = (bf16[64,2048]{1,0:T(8,128)(2,1)S(1)}, bf16[64,2048]{1,0:T(8,128)(2,1)S(1)}, u32[]{:S(2)}, u32[]{:S(2)}) collective-permute-start(bf16[64,2048]{1,0:T(8,128)(2,1)S(1)} %get-tuple-element.27), channel_id=1, source_target_pairs={{0,8},{1,33},{2,10},{3,35},{4,12},{5,37},{6,14},{7,39},{8,16},{9,4... | collective-permute-start | bytes 786440 | tf_op jit(solution)/shard_map/ppermute | solution.py:35
  19.0 0.4 collective-permute-start.3
  19.4 2.3 %collective-permute-start.4 = (bf16[64,2048]{1,0:T(8,128)(2,1)S(1)}, bf16[64,2048]{1,0:T(8,128)(2,1)S(1)}, u32[]{:S(2)}, u32[]{:S(2)}) collective-permute-start(bf16[64,2048]{1,0:T(8,128)(2,1)S(1)} %get-tuple-element.27), channel_id=1, source_target_pairs={{0,16},{1,65},{2,18},{3,67},{4,20},{5,69},{6,22},{7,71},{8,24},{9,... | collective-permute-start | bytes 786440 | tf_op jit(solution)/shard_map/ppermute | solution.py:35
  21.7 2.0 %collective-permute-done.2 = bf16[64,2048]{1,0:T(8,128)(2,1)S(1)} collective-permute-done((bf16[64,2048]{1,0:T(8,128)(2,1)S(1)}, bf16[64,2048]{1,0:T(8,128)(2,1)S(1)}, u32[]{:S(2)}, u32[]{:S(2)}) %collective-permute-start.2) | collective-permute-done | bytes 262176 | tf_op jit(solution)/shard_map/ppermute | solution.py:35
  23.8 1.6 %collective-permute-done.3 = bf16[64,2048]{1,0:T(8,128)(2,1)S(1)} collective-permute-done((bf16[64,2048]{1,0:T(8,128)(2,1)S(1)}, bf16[64,2048]{1,0:T(8,128)(2,1)S(1)}, u32[]{:S(2)}, u32[]{:S(2)}) %collective-permute-start.3) | collective-permute-done | bytes 262176 | tf_op jit(solution)/shard_map/ppermute | solution.py:35
  25.4 3.5 %collective-permute-done.4 = bf16[64,2048]{1,0:T(8,128)(2,1)S(1)} collective-permute-done((bf16[64,2048]{1,0:T(8,128)(2,1)S(1)}, bf16[64,2048]{1,0:T(8,128)(2,1)S(1)}, u32[]{:S(2)}, u32[]{:S(2)}) %collective-permute-start.4) | collective-permute-done | bytes 262176 | tf_op jit(solution)/shard_map/ppermute | solution.py:35
  28.9 4.5 %collective-permute-start.6 = (bf16[256,2048]{1,0:T(8,128)(2,1)S(1)}, bf16[256,2048]{1,0:T(8,128)(2,1)S(1)}, u32[]{:S(2)}, u32[]{:S(2)}) collective-permute-start(bf16[256,2048]{1,0:T(8,128)(2,1)S(1)} %constant_dynamic-update-slice_fusion.3.refs_0_), channel_id=1, source_target_pairs={{0,224},{1,25},{2,226},{3,27},{4,228},{5,29},{6,230},{7,31},{8,232... | collective-permute-start | bytes 3145736 | tf_op jit(solution)/shard_map/ppermute | solution.py:35
  33.4 0.0 collective-permute-start.5
  33.4 0.0 copy-done.2
  33.4 0.8 pad_maximum_fusion.1
  34.3 0.4 collective-permute-start.7
  34.7 0.9 %pad_maximum_fusion.2 = bf16[128,2048]{1,0:T(8,128)(2,1)} fusion(bf16[64,2048]{1,0:T(8,128)(2,1)S(1)} %collective-permute-done.4, bf16[64,2048]{1,0:T(8,128)(2,1)S(1)} %collective-permute-done.3), kind=kLoop, calls=%fused_computation.2 | loop fusion | flops 1048576 | bytes 1048576 | tf_op jit(solution)/shard_map/concatenate | solution.py:43
  35.6 4.2 %collective-permute-start.8 = (bf16[128,2048]{1,0:T(8,128)(2,1)}, bf16[128,2048]{1,0:T(8,128)(2,1)}, u32[]{:S(2)}, u32[]{:S(2)}) collective-permute-start(bf16[128,2048]{1,0:T(8,128)(2,1)} %pad_maximum_fusion.2), channel_id=1, source_target_pairs={{0,192},{1,17},{2,194},{3,19},{4,196},{5,21},{6,198},{7,23},{8,200... | collective-permute-start | bytes 1572872 | tf_op jit(solution)/shard_map/ppermute | solution.py:35
  39.7 0.1 pad_add_fusion.place
  39.8 0.0 copy-start
  39.8 2.2 %copy-done = bf16[1024,2048]{1,0:T(8,128)(2,1)S(1)} copy-done((bf16[1024,2048]{1,0:T(8,128)(2,1)S(1)}, bf16[1024,2048]{1,0:T(8,128)(2,1)}, u32[]{:S(2)}) %copy-start) | copy-done | bytes 4194328
  42.0 0.0 copy-start.1
  42.0 1.8 %shard_map.37 = (bf16[4,2048,256]{2,1,0:T(8,128)(2,1)S(1)}, f32[4,256]{1,0:T(4,128)S(1)}) custom-call(s32[4]{0:T(128)S(1)} %pad_add_fusion.place, bf16[1024,2048]{1,0:T(8,128)(2,1)S(1)} %copy-done), custom_call_target="tpu_custom_call" | custom-call | bytes 8388608 | tf_op jit(solution)/shard_map/pallas_call | solution.py:178
  43.8 15.4 %collective-permute-done.7.refs_3_ = bf16[128,2048]{1,0:T(8,128)(2,1)} collective-permute-done((bf16[128,2048]{1,0:T(8,128)(2,1)}, bf16[128,2048]{1,0:T(8,128)(2,1)}, u32[]{:S(2)}, u32[]{:S(2)}) %collective-permute-start.7) | collective-permute-done | bytes 524320 | tf_op jit(solution)/shard_map/ppermute | solution.py:35
  59.2 0.0 collective-permute-done.8.refs_4_
  59.2 0.0 collective-permute-done.6.refs_2_
  59.2 0.0 collective-permute-done.5.refs_1_
  59.2 0.0 copy-done.1
  59.2 6.9 %shard_map.38 = (f32[1024,512]{1,0:T(8,128)S(1)}, bf16[1024,512]{1,0:T(8,128)(2,1)S(1)}, f32[1024,128]{1,0:T(8,128)S(1)}) custom-call(s32[4]{0:T(128)S(1)} %pad_add_fusion.place, bf16[4,2048,256]{2,1,0:T(8,128)(2,1)S(1)} %get-tuple-element.16.turned_ref, bf16[8,256,256]{2,1,0:T(8,128)(2,1)S(1)} %copy-done.1, ...), custom_call_target="tpu_custom_call" | custom-call | flops 5368709120 | tf_op jit(solution)/shard_map/pallas_call | solution.py:178
  66.1 0.2 shard_map.39
  66.4 0.1 pad_maximum_fusion
  66.5 0.1 collective-permute-start.9
  66.6 2.7 %collective-permute-done.9.got_ref = bf16[1040,512]{1,0:T(8,128)(2,1)S(1)} collective-permute-done((bf16[1040,512]{1,0:T(8,128)(2,1)S(1)}, bf16[1040,512]{1,0:T(8,128)(2,1)S(1)}, u32[]{:S(2)}, u32[]{:S(2)}) %collective-permute-start.9) | collective-permute-done | bytes 1064992 | tf_op jit(solution)/shard_map/ppermute | solution.py:39
  69.2 0.2 shard_map.40
  69.5 1.6 %collective-permute-start.10 = (bf16[1040,256]{1,0:T(8,128)(2,1)S(1)}, bf16[1040,256]{1,0:T(8,128)(2,1)S(1)}, u32[]{:S(2)}, u32[]{:S(2)}) collective-permute-start(bf16[1040,256]{1,0:T(8,128)(2,1)S(1)} %get-tuple-element.24), channel_id=1, source_target_pairs={{0,2},{1,3},{2,0},{3,1},{4,6},{5,7},{6,4},{7,5},{8,10},{9,11},{10,... | collective-permute-start | bytes 1597448 | tf_op jit(solution)/shard_map/ppermute | solution.py:39
  71.0 12.7 %collective-permute-done.10.got_ref = bf16[1040,256]{1,0:T(8,128)(2,1)S(1)} collective-permute-done((bf16[1040,256]{1,0:T(8,128)(2,1)S(1)}, bf16[1040,256]{1,0:T(8,128)(2,1)S(1)}, u32[]{:S(2)}, u32[]{:S(2)}) %collective-permute-start.10) | collective-permute-done | bytes 532512 | tf_op jit(solution)/shard_map/ppermute | solution.py:39
  83.7 1.2 %shard_map.41 = f32[1024,256]{1,0:T(8,128)} custom-call(f32[1024,256]{1,0:T(8,128)S(1)} %get-tuple-element.23.mine_ref, bf16[1040,256]{1,0:T(8,128)(2,1)S(1)} %collective-permute-done.10.got_ref, f32[1,1024]{1,0:T(1,128)S(1)} %get-tuple-element.25.lanes_ref, f32[1,256]{1,0:T(1,128)S(1)} %get-tuple-element.26.train_ref), custom_call_target="tpu_custom_call" | custom-call | tf_op jit(solution)/shard_map/pallas_call | solution.py:178
  (5 shorter events, 0.1 us)
Async XLA Ops:
  0.0 33.4 %copy-start.2 = (bf16[16,2048]{1,0:T(8,128)(2,1)S(1)}, bf16[16,2048]{1,0:T(8,128)(2,1)}, u32[]{:S(2)}) copy-start(bf16[16,2048]{1,0:T(8,128)(2,1)} %param.3) | copy-start | bytes 196612
  0.0 9.9 %collective-permute-start = (bf16[16,2048]{1,0:T(8,128)(2,1)}, bf16[16,2048]{1,0:T(8,128)(2,1)S(1)}, u32[]{:S(2)}, u32[]{:S(2)}) collective-permute-start(bf16[16,2048]{1,0:T(8,128)(2,1)} %param.3), channel_id=1, source_target_pairs={{0,128},{1,129},{2,130},{3,131},{4,132},{5,133},{6,134},{7,135},{8... | collective-permute-start | bytes 196616 | tf_op jit(solution)/shard_map/ppermute | solution.py:35
  10.7 6.6 %collective-permute-start.1 = (bf16[32,2048]{1,0:T(8,128)(2,1)S(1)}, bf16[32,2048]{1,0:T(8,128)(2,1)S(1)}, u32[]{:S(2)}, u32[]{:S(2)}) collective-permute-start(bf16[32,2048]{1,0:T(8,128)(2,1)S(1)} %pad_maximum_fusion.3), channel_id=1, source_target_pairs={{0,4},{1,5},{2,6},{3,7},{4,0},{5,1},{6,2},{7,3},{8,12},{9,13},{10,... | collective-permute-start | bytes 393224 | tf_op jit(solution)/shard_map/ppermute | solution.py:35
  17.3 6.4 %collective-permute-start.2 = (bf16[64,2048]{1,0:T(8,128)(2,1)S(1)}, bf16[64,2048]{1,0:T(8,128)(2,1)S(1)}, u32[]{:S(2)}, u32[]{:S(2)}) collective-permute-start(bf16[64,2048]{1,0:T(8,128)(2,1)S(1)} %get-tuple-element.27), channel_id=1, source_target_pairs={{0,8},{1,33},{2,10},{3,35},{4,12},{5,37},{6,14},{7,39},{8,16},{9,4... | collective-permute-start | bytes 786440 | tf_op jit(solution)/shard_map/ppermute | solution.py:35
  19.0 6.4 %collective-permute-start.3 = (bf16[64,2048]{1,0:T(8,128)(2,1)S(1)}, bf16[64,2048]{1,0:T(8,128)(2,1)S(1)}, u32[]{:S(2)}, u32[]{:S(2)}) collective-permute-start(bf16[64,2048]{1,0:T(8,128)(2,1)S(1)} %get-tuple-element.27), channel_id=1, source_target_pairs={{0,24},{1,225},{2,26},{3,227},{4,28},{5,229},{6,30},{7,231},{8,0},... | collective-permute-start | bytes 786440 | tf_op jit(solution)/shard_map/ppermute | solution.py:35
  19.4 9.4 %collective-permute-start.4 = (bf16[64,2048]{1,0:T(8,128)(2,1)S(1)}, bf16[64,2048]{1,0:T(8,128)(2,1)S(1)}, u32[]{:S(2)}, u32[]{:S(2)}) collective-permute-start(bf16[64,2048]{1,0:T(8,128)(2,1)S(1)} %get-tuple-element.27), channel_id=1, source_target_pairs={{0,16},{1,65},{2,18},{3,67},{4,20},{5,69},{6,22},{7,71},{8,24},{9,... | collective-permute-start | bytes 786440 | tf_op jit(solution)/shard_map/ppermute | solution.py:35
  28.9 30.3 %collective-permute-start.6 = (bf16[256,2048]{1,0:T(8,128)(2,1)S(1)}, bf16[256,2048]{1,0:T(8,128)(2,1)S(1)}, u32[]{:S(2)}, u32[]{:S(2)}) collective-permute-start(bf16[256,2048]{1,0:T(8,128)(2,1)S(1)} %constant_dynamic-update-slice_fusion.3.refs_0_), channel_id=1, source_target_pairs={{0,224},{1,25},{2,226},{3,27},{4,228},{5,29},{6,230},{7,31},{8,232... | collective-permute-start | bytes 3145736 | tf_op jit(solution)/shard_map/ppermute | solution.py:35
  33.4 25.7 %collective-permute-start.5 = (bf16[256,2048]{1,0:T(8,128)(2,1)S(1)}, bf16[256,2048]{1,0:T(8,128)(2,1)S(1)}, u32[]{:S(2)}, u32[]{:S(2)}) collective-permute-start(bf16[256,2048]{1,0:T(8,128)(2,1)S(1)} %constant_dynamic-update-slice_fusion.3.refs_0_), channel_id=1, source_target_pairs={{0,32},{1,9},{2,34},{3,11},{4,36},{5,13},{6,38},{7,15},{8,40},{9,1... | collective-permute-start | bytes 3145736 | tf_op jit(solution)/shard_map/ppermute | solution.py:35
  34.3 24.9 %collective-permute-start.7 = (bf16[128,2048]{1,0:T(8,128)(2,1)}, bf16[128,2048]{1,0:T(8,128)(2,1)}, u32[]{:S(2)}, u32[]{:S(2)}) collective-permute-start(bf16[128,2048]{1,0:T(8,128)(2,1)} %pad_maximum_fusion.1), channel_id=1, source_target_pairs={{0,64},{1,17},{2,66},{3,19},{4,68},{5,21},{6,70},{7,23},{8,72},{9,... | collective-permute-start | bytes 1572872 | tf_op jit(solution)/shard_map/ppermute | solution.py:35
  35.6 23.6 %collective-permute-start.8 = (bf16[128,2048]{1,0:T(8,128)(2,1)}, bf16[128,2048]{1,0:T(8,128)(2,1)}, u32[]{:S(2)}, u32[]{:S(2)}) collective-permute-start(bf16[128,2048]{1,0:T(8,128)(2,1)} %pad_maximum_fusion.2), channel_id=1, source_target_pairs={{0,192},{1,17},{2,194},{3,19},{4,196},{5,21},{6,198},{7,23},{8,200... | collective-permute-start | bytes 1572872 | tf_op jit(solution)/shard_map/ppermute | solution.py:35
  39.8 2.2 %copy-start = (bf16[1024,2048]{1,0:T(8,128)(2,1)S(1)}, bf16[1024,2048]{1,0:T(8,128)(2,1)}, u32[]{:S(2)}) copy-start(bf16[1024,2048]{1,0:T(8,128)(2,1)} %train_ref.1) | copy-start | bytes 12582916
  42.0 17.2 %copy-start.1 = (bf16[8,256,256]{2,1,0:T(8,128)(2,1)S(1)}, bf16[8,256,256]{2,1,0:T(8,128)(2,1)}, u32[]{:S(2)}) copy-start(bf16[8,256,256]{2,1,0:T(8,128)(2,1)} %precond_ref.1) | copy-start | bytes 3145732
  66.5 2.8 %collective-permute-start.9 = (bf16[1040,512]{1,0:T(8,128)(2,1)S(1)}, bf16[1040,512]{1,0:T(8,128)(2,1)S(1)}, u32[]{:S(2)}, u32[]{:S(2)}) collective-permute-start(bf16[1040,512]{1,0:T(8,128)(2,1)S(1)} %pad_maximum_fusion), channel_id=1, source_target_pairs={{0,1},{1,0},{2,3},{3,2},{4,5},{5,4},{6,7},{7,6},{8,9},{9,8},{10,11... | collective-permute-start | bytes 3194888 | tf_op jit(solution)/shard_map/ppermute | solution.py:39
  69.5 14.2 %collective-permute-start.10 = (bf16[1040,256]{1,0:T(8,128)(2,1)S(1)}, bf16[1040,256]{1,0:T(8,128)(2,1)S(1)}, u32[]{:S(2)}, u32[]{:S(2)}) collective-permute-start(bf16[1040,256]{1,0:T(8,128)(2,1)S(1)} %get-tuple-element.24), channel_id=1, source_target_pairs={{0,2},{1,3},{2,0},{3,1},{4,6},{5,7},{6,4},{7,5},{8,10},{9,11},{10,... | collective-permute-start | bytes 1597448 | tf_op jit(solution)/shard_map/ppermute | solution.py:39

commit v2 on v1

v2 whole, which is shorter than its diff:
```python
import math

import jax
import jax.numpy as jnp
from jax import lax
from jax.experimental import pallas as pl
from jax.experimental.pallas import tpu as pltpu
from jax.sharding import PartitionSpec as P

F = 8192
EPS = 1e-06
NZ, NY, NX = 8, 4, 2
SHARD = 16
BLOCK = 4 * SHARD
NEAR = (0, -1, 1, -2)
VMEM = pl.BlockSpec(memory_space=pltpu.VMEM)
SMEM = pl.BlockSpec(memory_space=pltpu.SMEM)
MIB = 1 << 20


def row_index(z, y, x):
    return (z % NZ) * (NY * NX) + (y % NY) * NX + x % NX


def shift(value, even, odd=None):
    odd = even if odd is None else odd
    pairs = []
    for z in range(NZ):
        for y in range(NY):
            for x in range(NX):
                for f in range(4):
                    dz, dy, dx = odd if f % 2 else even
                    there = row_index(z + dz, y + dy, x + dx)
                    pairs.append((row_index(z, y, x) * 4 + f, there * 4 + f))
    return lax.ppermute(value, ("rows", "feat"), pairs)


def across(value, mask):
    return lax.ppermute(value, "feat", [(f, f ^ mask) for f in range(4)])


def join(*parts):
    return jnp.concatenate(parts, axis=0)


def together(*values):
    return lax.optimization_barrier(values)


def gather(own, early, first_product):
    pair = join(own, shift(own, (4, 0, 0)))
    four = join(pair, shift(pair, (0, 0, 1)))
    first = [
        shift(four, (0, 1, 0), (1, 0, 0)),
        shift(four, (0, -1, 0), (-1, 0, 0)),
        shift(four, (0, 2, 0), (2, 0, 0)),
    ]
    prepared = early(four)
    low, high, *prepared = together(join(four, first[0]), join(*first[1:]), *prepared)
    up, down = (1, 0, 0), (0, 1, 0)
    back_up, back_down = (-1, 0, 0), (0, -1, 0)
    low_before, high_after = shift(low, up, down), shift(high, back_up, back_down)
    high_before, low_after = shift(high, up, down), shift(low, back_up, back_down)
    product = first_product((low, high), prepared)
    low_before, high_after, *product = together(low_before, high_after, *product)
    low_far, high_far = shift(low_before, up, down), shift(high_after, back_up, back_down)
    return prepared, product, (low_before, high_after), (high_before, low_after), (low_far, high_far)


LOW, HIGH = NEAR[:2], NEAR[2:]
STAGES = (
    [[(a, 0) for a in LOW], [(a, 0) for a in HIGH]],
    [[(a, -1) for a in LOW], [(a, 1) for a in HIGH]],
    [[(a, -1) for a in HIGH], [(a, 1) for a in LOW]],
    [[(a, -2) for a in LOW], [(a, 2) for a in HIGH]],
)
ORDER = [block for stage in STAGES for piece in stage for block in piece]
STAGE_ROWS = [sum(len(piece) for piece in stage) * BLOCK for stage in STAGES]


def wrap(step):
    return -2 if step == 2 else step


EARLY = [block for block in ORDER if 2 not in map(abs, block)]
LATE = [block for block in ORDER if 2 in map(abs, block)]


def slot(block):
    at = ORDER.index(block) * BLOCK
    for stage, rows in enumerate(STAGE_ROWS):
        if at < rows:
            return stage, at
        at -= rows


def twin(block):
    other = (wrap(block[1]), wrap(block[0]))
    return next(b for b in ORDER if (wrap(b[0]), wrap(b[1])) == other)


def depth(core, block):
    return jnp.where(core == 0, block[1], block[0])


def first_row(place, block, part):
    z, y, x, core = place[0], place[1], place[2], place[3] % 2
    dz = depth(core, block)
    dy = jnp.where(core == 0, block[0], block[1])
    zz = lax.rem(z + dz + (4 * (part % 2) + NZ), NZ)
    yy = lax.rem(y + dy + NY, NY)
    xx = lax.rem(x + part // 2, NX)
    return pl.multiple_of((zz * (NY * NX) + yy * NX + xx) * SHARD, SHARD)


def twin_row(place, block, part):
    core = place[3] % 2
    other = twin(block)
    away = lax.rem(depth(core, block) - depth(1 - core, other) + 8, 8) // 4
    start = slot(other)[1]
    if slot(other)[0] == len(STAGES) - 1:
        start = start % (STAGE_ROWS[-1] // 2)
    return pl.multiple_of(start + (part // 2) * 2 * SHARD + ((part % 2) ^ away) * SHARD, SHARD)


def split3(value):
    high = value.astype(jnp.bfloat16)
    rest = value - high.astype(jnp.float32)
    middle = rest.astype(jnp.bfloat16)
    low = (rest - middle.astype(jnp.float32)).astype(jnp.bfloat16)
    return [high, middle, low]


def prepare_kernel(place, train_ref, turned_ref, sums_ref):
    me = place[3]
    for k, mask in enumerate((0, 2, 1, 3)):
        start = pl.multiple_of((me ^ mask) * 256, 256)
        for j in range(0, 2048, 512):
            block = train_ref[pl.ds(start, 256), j : j + 512].T
            turned_ref[k, j : j + 512, :] = block
            wide = block.astype(jnp.float32)
            part = jnp.sum(wide * wide, axis=0, keepdims=True)
            if j == 0:
                sums_ref[k : k + 1, :] = part
            else:
                sums_ref[k : k + 1, :] += part


def products(pieces, turned_ref, precond_ref, keep_ref, send_refs, sums_ref, rounded_ref):
    base = 0
    for piece in pieces:
        rows = piece.shape[0]
        here = slice(base, base + rows)
        squares = jnp.zeros((rows, 128), jnp.float32)
        for k in range(8):
            columns = slice(k * 256, (k + 1) * 256)
            value = jnp.dot(piece[:, columns], precond_ref[k], preferred_element_type=jnp.float32)
            rounded_ref[here, columns] = value.astype(jnp.bfloat16)
            value = value * value
            squares += value[:, :128] + value[:, 128:]
        sums_ref[here, :] = squares
        base += rows
    for base in range(0, base, 256):
        here = slice(base, base + 256)
        for k in (2, 3, 0, 1):
            value = jnp.dot(rounded_ref[here, :], turned_ref[k], preferred_element_type=jnp.float32)
            columns = slice((k % 2) * 256, (k % 2 + 1) * 256)
            if k < 2:
                keep_ref[here, columns] = value
            else:
                value = value.astype(jnp.bfloat16)
                rows = 256 // len(send_refs)
                for n, send_ref in enumerate(send_refs):
                    send_ref[slice(base, base + rows), columns] = value[n * rows : (n + 1) * rows]


def products_kernel(turned_ref, precond_ref, *refs):
    keep_ref, send_ref, sums_ref, rounded_ref = refs[-4:]
    products(refs[:-4], turned_ref, precond_ref, keep_ref, [send_ref], sums_ref, rounded_ref)


def last_products_kernel(
    place, turned_ref, precond_ref, low, high, sums0, sums1, sums2, train_ref, keep_ref, send_low, send_high, lanes_ref, rounded_ref, sums3, all_sums
):
    products((low, high), turned_ref, precond_ref, keep_ref, [send_low, send_high], sums3, rounded_ref)
    sums = (sums0, sums1, sums2, sums3)
    for block in ORDER:
        stage, at = slot(block)
        for part in range(4):
            here = slice(at + part * SHARD, at + (part + 1) * SHARD)
            all_sums[pl.ds(first_row(place, block, part), SHARD), :] = sums[stage][here, :]
    lanes = jnp.sum(all_sums[...].T, axis=0, keepdims=True)
    lanes_ref[...] = lanes
    extra = split3(lanes[:, :512]) + split3(lanes[:, 512:])
    extra += split3(jnp.concatenate([train_ref[2:3, :], train_ref[3:4, :]], axis=1))
    extra.append(jnp.zeros((SHARD - len(extra), 512), jnp.bfloat16))
    send_high[low.shape[0] :, :] = jnp.concatenate(extra, axis=0)


def add_blocks(place, blocks, keeps, gots, mine_ref, send_ref, at=0):
    first = at
    for block in blocks:
        stage, base = slot(block)
        there, start = slot(twin(block))
        if there == len(STAGES) - 1 and start >= STAGE_ROWS[-1] // 2:
            there += 1
        for part in range(4):
            own = keeps[stage][base + part * SHARD : base + (part + 1) * SHARD, :]
            total = own + gots[there][pl.ds(twin_row(place, block, part), SHARD), :].astype(jnp.float32)
            mine_ref[at : at + SHARD, :] = total[:, :256]
            send_ref[at - first : at - first + SHARD, :] = total[:, 256:].astype(jnp.bfloat16)
            at += SHARD


def early_kernel(place, keep0, keep1, keep2, got0, got1, got2, mine_ref, send_ref):
    add_blocks(place, EARLY, (keep0, keep1, keep2), (got0, got1, got2), mine_ref, send_ref)


def late_kernel(place, *refs):
    keeps, gots, rest = refs[: len(STAGES)], refs[len(STAGES) : 2 * len(STAGES) + 1], refs[2 * len(STAGES) + 1 :]
    lanes_ref, train_ref, mine_ref, send_low, send_high, lanes2_ref, train2_ref = rest
    add_blocks(place, LATE[:4], keeps, gots, mine_ref, send_low)
    add_blocks(place, LATE[4:], keeps, gots, mine_ref, send_high, 4 * BLOCK)
    got = gots[-1][keeps[-1].shape[0] // 2 :, :].astype(jnp.float32)
    extra = []
    for j in range(2):
        columns = slice(j * 512, (j + 1) * 512)
        total = lanes_ref[:, columns] + sum3(got, 3 * j)
        lanes2_ref[:, columns] = total
        extra += split3(total[:, :256]) + split3(total[:, 256:])
    train = sum3(got, 6)
    train2_ref[...] = train_ref[0:1, :] + train[:, :256]
    extra += split3(train_ref[1:2, :] + train[:, 256:])
    extra.append(jnp.zeros((SHARD - len(extra), 256), jnp.bfloat16))
    send_high[len(LATE[4:]) * BLOCK :, :] = jnp.concatenate(extra, axis=0)


def sum3(rows, at):
    return rows[at : at + 1] + (rows[at + 1 : at + 2] + rows[at + 2 : at + 3])


def merge_kernel(place, mine0, got0, mine1, all_ref):
    for blocks, mine, other in ((EARLY, mine0, got0), (LATE, mine1, None)):
        at = 0
        for block in blocks:
            for part in range(4):
                total = mine[at : at + SHARD, :]
                if other is not None:
                    total = total + other[at : at + SHARD, :].astype(jnp.float32)
                all_ref[pl.ds(first_row(place, block, part), SHARD), :] = total
                at += SHARD


def finish_kernel(place, all_ref, got1, got2, lanes_ref, train_ref, out_ref, sums_ref):
    sums_ref[...] = all_ref[...]
    for blocks, got in ((LATE[:4], got1), (LATE[4:], got2)):
        at = 0
        for block in blocks:
            for part in range(4):
                rows = pl.ds(first_row(place, block, part), SHARD)
                sums_ref[rows, :] += got[at : at + SHARD, :].astype(jnp.float32)
                at += SHARD
    got = got2[at:, :].astype(jnp.float32)
    query = lanes_ref[...] + jnp.concatenate([sum3(got, 3 * j) for j in range(4)], axis=1)
    query = 1.0 / jnp.sqrt(query + EPS)
    train = (1.0 / jnp.sqrt(train_ref[...] + sum3(got, 12) + EPS)) * math.sqrt(F)
    for i in range(0, 1024, 128):
        rows = slice(i, i + 128)
        scale = jnp.broadcast_to(query[:, rows], (128, 128)).T
        for j in range(0, 256, 128):
            columns = slice(j, j + 128)
            out_ref[rows, columns] = sums_ref[rows, columns] * scale * train[:, columns]


def call(kernel, outs, inputs, scratch=(), smem=0, moved=1):
    return pl.pallas_call(
        kernel,
        out_shape=[jax.ShapeDtypeStruct(s, d) for s, d in outs],
        in_specs=[SMEM] * smem + [VMEM] * (len(inputs) - smem),
        out_specs=[VMEM] * len(outs),
        scratch_shapes=list(scratch),
        compiler_params=pltpu.CompilerParams(vmem_limit_bytes=24 * MIB),
        cost_estimate=pl.CostEstimate(flops=1, bytes_accessed=moved, transcendentals=0),
    )(*inputs)


def on_device(query_grads, train_grads, precond):
    f32, bf16 = jnp.float32, jnp.bfloat16
    row = lax.axis_index("rows")
    place = jnp.stack([row // (NY * NX), row // NX % NY, row % NX, lax.axis_index("feat")]).astype(jnp.int32)

    def prepare(four):
        train, _ = together(train_grads, four)
        return call(
            prepare_kernel,
            [((4, 2048, 256), bf16), ((4, 256), f32)],
            [place, train],
            smem=1,
        )

    def product(pieces, prepared):
        rows = sum(piece.shape[0] for piece in pieces)
        return call(
            products_kernel,
            [((rows, 512), f32), ((rows, 512), bf16), ((rows, 128), f32)],
            [prepared[0], precond, *pieces],
            scratch=[pltpu.VMEM((rows, 2048), bf16)],
        )

    prepared, done, *stages, last = gather(query_grads, prepare, product)
    turned, train_sums = prepared
    keep, send, squares = done
    keeps, gots, sums = [keep], [across(send, 1)], [squares]
    for pieces in stages:
        *pieces, _ = together(*pieces, send)
        keep, send, squares = product(pieces, prepared)
        keeps.append(keep)
        gots.append(across(send, 1))
        sums.append(squares)
    early = len(EARLY) * BLOCK
    late = len(LATE) * BLOCK
    mine0, send = call(
        early_kernel, [((early, 256), f32), ((early, 256), bf16)], [place, *keeps, *gots], smem=1
    )
    got0 = across(send, 2)
    low, high, _ = together(*last, send)
    rows = STAGE_ROWS[-1]
    keep, send_low, send_high, lanes = call(
        last_products_kernel,
        [((rows, 512), f32), ((rows // 2, 512), bf16), ((rows // 2 + SHARD, 512), bf16), ((1, 1024), f32)],
        [place, turned, precond, low, high, *sums, train_sums],
        scratch=[pltpu.VMEM((rows, 2048), bf16), pltpu.VMEM((rows, 128), f32), pltpu.VMEM((1024, 128), f32)],
        smem=1,
    )
    mine1, send_low, send_high, lanes, train = call(
        late_kernel,
        [
            ((late, 256), f32),
            ((4 * BLOCK, 256), bf16),
            ((late - 4 * BLOCK + SHARD, 256), bf16),
            ((1, 1024), f32),
            ((1, 256), f32),
        ],
        [place, *keeps, keep, *gots, across(send_low, 1), across(send_high, 1), lanes, train_sums],
        smem=1,
    )
    got1, got2 = across(send_low, 2), across(send_high, 2)
    merged = call(merge_kernel, [((1024, 256), f32)], [place, mine0, got0, mine1], smem=1)[0]
    return call(
        finish_kernel,
        [((1024, 256), f32)],
        [place, merged, got1, got2, lanes, train],
        scratch=[pltpu.VMEM((1024, 256), f32)],
        smem=1,
    )[0]


def solution(mesh):
    in_specs = (P("rows", "feat"), P("rows", "feat"), P("feat", None, None))
    out_specs = P(None, ("rows", "feat"))
    return jax.shard_map(
        on_device, mesh=mesh, in_specs=in_specs, out_specs=out_specs, check_vma=False
    )
```

time: 86.5 us -> 68.4 us (0.79); the launches traced: 84.9 us -> 68.2 us
  waiting for transfers between devices: 43 us -> 19.5 us
  starting transfers between devices: 25.5 us -> 31.7 us
  Pallas kernels: 10.4 us -> 12.8 us
  other arithmetic: 2.7 us -> 1 us
    ppermute x9 -> x11, waiting for transfers between devices: 27.7 us -> 11.9 us  [shift(): return lax.ppermute(value, ('rows', 'feat'), pairs)]
    ppermute x2 -> x8, waiting for transfers between devices: 15.3 us -> 7.53 us  [across(): return lax.ppermute(value, 'feat', [(f, f ^ mask) for f in range(4)])]
    ppermute x2 -> x8, starting transfers between devices: 1.67 us -> 5.06 us  [across(): return lax.ppermute(value, 'feat', [(f, f ^ mask) for f in range(4)])]
    ppermute x9 -> x11, starting transfers between devices: 23.8 us -> 26.7 us  [shift(): return lax.ppermute(value, ('rows', 'feat'), pairs)]
    pallas_call x5 -> x9, Pallas kernels: 10.4 us -> 12.8 us  [call(): pl.pallas_call(kernel, out_shape=[jax.ShapeDtypeStruct(s, d) for s, d in...]
    concatenate x4 -> x3, other arithmetic: 2.62 us -> 0.92 us  [join(): return jnp.concatenate(parts, axis=0)]
    unnamed x10 -> x8, local copies, waits for them, and re-layouts: 3.12 us -> 3.08 us
  transfers between devices with their start and end apart: 11 -> 19, of which waited for: 8 -> 12; matrix products, arithmetic and copies ran while one was open for 3% -> 1% of each run, Pallas kernels for 2% -> 16%
where the time goes in v2:
time: 68.4 us; the launch traced here: 68.2 us
  starting transfers between devices  31.7 us (46%)
  waiting for transfers between devices  19.5 us (29%)
  Pallas kernels  12.8 us (19%)
  local copies, waits for them, and re-layouts  3.09 us (5%)
  other arithmetic  1 us (1%)
    ppermute x11, starting transfers between devices, shift(): return lax.ppermute(value, ('rows', 'feat'), pairs)  26.7 us
    pallas_call x9, Pallas kernels, call(): pl.pallas_call(kernel, out_shape=[jax.ShapeDtypeStruct(s, d) for s, d in...  12.8 us
    ppermute x11, waiting for transfers between devices, shift(): return lax.ppermute(value, ('rows', 'feat'), pairs)  11.9 us
    ppermute x8, waiting for transfers between devices, across(): return lax.ppermute(value, 'feat', [(f, f ^ mask) for f in range(4)])  7.53 us
    ppermute x8, starting transfers between devices, across(): return lax.ppermute(value, 'feat', [(f, f ^ mask) for f in range(4)])  5.06 us
    unnamed x8, local copies, waits for them, and re-layouts  3.08 us
  transfers between devices with their start and end apart: 19, of which 12 were waited for; matrix products, arithmetic and copies ran while one was open for 1% of the time, Pallas kernels for 16%

profile of v2, /device:TPU:8, one launch (start us, length us, event | category | flops | bytes accessed | tf_op | source)
XLA Modules:
  0.0 68.2 jit_solution(15677553389403275299)
XLA Ops:
  0.0 7.2 %collective-permute-start = (bf16[16,2048]{1,0:T(8,128)(2,1)}, bf16[16,2048]{1,0:T(8,128)(2,1)S(1)}, u32[]{:S(2)}, u32[]{:S(2)}) collective-permute-start(bf16[16,2048]{1,0:T(8,128)(2,1)} %param.3), channel_id=1, source_target_pairs={{0,128},{1,129},{2,130},{3,131},{4,132},{5,133},{6,134},{7,135},{8... | collective-permute-start | bytes 196616 | tf_op jit(solution)/shard_map/ppermute | solution.py:35
  7.2 0.9 %constant_dynamic-update-slice_fusion.2 = bf16[64,2048]{1,0:T(8,128)(2,1)S(1)} fusion(bf16[16,2048]{1,0:T(8,128)(2,1)} %param.3), kind=kLoop, calls=%fused_computation.5 | loop fusion | bytes 131072
  8.1 1.9 %collective-permute-done = bf16[16,2048]{1,0:T(8,128)(2,1)S(1)} collective-permute-done((bf16[16,2048]{1,0:T(8,128)(2,1)}, bf16[16,2048]{1,0:T(8,128)(2,1)S(1)}, u32[]{:S(2)}, u32[]{:S(2)}) %collective-permute-start) | collective-permute-done | bytes 65568 | tf_op jit(solution)/shard_map/ppermute | solution.py:35
  9.9 0.8 %pad_maximum_fusion.2 = bf16[32,2048]{1,0:T(8,128)(2,1)S(1)} fusion(bf16[16,2048]{1,0:T(8,128)(2,1)S(1)} %collective-permute-done, bf16[16,2048]{1,0:T(8,128)(2,1)} %param.3), kind=kLoop, calls=%fused_computation.2 | loop fusion | flops 262144 | bytes 262144 | tf_op jit(solution)/shard_map/concatenate | solution.py:43
  10.8 3.1 %collective-permute-start.1 = (bf16[32,2048]{1,0:T(8,128)(2,1)S(1)}, bf16[32,2048]{1,0:T(8,128)(2,1)S(1)}, u32[]{:S(2)}, u32[]{:S(2)}) collective-permute-start(bf16[32,2048]{1,0:T(8,128)(2,1)S(1)} %pad_maximum_fusion.2), channel_id=1, source_target_pairs={{0,4},{1,5},{2,6},{3,7},{4,0},{5,1},{6,2},{7,3},{8,12},{9,13},{10,... | collective-permute-start | bytes 393224 | tf_op jit(solution)/shard_map/ppermute | solution.py:35
  13.9 3.4 %collective-permute-done.1 = bf16[32,2048]{1,0:T(8,128)(2,1)S(1)} collective-permute-done((bf16[32,2048]{1,0:T(8,128)(2,1)S(1)}, bf16[32,2048]{1,0:T(8,128)(2,1)S(1)}, u32[]{:S(2)}, u32[]{:S(2)}) %collective-permute-start.1) | collective-permute-done | bytes 131104 | tf_op jit(solution)/shard_map/ppermute | solution.py:35
  17.4 1.7 %collective-permute-start.2 = (bf16[64,2048]{1,0:T(8,128)(2,1)S(1)}, bf16[64,2048]{1,0:T(8,128)(2,1)S(1)}, u32[]{:S(2)}, u32[]{:S(2)}) collective-permute-start(bf16[64,2048]{1,0:T(8,128)(2,1)S(1)} %constant_dynamic-update-slice_fusion), channel_id=1, source_target_pairs={{0,8},{1,33},{2,10},{3,35},{4,12},{5,37},{6,14},{7,39},{8,16},{9,4... | collective-permute-start | bytes 786440 | tf_op jit(solution)/shard_map/ppermute | solution.py:35
  19.0 1.2 %collective-permute-start.4 = (bf16[64,2048]{1,0:T(8,128)(2,1)S(1)}, bf16[64,2048]{1,0:T(8,128)(2,1)S(1)}, u32[]{:S(2)}, u32[]{:S(2)}) collective-permute-start(bf16[64,2048]{1,0:T(8,128)(2,1)S(1)} %constant_dynamic-update-slice_fusion), channel_id=1, source_target_pairs={{0,16},{1,65},{2,18},{3,67},{4,20},{5,69},{6,22},{7,71},{8,24},{9,... | collective-permute-start | bytes 786440 | tf_op jit(solution)/shard_map/ppermute | solution.py:35
  20.2 2.1 %collective-permute-start.3 = (bf16[64,2048]{1,0:T(8,128)(2,1)S(1)}, bf16[64,2048]{1,0:T(8,128)(2,1)S(1)}, u32[]{:S(2)}, u32[]{:S(2)}) collective-permute-start(bf16[64,2048]{1,0:T(8,128)(2,1)S(1)} %constant_dynamic-update-slice_fusion), channel_id=1, source_target_pairs={{0,24},{1,225},{2,26},{3,227},{4,28},{5,229},{6,30},{7,231},{8,0},... | collective-permute-start | bytes 786440 | tf_op jit(solution)/shard_map/ppermute | solution.py:35
  22.4 0.1 pad_add_fusion.place
  22.5 2.2 %copy-done.1 = bf16[1024,2048]{1,0:T(8,128)(2,1)S(1)} copy-done((bf16[1024,2048]{1,0:T(8,128)(2,1)S(1)}, bf16[1024,2048]{1,0:T(8,128)(2,1)}, u32[]{:S(2)}) %copy-start.1) | copy-done | bytes 4194328
  24.6 1.8 %shard_map.37 = (bf16[4,2048,256]{2,1,0:T(8,128)(2,1)S(1)}, f32[4,256]{1,0:T(4,128)S(1)}) custom-call(s32[4]{0:T(128)S(1)} %pad_add_fusion.place, bf16[1024,2048]{1,0:T(8,128)(2,1)S(1)} %copy-done.1), custom_call_target="tpu_custom_call" | custom-call | flops 1 | bytes 1 | tf_op jit(solution)/shard_map/pallas_call | solution.py:276
  26.4 0.0 collective-permute-done.2
  26.5 0.5 collective-permute-done.4
  27.0 2.4 %collective-permute-done.3 = bf16[64,2048]{1,0:T(8,128)(2,1)S(1)} collective-permute-done((bf16[64,2048]{1,0:T(8,128)(2,1)S(1)}, bf16[64,2048]{1,0:T(8,128)(2,1)S(1)}, u32[]{:S(2)}, u32[]{:S(2)}) %collective-permute-start.3) | collective-permute-done | bytes 262176 | tf_op jit(solution)/shard_map/ppermute | solution.py:35
  29.5 1.6 %collective-permute-start.5 = (bf16[128,2048]{1,0:T(8,128)(2,1)S(1)}, bf16[128,2048]{1,0:T(8,128)(2,1)S(1)}, u32[]{:S(2)}, u32[]{:S(2)}) collective-permute-start(bf16[128,2048]{1,0:T(8,128)(2,1)S(1)} %pad_maximum_fusion.refs_0_), channel_id=1, source_target_pairs={{0,32},{1,9},{2,34},{3,11},{4,36},{5,13},{6,38},{7,15},{8,40},{9,1... | collective-permute-start | bytes 1572872 | tf_op jit(solution)/shard_map/ppermute | solution.py:35
  31.1 2.6 %collective-permute-start.6 = (bf16[128,2048]{1,0:T(8,128)(2,1)S(1)}, bf16[128,2048]{1,0:T(8,128)(2,1)S(1)}, u32[]{:S(2)}, u32[]{:S(2)}) collective-permute-start(bf16[128,2048]{1,0:T(8,128)(2,1)S(1)} %pad_maximum_fusion.1.refs_1_), channel_id=1, source_target_pairs={{0,224},{1,25},{2,226},{3,27},{4,228},{5,29},{6,230},{7,31},{8,232... | collective-permute-start | bytes 1572872 | tf_op jit(solution)/shard_map/ppermute | solution.py:35
  33.7 3.6 %collective-permute-start.8 = (bf16[128,2048]{1,0:T(8,128)(2,1)S(1)}, bf16[128,2048]{1,0:T(8,128)(2,1)S(1)}, u32[]{:S(2)}, u32[]{:S(2)}) collective-permute-start(bf16[128,2048]{1,0:T(8,128)(2,1)S(1)} %pad_maximum_fusion.refs_0_), channel_id=1, source_target_pairs={{0,224},{1,25},{2,226},{3,27},{4,228},{5,29},{6,230},{7,31},{8,232... | collective-permute-start | bytes 1572872 | tf_op jit(solution)/shard_map/ppermute | solution.py:35
  37.3 0.0 collective-permute-start.7
  37.3 1.5 %shard_map.38 = (f32[256,512]{1,0:T(8,128)S(1)}, bf16[256,512]{1,0:T(8,128)(2,1)S(1)}, f32[256,128]{1,0:T(8,128)S(1)}) custom-call(bf16[4,2048,256]{2,1,0:T(8,128)(2,1)S(1)} %get-tuple-element.48.turned_ref, bf16[8,256,256]{2,1,0:T(8,128)(2,1)S(1)} %copy-done, bf16[128,2048]{1,0:T(8,128)(2,1)S(1)} %pad_maximum_fusion.refs_0_, ...), custom_call_target="tpu_custom_call" | custom-call | flops 1 | bytes 1 | tf_op jit(solution)/shard_map/pallas_call | solution.py:276
  38.8 1.9 %collective-permute-done.5.refs_0_ = bf16[128,2048]{1,0:T(8,128)(2,1)S(1)} collective-permute-done((bf16[128,2048]{1,0:T(8,128)(2,1)S(1)}, bf16[128,2048]{1,0:T(8,128)(2,1)S(1)}, u32[]{:S(2)}, u32[]{:S(2)}) %collective-permute-start.5) | collective-permute-done | bytes 524320 | tf_op jit(solution)/shard_map/ppermute | solution.py:35
  40.8 0.0 collective-permute-done.6.refs_1_
  40.8 1.1 %collective-permute-start.13 = (bf16[128,2048]{1,0:T(8,128)(2,1)S(1)}, bf16[128,2048]{1,0:T(8,128)(2,1)S(1)}, u32[]{:S(2)}, u32[]{:S(2)}) collective-permute-start(bf16[128,2048]{1,0:T(8,128)(2,1)S(1)} %collective-permute-done.5.refs_0_), channel_id=1, source_target_pairs={{0,32},{1,9},{2,34},{3,11},{4,36},{5,13},{6,38},{7,15},{8,40},{9,1... | collective-permute-start | bytes 1572872 | tf_op jit(solution)/shard_map/ppermute | solution.py:35
  41.9 2.4 %collective-permute-start.14 = (bf16[128,2048]{1,0:T(8,128)(2,1)S(1)}, bf16[128,2048]{1,0:T(8,128)(2,1)S(1)}, u32[]{:S(2)}, u32[]{:S(2)}) collective-permute-start(bf16[128,2048]{1,0:T(8,128)(2,1)S(1)} %collective-permute-done.6.refs_1_), channel_id=1, source_target_pairs={{0,224},{1,25},{2,226},{3,27},{4,228},{5,29},{6,230},{7,31},{8,232... | collective-permute-start | bytes 1572872 | tf_op jit(solution)/shard_map/ppermute | solution.py:35
  44.3 0.0 collective-permute-start.9
  44.3 1.6 %shard_map.39 = (f32[256,512]{1,0:T(8,128)S(1)}, bf16[256,512]{1,0:T(8,128)(2,1)S(1)}, f32[256,128]{1,0:T(8,128)S(1)}) custom-call(bf16[4,2048,256]{2,1,0:T(8,128)(2,1)S(1)} %get-tuple-element.48.turned_ref, bf16[8,256,256]{2,1,0:T(8,128)(2,1)S(1)} %copy-done, bf16[128,2048]{1,0:T(8,128)(2,1)S(1)} %collective-permute-done.5.refs_0_, ...), custom_call_target="tpu_custom_call" | custom-call | flops 1 | bytes 1 | tf_op jit(solution)/shard_map/pallas_call | solution.py:276
  45.9 0.1 collective-permute-done.8.refs_1_
  46.0 1.6 %collective-permute-done.7.refs_0_ = bf16[128,2048]{1,0:T(8,128)(2,1)S(1)} collective-permute-done((bf16[128,2048]{1,0:T(8,128)(2,1)S(1)}, bf16[128,2048]{1,0:T(8,128)(2,1)S(1)}, u32[]{:S(2)}, u32[]{:S(2)}) %collective-permute-start.7) | collective-permute-done | bytes 524320 | tf_op jit(solution)/shard_map/ppermute | solution.py:35
  47.7 1.6 %shard_map.40 = (f32[256,512]{1,0:T(8,128)S(1)}, bf16[256,512]{1,0:T(8,128)(2,1)S(1)}, f32[256,128]{1,0:T(8,128)S(1)}) custom-call(bf16[4,2048,256]{2,1,0:T(8,128)(2,1)S(1)} %get-tuple-element.48.turned_ref, bf16[8,256,256]{2,1,0:T(8,128)(2,1)S(1)} %copy-done, bf16[128,2048]{1,0:T(8,128)(2,1)S(1)} %collective-permute-done.7.refs_0_, ...), custom_call_target="tpu_custom_call" | custom-call | flops 1 | bytes 1 | tf_op jit(solution)/shard_map/pallas_call | solution.py:276
  49.2 0.1 collective-permute-start.11
  49.3 0.5 collective-permute-start.10
  49.8 0.0 collective-permute-done.9.got0.refs_4_
  49.8 1.0 %collective-permute-done.11.got2.refs_6_ = bf16[256,512]{1,0:T(8,128)(2,1)S(1)} collective-permute-done((bf16[256,512]{1,0:T(8,128)(2,1)S(1)}, bf16[256,512]{1,0:T(8,128)(2,1)S(1)}, u32[]{:S(2)}, u32[]{:S(2)}) %collective-permute-start.11) | collective-permute-done | bytes 262176 | tf_op jit(solution)/shard_map/ppermute | solution.py:39
  50.8 0.4 collective-permute-done.10.got1.refs_5_
  51.2 0.7 shard_map.41
  51.9 1.8 %collective-permute-start.12 = (bf16[576,256]{1,0:T(8,128)(2,1)S(1)}, bf16[576,256]{1,0:T(8,128)(2,1)S(1)}, u32[]{:S(2)}, u32[]{:S(2)}) collective-permute-start(bf16[576,256]{1,0:T(8,128)(2,1)S(1)} %get-tuple-element.65), channel_id=1, source_target_pairs={{0,2},{1,3},{2,0},{3,1},{4,6},{5,7},{6,4},{7,5},{8,10},{9,11},{10,... | collective-permute-start | bytes 884744 | tf_op jit(solution)/shard_map/ppermute | solution.py:39
  53.7 0.0 collective-permute-done.13.low
  53.7 2.2 %shard_map.42 = (f32[256,512]{1,0:T(8,128)S(1)}, bf16[128,512]{1,0:T(8,128)(2,1)S(1)}, bf16[144,512]{1,0:T(8,128)(2,1)S(1)}, f32[1,1024]{1,0:T(1,128)S(1)}) custom-call(s32[4]{0:T(128)S(1)} %pad_add_fusion.place, bf16[4,2048,256]{2,1,0:T(8,128)(2,1)S(1)} %get-tuple-element.48.turned_ref, bf16[8,256,256]{2,1,0:T(8,128)(2,1)S(1)} %copy-done, ...), custom_call_target="tpu_custom_call" | custom-call | flops 1 | bytes 1 | tf_op jit(solution)/shard_map/pallas_call | solution.py:276
  55.9 0.1 collective-permute-start.16
  56.0 0.5 collective-permute-start.15
  56.5 1.0 %collective-permute-done.15.refs_7_ = bf16[128,512]{1,0:T(8,128)(2,1)S(1)} collective-permute-done((bf16[128,512]{1,0:T(8,128)(2,1)S(1)}, bf16[128,512]{1,0:T(8,128)(2,1)S(1)}, u32[]{:S(2)}, u32[]{:S(2)}) %collective-permute-start.15) | collective-permute-done | bytes 131104 | tf_op jit(solution)/shard_map/ppermute | solution.py:39
  57.6 0.7 %shard_map.43 = (f32[448,256]{1,0:T(8,128)S(1)}, bf16[256,256]{1,0:T(8,128)(2,1)S(1)}, bf16[208,256]{1,0:T(8,128)(2,1)S(1)}, f32[1,1024]{1,0:T(1,128)S(1)}, f32[1,256]{1,0:T(1,128)S(1)}) custom-call(s32[4]{0:T(128)S(1)} %pad_add_fusion.place, f32[256,512]{1,0:T(8,128)S(1)} %get-tuple-element.52.keep0.refs_0_, ...), custom_call_target="tpu_custom_call" | custom-call | flops 1 | bytes 1 | tf_op jit(solution)/shard_map/pallas_call | solution.py:276
  58.3 1.4 %collective-permute-start.17 = (bf16[256,256]{1,0:T(8,128)(2,1)S(1)}, bf16[256,256]{1,0:T(8,128)(2,1)S(1)}, u32[]{:S(2)}, u32[]{:S(2)}) collective-permute-start(bf16[256,256]{1,0:T(8,128)(2,1)S(1)} %get-tuple-element.77), channel_id=1, source_target_pairs={{0,2},{1,3},{2,0},{3,1},{4,6},{5,7},{6,4},{7,5},{8,10},{9,11},{10,... | collective-permute-start | bytes 393224 | tf_op jit(solution)/shard_map/ppermute | solution.py:39
  59.7 0.7 %collective-permute-start.18 = (bf16[208,256]{1,0:T(8,128)(2,1)S(1)}, bf16[208,256]{1,0:T(8,128)(2,1)S(1)}, u32[]{:S(2)}, u32[]{:S(2)}) collective-permute-start(bf16[208,256]{1,0:T(8,128)(2,1)S(1)} %get-tuple-element.78), channel_id=1, source_target_pairs={{0,2},{1,3},{2,0},{3,1},{4,6},{5,7},{6,4},{7,5},{8,10},{9,11},{10,... | collective-permute-start | bytes 319496 | tf_op jit(solution)/shard_map/ppermute | solution.py:39
  60.4 0.6 collective-permute-done.12.got0
  61.0 0.9 %shard_map.44.all_ref = f32[1024,256]{1,0:T(8,128)S(1)} custom-call(s32[4]{0:T(128)S(1)} %pad_add_fusion.place, f32[576,256]{1,0:T(8,128)S(1)} %get-tuple-element.64.mine0, bf16[576,256]{1,0:T(8,128)(2,1)S(1)} %collective-permute-done.12.got0, f32[448,256]{1,0:T(8,128)S(1)} %get-tuple-element.76.mine1), custom_call_target="tpu_custom_call" | custom-call | flops 1 | bytes 1 | tf_op jit(solution)/shard_map/pallas_call | solution.py:276
  61.9 4.4 %collective-permute-done.18.got2 = bf16[208,256]{1,0:T(8,128)(2,1)S(1)} collective-permute-done((bf16[208,256]{1,0:T(8,128)(2,1)S(1)}, bf16[208,256]{1,0:T(8,128)(2,1)S(1)}, u32[]{:S(2)}, u32[]{:S(2)}) %collective-permute-start.18) | collective-permute-done | bytes 106528 | tf_op jit(solution)/shard_map/ppermute | solution.py:39
  66.4 1.8 %shard_map.45 = f32[1024,256]{1,0:T(8,128)} custom-call(s32[4]{0:T(128)S(1)} %pad_add_fusion.place, f32[1024,256]{1,0:T(8,128)S(1)} %shard_map.44.all_ref, bf16[256,256]{1,0:T(8,128)(2,1)S(1)} %collective-permute-done.17.got1, bf16[208,256]{1,0:T(8,128)(2,1)S(1)} %collective-permute-done.18.got2, f32[1,1024]{1,0:T(1,128)S(1)} %get-tuple-element.79.lanes_ref, ...), custom_call_target="tpu_custom_call" | custom-call | flops 1 | bytes 1 | tf_op jit(solution)/shard_map/pallas_call | solution.py:276
  (12 shorter events, 0.1 us)
Async XLA Ops:
  0.0 37.3 %copy-start = (bf16[8,256,256]{2,1,0:T(8,128)(2,1)S(1)}, bf16[8,256,256]{2,1,0:T(8,128)(2,1)}, u32[]{:S(2)}) copy-start(bf16[8,256,256]{2,1,0:T(8,128)(2,1)} %precond_ref.7) | copy-start | bytes 3145732
  0.0 9.9 %collective-permute-start = (bf16[16,2048]{1,0:T(8,128)(2,1)}, bf16[16,2048]{1,0:T(8,128)(2,1)S(1)}, u32[]{:S(2)}, u32[]{:S(2)}) collective-permute-start(bf16[16,2048]{1,0:T(8,128)(2,1)} %param.3), channel_id=1, source_target_pairs={{0,128},{1,129},{2,130},{3,131},{4,132},{5,133},{6,134},{7,135},{8... | collective-permute-start | bytes 196616 | tf_op jit(solution)/shard_map/ppermute | solution.py:35
  10.8 6.6 %collective-permute-start.1 = (bf16[32,2048]{1,0:T(8,128)(2,1)S(1)}, bf16[32,2048]{1,0:T(8,128)(2,1)S(1)}, u32[]{:S(2)}, u32[]{:S(2)}) collective-permute-start(bf16[32,2048]{1,0:T(8,128)(2,1)S(1)} %pad_maximum_fusion.2), channel_id=1, source_target_pairs={{0,4},{1,5},{2,6},{3,7},{4,0},{5,1},{6,2},{7,3},{8,12},{9,13},{10,... | collective-permute-start | bytes 393224 | tf_op jit(solution)/shard_map/ppermute | solution.py:35
  17.4 9.1 %collective-permute-start.2 = (bf16[64,2048]{1,0:T(8,128)(2,1)S(1)}, bf16[64,2048]{1,0:T(8,128)(2,1)S(1)}, u32[]{:S(2)}, u32[]{:S(2)}) collective-permute-start(bf16[64,2048]{1,0:T(8,128)(2,1)S(1)} %constant_dynamic-update-slice_fusion), channel_id=1, source_target_pairs={{0,8},{1,33},{2,10},{3,35},{4,12},{5,37},{6,14},{7,39},{8,16},{9,4... | collective-permute-start | bytes 786440 | tf_op jit(solution)/shard_map/ppermute | solution.py:35
  19.0 8.0 %collective-permute-start.4 = (bf16[64,2048]{1,0:T(8,128)(2,1)S(1)}, bf16[64,2048]{1,0:T(8,128)(2,1)S(1)}, u32[]{:S(2)}, u32[]{:S(2)}) collective-permute-start(bf16[64,2048]{1,0:T(8,128)(2,1)S(1)} %constant_dynamic-update-slice_fusion), channel_id=1, source_target_pairs={{0,16},{1,65},{2,18},{3,67},{4,20},{5,69},{6,22},{7,71},{8,24},{9,... | collective-permute-start | bytes 786440 | tf_op jit(solution)/shard_map/ppermute | solution.py:35
  20.2 9.2 %collective-permute-start.3 = (bf16[64,2048]{1,0:T(8,128)(2,1)S(1)}, bf16[64,2048]{1,0:T(8,128)(2,1)S(1)}, u32[]{:S(2)}, u32[]{:S(2)}) collective-permute-start(bf16[64,2048]{1,0:T(8,128)(2,1)S(1)} %constant_dynamic-update-slice_fusion), channel_id=1, source_target_pairs={{0,24},{1,225},{2,26},{3,227},{4,28},{5,229},{6,30},{7,231},{8,0},... | collective-permute-start | bytes 786440 | tf_op jit(solution)/shard_map/ppermute | solution.py:35
  22.5 2.2 %copy-start.1 = (bf16[1024,2048]{1,0:T(8,128)(2,1)S(1)}, bf16[1024,2048]{1,0:T(8,128)(2,1)}, u32[]{:S(2)}) copy-start(bf16[1024,2048]{1,0:T(8,128)(2,1)} %train_ref) | copy-start | bytes 12582916
  24.6 1.8 %copy-start.2 = (bf16[16,2048]{1,0:T(8,128)(2,1)S(1)}, bf16[16,2048]{1,0:T(8,128)(2,1)}, u32[]{:S(2)}) copy-start(bf16[16,2048]{1,0:T(8,128)(2,1)} %param.3) | copy-start | bytes 196612
  29.5 11.3 %collective-permute-start.5 = (bf16[128,2048]{1,0:T(8,128)(2,1)S(1)}, bf16[128,2048]{1,0:T(8,128)(2,1)S(1)}, u32[]{:S(2)}, u32[]{:S(2)}) collective-permute-start(bf16[128,2048]{1,0:T(8,128)(2,1)S(1)} %pad_maximum_fusion.refs_0_), channel_id=1, source_target_pairs={{0,32},{1,9},{2,34},{3,11},{4,36},{5,13},{6,38},{7,15},{8,40},{9,1... | collective-permute-start | bytes 1572872 | tf_op jit(solution)/shard_map/ppermute | solution.py:35
  31.1 9.7 %collective-permute-start.6 = (bf16[128,2048]{1,0:T(8,128)(2,1)S(1)}, bf16[128,2048]{1,0:T(8,128)(2,1)S(1)}, u32[]{:S(2)}, u32[]{:S(2)}) collective-permute-start(bf16[128,2048]{1,0:T(8,128)(2,1)S(1)} %pad_maximum_fusion.1.refs_1_), channel_id=1, source_target_pairs={{0,224},{1,25},{2,226},{3,27},{4,228},{5,29},{6,230},{7,31},{8,232... | collective-permute-start | bytes 1572872 | tf_op jit(solution)/shard_map/ppermute | solution.py:35
  33.7 12.3 %collective-permute-start.8 = (bf16[128,2048]{1,0:T(8,128)(2,1)S(1)}, bf16[128,2048]{1,0:T(8,128)(2,1)S(1)}, u32[]{:S(2)}, u32[]{:S(2)}) collective-permute-start(bf16[128,2048]{1,0:T(8,128)(2,1)S(1)} %pad_maximum_fusion.refs_0_), channel_id=1, source_target_pairs={{0,224},{1,25},{2,226},{3,27},{4,228},{5,29},{6,230},{7,31},{8,232... | collective-permute-start | bytes 1572872 | tf_op jit(solution)/shard_map/ppermute | solution.py:35
  37.3 10.4 %collective-permute-start.7 = (bf16[128,2048]{1,0:T(8,128)(2,1)S(1)}, bf16[128,2048]{1,0:T(8,128)(2,1)S(1)}, u32[]{:S(2)}, u32[]{:S(2)}) collective-permute-start(bf16[128,2048]{1,0:T(8,128)(2,1)S(1)} %pad_maximum_fusion.1.refs_1_), channel_id=1, source_target_pairs={{0,32},{1,9},{2,34},{3,11},{4,36},{5,13},{6,38},{7,15},{8,40},{9,1... | collective-permute-start | bytes 1572872 | tf_op jit(solution)/shard_map/ppermute | solution.py:35
  40.8 12.9 %collective-permute-start.13 = (bf16[128,2048]{1,0:T(8,128)(2,1)S(1)}, bf16[128,2048]{1,0:T(8,128)(2,1)S(1)}, u32[]{:S(2)}, u32[]{:S(2)}) collective-permute-start(bf16[128,2048]{1,0:T(8,128)(2,1)S(1)} %collective-permute-done.5.refs_0_), channel_id=1, source_target_pairs={{0,32},{1,9},{2,34},{3,11},{4,36},{5,13},{6,38},{7,15},{8,40},{9,1... | collective-permute-start | bytes 1572872 | tf_op jit(solution)/shard_map/ppermute | solution.py:35
  41.9 11.8 %collective-permute-start.14 = (bf16[128,2048]{1,0:T(8,128)(2,1)S(1)}, bf16[128,2048]{1,0:T(8,128)(2,1)S(1)}, u32[]{:S(2)}, u32[]{:S(2)}) collective-permute-start(bf16[128,2048]{1,0:T(8,128)(2,1)S(1)} %collective-permute-done.6.refs_1_), channel_id=1, source_target_pairs={{0,224},{1,25},{2,226},{3,27},{4,228},{5,29},{6,230},{7,31},{8,232... | collective-permute-start | bytes 1572872 | tf_op jit(solution)/shard_map/ppermute | solution.py:35
  44.3 5.5 %collective-permute-start.9 = (bf16[256,512]{1,0:T(8,128)(2,1)S(1)}, bf16[256,512]{1,0:T(8,128)(2,1)S(1)}, u32[]{:S(2)}, u32[]{:S(2)}) collective-permute-start(bf16[256,512]{1,0:T(8,128)(2,1)S(1)} %get-tuple-element.55), channel_id=1, source_target_pairs={{0,1},{1,0},{2,3},{3,2},{4,5},{5,4},{6,7},{7,6},{8,9},{9,8},{10,11... | collective-permute-start | bytes 786440 | tf_op jit(solution)/shard_map/ppermute | solution.py:39
  49.2 1.6 %collective-permute-start.11 = (bf16[256,512]{1,0:T(8,128)(2,1)S(1)}, bf16[256,512]{1,0:T(8,128)(2,1)S(1)}, u32[]{:S(2)}, u32[]{:S(2)}) collective-permute-start(bf16[256,512]{1,0:T(8,128)(2,1)S(1)} %get-tuple-element.63), channel_id=1, source_target_pairs={{0,1},{1,0},{2,3},{3,2},{4,5},{5,4},{6,7},{7,6},{8,9},{9,8},{10,11... | collective-permute-start | bytes 786440 | tf_op jit(solution)/shard_map/ppermute | solution.py:39
  49.3 1.9 %collective-permute-start.10 = (bf16[256,512]{1,0:T(8,128)(2,1)S(1)}, bf16[256,512]{1,0:T(8,128)(2,1)S(1)}, u32[]{:S(2)}, u32[]{:S(2)}) collective-permute-start(bf16[256,512]{1,0:T(8,128)(2,1)S(1)} %get-tuple-element.59), channel_id=1, source_target_pairs={{0,1},{1,0},{2,3},{3,2},{4,5},{5,4},{6,7},{7,6},{8,9},{9,8},{10,11... | collective-permute-start | bytes 786440 | tf_op jit(solution)/shard_map/ppermute | solution.py:39
  51.9 9.1 %collective-permute-start.12 = (bf16[576,256]{1,0:T(8,128)(2,1)S(1)}, bf16[576,256]{1,0:T(8,128)(2,1)S(1)}, u32[]{:S(2)}, u32[]{:S(2)}) collective-permute-start(bf16[576,256]{1,0:T(8,128)(2,1)S(1)} %get-tuple-element.65), channel_id=1, source_target_pairs={{0,2},{1,3},{2,0},{3,1},{4,6},{5,7},{6,4},{7,5},{8,10},{9,11},{10,... | collective-permute-start | bytes 884744 | tf_op jit(solution)/shard_map/ppermute | solution.py:39
  55.9 1.6 %collective-permute-start.16 = (bf16[144,512]{1,0:T(8,128)(2,1)S(1)}, bf16[144,512]{1,0:T(8,128)(2,1)S(1)}, u32[]{:S(2)}, u32[]{:S(2)}) collective-permute-start(bf16[144,512]{1,0:T(8,128)(2,1)S(1)} %get-tuple-element.74), channel_id=1, source_target_pairs={{0,1},{1,0},{2,3},{3,2},{4,5},{5,4},{6,7},{7,6},{8,9},{9,8},{10,11... | collective-permute-start | bytes 442376 | tf_op jit(solution)/shard_map/ppermute | solution.py:39
  56.0 1.5 %collective-permute-start.15 = (bf16[128,512]{1,0:T(8,128)(2,1)S(1)}, bf16[128,512]{1,0:T(8,128)(2,1)S(1)}, u32[]{:S(2)}, u32[]{:S(2)}) collective-permute-start(bf16[128,512]{1,0:T(8,128)(2,1)S(1)} %get-tuple-element.73), channel_id=1, source_target_pairs={{0,1},{1,0},{2,3},{3,2},{4,5},{5,4},{6,7},{7,6},{8,9},{9,8},{10,11... | collective-permute-start | bytes 393224 | tf_op jit(solution)/shard_map/ppermute | solution.py:39
  58.3 8.1 %collective-permute-start.17 = (bf16[256,256]{1,0:T(8,128)(2,1)S(1)}, bf16[256,256]{1,0:T(8,128)(2,1)S(1)}, u32[]{:S(2)}, u32[]{:S(2)}) collective-permute-start(bf16[256,256]{1,0:T(8,128)(2,1)S(1)} %get-tuple-element.77), channel_id=1, source_target_pairs={{0,2},{1,3},{2,0},{3,1},{4,6},{5,7},{6,4},{7,5},{8,10},{9,11},{10,... | collective-permute-start | bytes 393224 | tf_op jit(solution)/shard_map/ppermute | solution.py:39
  59.7 6.7 %collective-permute-start.18 = (bf16[208,256]{1,0:T(8,128)(2,1)S(1)}, bf16[208,256]{1,0:T(8,128)(2,1)S(1)}, u32[]{:S(2)}, u32[]{:S(2)}) collective-permute-start(bf16[208,256]{1,0:T(8,128)(2,1)S(1)} %get-tuple-element.78), channel_id=1, source_target_pairs={{0,2},{1,3},{2,0},{3,1},{4,6},{5,7},{6,4},{7,5},{8,10},{9,11},{10,... | collective-permute-start | bytes 319496 | tf_op jit(solution)/shard_map/ppermute | solution.py:39

commit v3 on v2

--- a/solution.py
+++ b/solution.py
@@ -48,7 +48,8 @@
 
 
 def gather(own, early, first_product):
-    pair = join(own, shift(own, (4, 0, 0)))
+    near = call(copy_kernel, [(own.shape, own.dtype)], [own])[0]
+    pair = join(near, shift(own, (4, 0, 0)))
     four = join(pair, shift(pair, (0, 0, 1)))
     first = [
         shift(four, (0, 1, 0), (1, 0, 0)),
@@ -76,6 +77,7 @@
 )
 ORDER = [block for stage in STAGES for piece in stage for block in piece]
 STAGE_ROWS = [sum(len(piece) for piece in stage) * BLOCK for stage in STAGES]
+SENDS = (1, 1, 2, 2)
 
 
 def wrap(step):
@@ -100,27 +102,26 @@
 
 
 def depth(core, block):
-    return jnp.where(core == 0, block[1], block[0])
-
-
-def first_row(place, block, part):
-    z, y, x, core = place[0], place[1], place[2], place[3] % 2
+    return block[1] if block[0] == block[1] else jnp.where(core == 0, block[1], block[0])
+
+
+def first_rows(place, block):
+    z, y, x, core = place[0], place[1], place[2], place[3] & 1
     dz = depth(core, block)
-    dy = jnp.where(core == 0, block[0], block[1])
-    zz = lax.rem(z + dz + (4 * (part % 2) + NZ), NZ)
-    yy = lax.rem(y + dy + NY, NY)
-    xx = lax.rem(x + part // 2, NX)
-    return pl.multiple_of((zz * (NY * NX) + yy * NX + xx) * SHARD, SHARD)
-
-
-def twin_row(place, block, part):
-    core = place[3] % 2
-    other = twin(block)
-    away = lax.rem(depth(core, block) - depth(1 - core, other) + 8, 8) // 4
-    start = slot(other)[1]
-    if slot(other)[0] == len(STAGES) - 1:
-        start = start % (STAGE_ROWS[-1] // 2)
-    return pl.multiple_of(start + (part // 2) * 2 * SHARD + ((part % 2) ^ away) * SHARD, SHARD)
+    dy = depth(1 - core, block)
+    row = ((z + dz) & (NZ - 1)) * (NY * NX) + ((y + dy) & (NY - 1)) * NX + x
+    return [pl.multiple_of((row ^ (NZ // 2 * NY * NX * (part % 2) + part // 2)) * SHARD, SHARD) for part in range(4)]
+
+
+def twin_rows(place, block):
+    core = place[3] & 1
+    stage, start = slot(twin(block))
+    each = STAGE_ROWS[stage] // SENDS[stage]
+    parts = [start % each + part * SHARD for part in range(4)]
+    if 2 in (block[1], twin(block)[1]):
+        away = (((depth(core, block) - depth(1 - core, twin(block))) >> 2) & 1) * SHARD
+        parts = [pl.multiple_of(row ^ away, SHARD) for row in parts]
+    return sum(SENDS[:stage]) + start // each, parts
 
 
 def split3(value):
@@ -129,6 +130,10 @@
     middle = rest.astype(jnp.bfloat16)
     low = (rest - middle.astype(jnp.float32)).astype(jnp.bfloat16)
     return [high, middle, low]
+
+
+def copy_kernel(from_ref, to_ref):
+    to_ref[...] = from_ref[...]
 
 
 def prepare_kernel(place, train_ref, turned_ref, sums_ref):
@@ -146,7 +151,7 @@
                 sums_ref[k : k + 1, :] += part
 
 
-def products(pieces, turned_ref, precond_ref, keep_ref, send_refs, sums_ref, rounded_ref):
+def condition(pieces, precond_ref, sums_ref, rounded_ref):
     base = 0
     for piece in pieces:
         rows = piece.shape[0]
@@ -160,35 +165,38 @@
             squares += value[:, :128] + value[:, 128:]
         sums_ref[here, :] = squares
         base += rows
-    for base in range(0, base, 256):
-        here = slice(base, base + 256)
-        for k in (2, 3, 0, 1):
-            value = jnp.dot(rounded_ref[here, :], turned_ref[k], preferred_element_type=jnp.float32)
-            columns = slice((k % 2) * 256, (k % 2 + 1) * 256)
-            if k < 2:
-                keep_ref[here, columns] = value
-            else:
-                value = value.astype(jnp.bfloat16)
-                rows = 256 // len(send_refs)
-                for n, send_ref in enumerate(send_refs):
-                    send_ref[slice(base, base + rows), columns] = value[n * rows : (n + 1) * rows]
-
-
-def products_kernel(turned_ref, precond_ref, *refs):
-    keep_ref, send_ref, sums_ref, rounded_ref = refs[-4:]
-    products(refs[:-4], turned_ref, precond_ref, keep_ref, [send_ref], sums_ref, rounded_ref)
-
-
-def last_products_kernel(
-    place, turned_ref, precond_ref, low, high, sums0, sums1, sums2, train_ref, keep_ref, send_low, send_high, lanes_ref, rounded_ref, sums3, all_sums
+
+
+def multiply(rounded_ref, turned_ref, refs, first):
+    each = rounded_ref.shape[0] // len(refs)
+    for k in range(2):
+        value = jnp.dot(rounded_ref[...], turned_ref[first + k], preferred_element_type=jnp.float32)
+        for n, ref in enumerate(refs):
+            ref[:each, k * 256 : (k + 1) * 256] = value[n * each : (n + 1) * each].astype(ref.dtype)
+
+
+def products_kernel(turned_ref, precond_ref, low, high, keep_ref, *refs):
+    *send_refs, sums_ref, rounded_ref = refs
+    condition((low, high), precond_ref, sums_ref, rounded_ref)
+    multiply(rounded_ref, turned_ref, send_refs, 2)
+    multiply(rounded_ref, turned_ref, [keep_ref], 0)
+
+
+def last_kept_kernel(turned_ref, rounded_ref, keep_ref):
+    multiply(rounded_ref, turned_ref, [keep_ref], 0)
+
+
+def last_sent_kernel(
+    place, turned_ref, precond_ref, low, high, sums0, sums1, sums2, train_ref, rounded_ref, send_low, send_high, lanes_ref, sums3, all_sums
 ):
-    products((low, high), turned_ref, precond_ref, keep_ref, [send_low, send_high], sums3, rounded_ref)
+    condition((low, high), precond_ref, sums3, rounded_ref)
+    multiply(rounded_ref, turned_ref, [send_low, send_high], 2)
     sums = (sums0, sums1, sums2, sums3)
     for block in ORDER:
         stage, at = slot(block)
-        for part in range(4):
+        for part, row in enumerate(first_rows(place, block)):
             here = slice(at + part * SHARD, at + (part + 1) * SHARD)
-            all_sums[pl.ds(first_row(place, block, part), SHARD), :] = sums[stage][here, :]
+            all_sums[pl.ds(row, SHARD), :] = sums[stage][here, :]
     lanes = jnp.sum(all_sums[...].T, axis=0, keepdims=True)
     lanes_ref[...] = lanes
     extra = split3(lanes[:, :512]) + split3(lanes[:, 512:])
@@ -201,23 +209,23 @@
     first = at
     for block in blocks:
         stage, base = slot(block)
-        there, start = slot(twin(block))
-        if there == len(STAGES) - 1 and start >= STAGE_ROWS[-1] // 2:
-            there += 1
-        for part in range(4):
+        there, rows = twin_rows(place, block)
+        for part, row in enumerate(rows):
             own = keeps[stage][base + part * SHARD : base + (part + 1) * SHARD, :]
-            total = own + gots[there][pl.ds(twin_row(place, block, part), SHARD), :].astype(jnp.float32)
+            total = own + gots[there][pl.ds(row, SHARD), :].astype(jnp.float32)
             mine_ref[at : at + SHARD, :] = total[:, :256]
             send_ref[at - first : at - first + SHARD, :] = total[:, 256:].astype(jnp.bfloat16)
             at += SHARD
 
 
-def early_kernel(place, keep0, keep1, keep2, got0, got1, got2, mine_ref, send_ref):
-    add_blocks(place, EARLY, (keep0, keep1, keep2), (got0, got1, got2), mine_ref, send_ref)
+def early_kernel(place, *refs):
+    keeps, gots = refs[: len(STAGES) - 1], refs[len(STAGES) - 1 : -2]
+    add_blocks(place, EARLY, keeps, gots, *refs[-2:])
 
 
 def late_kernel(place, *refs):
-    keeps, gots, rest = refs[: len(STAGES)], refs[len(STAGES) : 2 * len(STAGES) + 1], refs[2 * len(STAGES) + 1 :]
+    first, last = len(STAGES), len(STAGES) + sum(SENDS)
+    keeps, gots, rest = refs[:first], refs[first:last], refs[last:]
     lanes_ref, train_ref, mine_ref, send_low, send_high, lanes2_ref, train2_ref = rest
     add_blocks(place, LATE[:4], keeps, gots, mine_ref, send_low)
     add_blocks(place, LATE[4:], keeps, gots, mine_ref, send_high, 4 * BLOCK)
@@ -239,48 +247,46 @@
     return rows[at : at + 1] + (rows[at + 1 : at + 2] + rows[at + 2 : at + 3])
 
 
-def merge_kernel(place, mine0, got0, mine1, all_ref):
-    for blocks, mine, other in ((EARLY, mine0, got0), (LATE, mine1, None)):
-        at = 0
-        for block in blocks:
-            for part in range(4):
-                total = mine[at : at + SHARD, :]
-                if other is not None:
-                    total = total + other[at : at + SHARD, :].astype(jnp.float32)
-                all_ref[pl.ds(first_row(place, block, part), SHARD), :] = total
-                at += SHARD
-
-
-def finish_kernel(place, all_ref, got1, got2, lanes_ref, train_ref, out_ref, sums_ref):
-    sums_ref[...] = all_ref[...]
-    for blocks, got in ((LATE[:4], got1), (LATE[4:], got2)):
-        at = 0
-        for block in blocks:
-            for part in range(4):
-                rows = pl.ds(first_row(place, block, part), SHARD)
-                sums_ref[rows, :] += got[at : at + SHARD, :].astype(jnp.float32)
-                at += SHARD
-    got = got2[at:, :].astype(jnp.float32)
+def merge_kernel(mine0, got0, all_ref):
+    all_ref[...] = mine0[...] + got0[...].astype(jnp.float32)
+
+
+def finish_kernel(place, early_ref, mine1, got1, got2, lanes_ref, train_ref, out_ref, scale_ref, sums_ref, sem):
+    split = got1.shape[0]
+    late = mine1.shape[0]
+    got = got2[late - split :, :].astype(jnp.float32)
     query = lanes_ref[...] + jnp.concatenate([sum3(got, 3 * j) for j in range(4)], axis=1)
     query = 1.0 / jnp.sqrt(query + EPS)
+    for i in range(0, 1024, 128):
+        scale_ref[i : i + 128, :] = jnp.broadcast_to(query[:, i : i + 128], (128, 128)).T
     train = (1.0 / jnp.sqrt(train_ref[...] + sum3(got, 12) + EPS)) * math.sqrt(F)
-    for i in range(0, 1024, 128):
-        rows = slice(i, i + 128)
-        scale = jnp.broadcast_to(query[:, rows], (128, 128)).T
-        for j in range(0, 256, 128):
-            columns = slice(j, j + 128)
-            out_ref[rows, columns] = sums_ref[rows, columns] * scale * train[:, columns]
-
-
-def call(kernel, outs, inputs, scratch=(), smem=0, moved=1):
+    at = 0
+    for block in EARLY + LATE:
+        for row in first_rows(place, block):
+            base = at - len(EARLY) * BLOCK
+            if base < 0:
+                total = early_ref[at : at + SHARD, :]
+            else:
+                other = got1[base : base + SHARD, :] if base < split else got2[base - split : base - split + SHARD, :]
+                total = mine1[base : base + SHARD, :] + other.astype(jnp.float32)
+            rows = pl.ds(row, SHARD)
+            scale = scale_ref[rows, :]
+            for j in range(0, 256, 128):
+                sums_ref[at : at + SHARD, j : j + 128] = total[:, j : j + 128] * scale * train[:, j : j + 128]
+            pltpu.make_async_copy(sums_ref.at[at : at + SHARD, :], out_ref.at[rows, :], sem).start()
+            at += SHARD
+    pltpu.make_async_copy(sums_ref, out_ref, sem).wait()
+
+
+def call(kernel, outs, inputs, scratch=(), smem=0, out_spec=VMEM):
     return pl.pallas_call(
         kernel,
         out_shape=[jax.ShapeDtypeStruct(s, d) for s, d in outs],
         in_specs=[SMEM] * smem + [VMEM] * (len(inputs) - smem),
-        out_specs=[VMEM] * len(outs),
+        out_specs=[out_spec] * len(outs),
         scratch_shapes=list(scratch),
         compiler_params=pltpu.CompilerParams(vmem_limit_bytes=24 * MIB),
-        cost_estimate=pl.CostEstimate(flops=1, bytes_accessed=moved, transcendentals=0),
+        cost_estimate=pl.CostEstimate(flops=1, bytes_accessed=1, transcendentals=0),
     )(*inputs)
 
 
@@ -298,11 +304,11 @@
             smem=1,
         )
 
-    def product(pieces, prepared):
+    def product(pieces, prepared, sends=1):
         rows = sum(piece.shape[0] for piece in pieces)
         return call(
             products_kernel,
-            [((rows, 512), f32), ((rows, 512), bf16), ((rows, 128), f32)],
+            [((rows, 512), f32), *[((rows // sends, 512), bf16)] * sends, ((rows, 128), f32)],
             [prepared[0], precond, *pieces],
             scratch=[pltpu.VMEM((rows, 2048), bf16)],
         )
@@ -311,11 +317,11 @@
     turned, train_sums = prepared
     keep, send, squares = done
     keeps, gots, sums = [keep], [across(send, 1)], [squares]
-    for pieces in stages:
-        *pieces, _ = together(*pieces, send)
-        keep, send, squares = product(pieces, prepared)
+    for n, pieces in enumerate(stages):
+        *pieces, _ = together(*pieces, gots[-1] if n else send)
+        keep, *sends, squares = product(pieces, prepared, SENDS[n + 1])
         keeps.append(keep)
-        gots.append(across(send, 1))
+        gots += [across(send, 1) for send in sends]
         sums.append(squares)
     early = len(EARLY) * BLOCK
     late = len(LATE) * BLOCK
@@ -325,13 +331,14 @@
     got0 = across(send, 2)
     low, high, _ = together(*last, send)
     rows = STAGE_ROWS[-1]
-    keep, send_low, send_high, lanes = call(
-        last_products_kernel,
-        [((rows, 512), f32), ((rows // 2, 512), bf16), ((rows // 2 + SHARD, 512), bf16), ((1, 1024), f32)],
+    rounded, send_low, send_high, lanes = call(
+        last_sent_kernel,
+        [((rows, 2048), bf16), ((rows // 2, 512), bf16), ((rows // 2 + SHARD, 512), bf16), ((1, 1024), f32)],
         [place, turned, precond, low, high, *sums, train_sums],
-        scratch=[pltpu.VMEM((rows, 2048), bf16), pltpu.VMEM((rows, 128), f32), pltpu.VMEM((1024, 128), f32)],
+        scratch=[pltpu.VMEM((rows, 128), f32), pltpu.VMEM((1024, 128), f32)],
         smem=1,
     )
+    keep = call(last_kept_kernel, [((rows, 512), f32)], [turned, rounded])[0]
     mine1, send_low, send_high, lanes, train = call(
         late_kernel,
         [
@@ -345,13 +352,14 @@
         smem=1,
     )
     got1, got2 = across(send_low, 2), across(send_high, 2)
-    merged = call(merge_kernel, [((1024, 256), f32)], [place, mine0, got0, mine1], smem=1)[0]
+    merged = call(merge_kernel, [((early, 256), f32)], [mine0, got0])[0]
     return call(
         finish_kernel,
         [((1024, 256), f32)],
-        [place, merged, got1, got2, lanes, train],
-        scratch=[pltpu.VMEM((1024, 256), f32)],
+        [place, merged, mine1, got1, got2, lanes, train],
+        scratch=[pltpu.VMEM((1024, 128), f32), pltpu.VMEM((1024, 256), f32), pltpu.SemaphoreType.DMA],
         smem=1,
+        out_spec=pl.BlockSpec(memory_space=pl.ANY),
     )[0]
 
 

time: 68.4 us -> 67.2 us (0.982)
  Pallas kernels: 12.8 us -> 11.9 us
  other arithmetic: 1 us -> 0.18 us
    ppermute x8 -> x9, waiting for transfers between devices: 7.53 us -> 8.95 us  [across(): return lax.ppermute(value, 'feat', [(f, f ^ mask) for f in range(4)])]
    ppermute x11, waiting for transfers between devices: 11.9 us -> 10.6 us  [shift(): return lax.ppermute(value, ('rows', 'feat'), pairs)]
    pallas_call x9 -> x11, Pallas kernels: 12.8 us -> 11.9 us  [call(): pl.pallas_call(kernel, out_shape=[jax.ShapeDtypeStruct(s, d) for s, d in...]
    concatenate x3 -> x4, other arithmetic: 0.92 us -> 0.1 us  [join(): return jnp.concatenate(parts, axis=0)]
    ppermute x8 -> x9, starting transfers between devices: 5.06 us -> 5.3 us  [across(): return lax.ppermute(value, 'feat', [(f, f ^ mask) for f in range(4)])]
    unnamed x8 -> x6, local copies, waits for them, and re-layouts: 3.08 us -> 3.07 us
  transfers between devices with their start and end apart: 19 -> 20, of which waited for: 12 -> 12; matrix products, arithmetic and copies ran while one was open for 1% -> 0% of each run, Pallas kernels for 16% -> 15%
where the time goes in v3:
time: 67.2 us; the launch traced here: 66.9 us
  starting transfers between devices  32 us (48%)
  waiting for transfers between devices  19.5 us (29%)
  Pallas kernels  11.9 us (18%)
  local copies, waits for them, and re-layouts  3.07 us (5%)
    ppermute x11, starting transfers between devices, shift(): return lax.ppermute(value, ('rows', 'feat'), pairs)  26.7 us
    pallas_call x11, Pallas kernels, call(): pl.pallas_call(kernel, out_shape=[jax.ShapeDtypeStruct(s, d) for s, d in...  11.9 us
    ppermute x11, waiting for transfers between devices, shift(): return lax.ppermute(value, ('rows', 'feat'), pairs)  10.6 us
    ppermute x9, waiting for transfers between devices, across(): return lax.ppermute(value, 'feat', [(f, f ^ mask) for f in range(4)])  8.95 us
    ppermute x9, starting transfers between devices, across(): return lax.ppermute(value, 'feat', [(f, f ^ mask) for f in range(4)])  5.3 us
    unnamed x6, local copies, waits for them, and re-layouts  3.07 us
  transfers between devices with their start and end apart: 20, of which 12 were waited for; matrix products, arithmetic and copies ran while one was open for 0% of the time, Pallas kernels for 15%

profile of v3, /device:TPU:8, one launch (start us, length us, event | category | flops | bytes accessed | tf_op | source)
XLA Modules:
  0.0 66.9 jit_solution(14204567068165222488)
XLA Ops:
  0.0 7.2 %collective-permute-start = (bf16[16,2048]{1,0:T(8,128)(2,1)}, bf16[16,2048]{1,0:T(8,128)(2,1)S(1)}, u32[]{:S(2)}, u32[]{:S(2)}) collective-permute-start(bf16[16,2048]{1,0:T(8,128)(2,1)} %from_ref.1), channel_id=1, source_target_pairs={{0,128},{1,129},{2,130},{3,131},{4,132},{5,133},{6,134},{7,135},{8... | collective-permute-start | bytes 196616 | tf_op jit(solution)/shard_map/ppermute | solution.py:35
  7.2 0.9 %copy-done.2 = bf16[16,2048]{1,0:T(8,128)(2,1)S(1)} copy-done((bf16[16,2048]{1,0:T(8,128)(2,1)S(1)}, bf16[16,2048]{1,0:T(8,128)(2,1)}, u32[]{:S(2)}) %copy-start.2) | copy-done | bytes 65560
  8.1 1.9 %collective-permute-done = bf16[16,2048]{1,0:T(8,128)(2,1)S(1)} collective-permute-done((bf16[16,2048]{1,0:T(8,128)(2,1)}, bf16[16,2048]{1,0:T(8,128)(2,1)S(1)}, u32[]{:S(2)}, u32[]{:S(2)}) %collective-permute-start) | collective-permute-done | bytes 65568 | tf_op jit(solution)/shard_map/ppermute | solution.py:35
  10.0 3.1 %collective-permute-start.1 = (bf16[32,2048]{1,0:T(8,128)(2,1)S(1)}, bf16[32,2048]{1,0:T(8,128)(2,1)S(1)}, u32[]{:S(2)}, u32[]{:S(2)}) collective-permute-start(bf16[32,2048]{1,0:T(8,128)(2,1)S(1)} %pad_maximum_fusion.3), channel_id=1, source_target_pairs={{0,4},{1,5},{2,6},{3,7},{4,0},{5,1},{6,2},{7,3},{8,12},{9,13},{10,... | collective-permute-start | bytes 393224 | tf_op jit(solution)/shard_map/ppermute | solution.py:35
  13.1 3.4 %collective-permute-done.1 = bf16[32,2048]{1,0:T(8,128)(2,1)S(1)} collective-permute-done((bf16[32,2048]{1,0:T(8,128)(2,1)S(1)}, bf16[32,2048]{1,0:T(8,128)(2,1)S(1)}, u32[]{:S(2)}, u32[]{:S(2)}) %collective-permute-start.1) | collective-permute-done | bytes 131104 | tf_op jit(solution)/shard_map/ppermute | solution.py:35
  16.5 1.7 %collective-permute-start.2 = (bf16[64,2048]{1,0:T(8,128)(2,1)S(1)}, bf16[64,2048]{1,0:T(8,128)(2,1)S(1)}, u32[]{:S(2)}, u32[]{:S(2)}) collective-permute-start(bf16[64,2048]{1,0:T(8,128)(2,1)S(1)} %pad_maximum_fusion.2), channel_id=1, source_target_pairs={{0,8},{1,33},{2,10},{3,35},{4,12},{5,37},{6,14},{7,39},{8,16},{9,4... | collective-permute-start | bytes 786440 | tf_op jit(solution)/shard_map/ppermute | solution.py:35
  18.2 1.2 %collective-permute-start.4 = (bf16[64,2048]{1,0:T(8,128)(2,1)S(1)}, bf16[64,2048]{1,0:T(8,128)(2,1)S(1)}, u32[]{:S(2)}, u32[]{:S(2)}) collective-permute-start(bf16[64,2048]{1,0:T(8,128)(2,1)S(1)} %pad_maximum_fusion.2), channel_id=1, source_target_pairs={{0,16},{1,65},{2,18},{3,67},{4,20},{5,69},{6,22},{7,71},{8,24},{9,... | collective-permute-start | bytes 786440 | tf_op jit(solution)/shard_map/ppermute | solution.py:35
  19.4 2.1 %collective-permute-start.3 = (bf16[64,2048]{1,0:T(8,128)(2,1)S(1)}, bf16[64,2048]{1,0:T(8,128)(2,1)S(1)}, u32[]{:S(2)}, u32[]{:S(2)}) collective-permute-start(bf16[64,2048]{1,0:T(8,128)(2,1)S(1)} %pad_maximum_fusion.2), channel_id=1, source_target_pairs={{0,24},{1,225},{2,26},{3,227},{4,28},{5,229},{6,30},{7,231},{8,0},... | collective-permute-start | bytes 786440 | tf_op jit(solution)/shard_map/ppermute | solution.py:35
  21.5 0.1 pad_add_fusion.place
  21.6 2.2 %copy-done.1 = bf16[1024,2048]{1,0:T(8,128)(2,1)S(1)} copy-done((bf16[1024,2048]{1,0:T(8,128)(2,1)S(1)}, bf16[1024,2048]{1,0:T(8,128)(2,1)}, u32[]{:S(2)}) %copy-start.1) | copy-done | bytes 4194328
  23.8 1.8 %shard_map.38 = (bf16[4,2048,256]{2,1,0:T(8,128)(2,1)S(1)}, f32[4,256]{1,0:T(4,128)S(1)}) custom-call(s32[4]{0:T(128)S(1)} %pad_add_fusion.place, bf16[1024,2048]{1,0:T(8,128)(2,1)S(1)} %copy-done.1), custom_call_target="tpu_custom_call" | custom-call | flops 1 | bytes 1 | tf_op jit(solution)/shard_map/pallas_call | solution.py:282
  25.7 0.5 collective-permute-done.4
  26.2 2.4 %collective-permute-done.3 = bf16[64,2048]{1,0:T(8,128)(2,1)S(1)} collective-permute-done((bf16[64,2048]{1,0:T(8,128)(2,1)S(1)}, bf16[64,2048]{1,0:T(8,128)(2,1)S(1)}, u32[]{:S(2)}, u32[]{:S(2)}) %collective-permute-start.3) | collective-permute-done | bytes 262176 | tf_op jit(solution)/shard_map/ppermute | solution.py:35
  28.6 1.6 %collective-permute-start.5 = (bf16[128,2048]{1,0:T(8,128)(2,1)S(1)}, bf16[128,2048]{1,0:T(8,128)(2,1)S(1)}, u32[]{:S(2)}, u32[]{:S(2)}) collective-permute-start(bf16[128,2048]{1,0:T(8,128)(2,1)S(1)} %pad_maximum_fusion.low), channel_id=1, source_target_pairs={{0,32},{1,9},{2,34},{3,11},{4,36},{5,13},{6,38},{7,15},{8,40},{9,1... | collective-permute-start | bytes 1572872 | tf_op jit(solution)/shard_map/ppermute | solution.py:35
  30.2 2.6 %collective-permute-start.6 = (bf16[128,2048]{1,0:T(8,128)(2,1)S(1)}, bf16[128,2048]{1,0:T(8,128)(2,1)S(1)}, u32[]{:S(2)}, u32[]{:S(2)}) collective-permute-start(bf16[128,2048]{1,0:T(8,128)(2,1)S(1)} %pad_maximum_fusion.1.high), channel_id=1, source_target_pairs={{0,224},{1,25},{2,226},{3,27},{4,228},{5,29},{6,230},{7,31},{8,232... | collective-permute-start | bytes 1572872 | tf_op jit(solution)/shard_map/ppermute | solution.py:35
  32.9 0.0 collective-permute-start.7
  32.9 3.6 %collective-permute-start.8 = (bf16[128,2048]{1,0:T(8,128)(2,1)S(1)}, bf16[128,2048]{1,0:T(8,128)(2,1)S(1)}, u32[]{:S(2)}, u32[]{:S(2)}) collective-permute-start(bf16[128,2048]{1,0:T(8,128)(2,1)S(1)} %pad_maximum_fusion.low), channel_id=1, source_target_pairs={{0,224},{1,25},{2,226},{3,27},{4,228},{5,29},{6,230},{7,31},{8,232... | collective-permute-start | bytes 1572872 | tf_op jit(solution)/shard_map/ppermute | solution.py:35
  36.4 1.6 %shard_map.39 = (f32[256,512]{1,0:T(8,128)S(1)}, bf16[256,512]{1,0:T(8,128)(2,1)S(1)}, f32[256,128]{1,0:T(8,128)S(1)}) custom-call(bf16[4,2048,256]{2,1,0:T(8,128)(2,1)S(1)} %get-tuple-element.49.turned_ref, bf16[8,256,256]{2,1,0:T(8,128)(2,1)S(1)} %copy-done, bf16[128,2048]{1,0:T(8,128)(2,1)S(1)} %pad_maximum_fusion.low, ...), custom_call_target="tpu_custom_call" | custom-call | flops 1 | bytes 1 | tf_op jit(solution)/shard_map/pallas_call | solution.py:282
  38.0 1.9 %collective-permute-done.5.low = bf16[128,2048]{1,0:T(8,128)(2,1)S(1)} collective-permute-done((bf16[128,2048]{1,0:T(8,128)(2,1)S(1)}, bf16[128,2048]{1,0:T(8,128)(2,1)S(1)}, u32[]{:S(2)}, u32[]{:S(2)}) %collective-permute-start.5) | collective-permute-done | bytes 524320 | tf_op jit(solution)/shard_map/ppermute | solution.py:35
  39.9 0.0 collective-permute-done.6.high
  39.9 1.1 %collective-permute-start.14 = (bf16[128,2048]{1,0:T(8,128)(2,1)S(1)}, bf16[128,2048]{1,0:T(8,128)(2,1)S(1)}, u32[]{:S(2)}, u32[]{:S(2)}) collective-permute-start(bf16[128,2048]{1,0:T(8,128)(2,1)S(1)} %collective-permute-done.5.low), channel_id=1, source_target_pairs={{0,32},{1,9},{2,34},{3,11},{4,36},{5,13},{6,38},{7,15},{8,40},{9,1... | collective-permute-start | bytes 1572872 | tf_op jit(solution)/shard_map/ppermute | solution.py:35
  41.1 2.4 %collective-permute-start.15 = (bf16[128,2048]{1,0:T(8,128)(2,1)S(1)}, bf16[128,2048]{1,0:T(8,128)(2,1)S(1)}, u32[]{:S(2)}, u32[]{:S(2)}) collective-permute-start(bf16[128,2048]{1,0:T(8,128)(2,1)S(1)} %collective-permute-done.6.high), channel_id=1, source_target_pairs={{0,224},{1,25},{2,226},{3,27},{4,228},{5,29},{6,230},{7,31},{8,232... | collective-permute-start | bytes 1572872 | tf_op jit(solution)/shard_map/ppermute | solution.py:35
  43.5 1.6 %shard_map.40 = (f32[256,512]{1,0:T(8,128)S(1)}, bf16[256,512]{1,0:T(8,128)(2,1)S(1)}, f32[256,128]{1,0:T(8,128)S(1)}) custom-call(bf16[4,2048,256]{2,1,0:T(8,128)(2,1)S(1)} %get-tuple-element.49.turned_ref, bf16[8,256,256]{2,1,0:T(8,128)(2,1)S(1)} %copy-done, bf16[128,2048]{1,0:T(8,128)(2,1)S(1)} %collective-permute-done.5.low, ...), custom_call_target="tpu_custom_call" | custom-call | flops 1 | bytes 1 | tf_op jit(solution)/shard_map/pallas_call | solution.py:282
  45.1 0.1 collective-permute-start.9
  45.2 0.4 collective-permute-done.7.low
  45.5 0.1 collective-permute-start.10
  45.7 0.0 collective-permute-done.8.high
  45.7 1.0 %collective-permute-done.9.refs_4_.refs_5_ = bf16[256,512]{1,0:T(8,128)(2,1)S(1)} collective-permute-done((bf16[256,512]{1,0:T(8,128)(2,1)S(1)}, bf16[256,512]{1,0:T(8,128)(2,1)S(1)}, u32[]{:S(2)}, u32[]{:S(2)}) %collective-permute-start.9) | collective-permute-done | bytes 262176 | tf_op jit(solution)/shard_map/ppermute | solution.py:39
  46.7 1.6 %shard_map.41 = (f32[256,512]{1,0:T(8,128)S(1)}, bf16[128,512]{1,0:T(8,128)(2,1)S(1)}, bf16[128,512]{1,0:T(8,128)(2,1)S(1)}, f32[256,128]{1,0:T(8,128)S(1)}) custom-call(bf16[4,2048,256]{2,1,0:T(8,128)(2,1)S(1)} %get-tuple-element.49.turned_ref, bf16[8,256,256]{2,1,0:T(8,128)(2,1)S(1)} %copy-done, bf16[128,2048]{1,0:T(8,128)(2,1)S(1)} %collective-permute-done.7.low, ...), custom_call_target="tpu_custom_call" | custom-call | flops 1 | bytes 1 | tf_op jit(solution)/shard_map/pallas_call | solution.py:282
  48.3 0.2 collective-permute-start.11
  48.5 0.4 collective-permute-start.12
  48.9 0.8 %collective-permute-done.11.refs_5_.refs_6_ = bf16[128,512]{1,0:T(8,128)(2,1)S(1)} collective-permute-done((bf16[128,512]{1,0:T(8,128)(2,1)S(1)}, bf16[128,512]{1,0:T(8,128)(2,1)S(1)}, u32[]{:S(2)}, u32[]{:S(2)}) %collective-permute-start.11) | collective-permute-done | bytes 131104 | tf_op jit(solution)/shard_map/ppermute | solution.py:39
  49.7 0.2 collective-permute-done.12.refs_6_.refs_7_
  49.9 0.6 shard_map.42
  50.6 1.8 %collective-permute-start.13 = (bf16[576,256]{1,0:T(8,128)(2,1)S(1)}, bf16[576,256]{1,0:T(8,128)(2,1)S(1)}, u32[]{:S(2)}, u32[]{:S(2)}) collective-permute-start(bf16[576,256]{1,0:T(8,128)(2,1)S(1)} %get-tuple-element.67), channel_id=1, source_target_pairs={{0,2},{1,3},{2,0},{3,1},{4,6},{5,7},{6,4},{7,5},{8,10},{9,11},{10,... | collective-permute-start | bytes 884744 | tf_op jit(solution)/shard_map/ppermute | solution.py:39
  52.3 0.0 collective-permute-done.14.low
  52.3 1.6 %shard_map.44 = (bf16[256,2048]{1,0:T(8,128)(2,1)S(1)}, bf16[128,512]{1,0:T(8,128)(2,1)S(1)}, bf16[144,512]{1,0:T(8,128)(2,1)S(1)}, f32[1,1024]{1,0:T(1,128)S(1)}) custom-call(s32[4]{0:T(128)S(1)} %pad_add_fusion.place, bf16[4,2048,256]{2,1,0:T(8,128)(2,1)S(1)} %get-tuple-element.49.turned_ref, bf16[8,256,256]{2,1,0:T(8,128)(2,1)S(1)} %copy-done, ...), custom_call_target="tpu_custom_call" | custom-call | flops 1 | bytes 1 | tf_op jit(solution)/shard_map/pallas_call | solution.py:282
  53.9 0.1 collective-permute-start.17
  54.0 0.5 collective-permute-start.16
  54.5 0.7 %shard_map.45.refs_3_ = f32[256,512]{1,0:T(8,128)S(1)} custom-call(bf16[4,2048,256]{2,1,0:T(8,128)(2,1)S(1)} %get-tuple-element.49.turned_ref, bf16[256,2048]{1,0:T(8,128)(2,1)S(1)} %get-tuple-element.74.rounded_ref), custom_call_target="tpu_custom_call" | custom-call | flops 1 | bytes 1 | tf_op jit(solution)/shard_map/pallas_call | solution.py:282
  55.2 0.3 collective-permute-done.16.refs_8_
  55.6 0.7 shard_map.46
  56.2 0.4 collective-permute-start.18
  56.7 1.7 %collective-permute-start.19 = (bf16[208,256]{1,0:T(8,128)(2,1)S(1)}, bf16[208,256]{1,0:T(8,128)(2,1)S(1)}, u32[]{:S(2)}, u32[]{:S(2)}) collective-permute-start(bf16[208,256]{1,0:T(8,128)(2,1)S(1)} %get-tuple-element.80), channel_id=1, source_target_pairs={{0,2},{1,3},{2,0},{3,1},{4,6},{5,7},{6,4},{7,5},{8,10},{9,11},{10,... | collective-permute-start | bytes 319496 | tf_op jit(solution)/shard_map/ppermute | solution.py:39
  58.3 2.1 %collective-permute-done.13.got0 = bf16[576,256]{1,0:T(8,128)(2,1)S(1)} collective-permute-done((bf16[576,256]{1,0:T(8,128)(2,1)S(1)}, bf16[576,256]{1,0:T(8,128)(2,1)S(1)}, u32[]{:S(2)}, u32[]{:S(2)}) %collective-permute-start.13) | collective-permute-done | bytes 294944 | tf_op jit(solution)/shard_map/ppermute | solution.py:39
  60.5 0.1 shard_map.43.early_ref
  60.5 4.4 %collective-permute-done.19.got2 = bf16[208,256]{1,0:T(8,128)(2,1)S(1)} collective-permute-done((bf16[208,256]{1,0:T(8,128)(2,1)S(1)}, bf16[208,256]{1,0:T(8,128)(2,1)S(1)}, u32[]{:S(2)}, u32[]{:S(2)}) %collective-permute-start.19) | collective-permute-done | bytes 106528 | tf_op jit(solution)/shard_map/ppermute | solution.py:39
  65.0 1.7 %shard_map.47 = f32[1024,256]{1,0:T(8,128)} custom-call(s32[4]{0:T(128)S(1)} %pad_add_fusion.place, f32[576,256]{1,0:T(8,128)S(1)} %shard_map.43.early_ref, f32[448,256]{1,0:T(8,128)S(1)} %get-tuple-element.78.mine1, bf16[256,256]{1,0:T(8,128)(2,1)S(1)} %collective-permute-done.18.got1, bf16[208,256]{1,0:T(8,128)(2,1)S(1)} %collective-permute-done.19.got2, ...), custom_call_target="tpu_custom_call" | custom-call | flops 1 | bytes 1 | tf_op jit(solution)/shard_map/pallas_call | solution.py:282
  (14 shorter events, 0.1 us)
Async XLA Ops:
  0.0 36.4 %copy-start = (bf16[8,256,256]{2,1,0:T(8,128)(2,1)S(1)}, bf16[8,256,256]{2,1,0:T(8,128)(2,1)}, u32[]{:S(2)}) copy-start(bf16[8,256,256]{2,1,0:T(8,128)(2,1)} %precond_ref.7) | copy-start | bytes 3145732
  0.0 9.9 %collective-permute-start = (bf16[16,2048]{1,0:T(8,128)(2,1)}, bf16[16,2048]{1,0:T(8,128)(2,1)S(1)}, u32[]{:S(2)}, u32[]{:S(2)}) collective-permute-start(bf16[16,2048]{1,0:T(8,128)(2,1)} %from_ref.1), channel_id=1, source_target_pairs={{0,128},{1,129},{2,130},{3,131},{4,132},{5,133},{6,134},{7,135},{8... | collective-permute-start | bytes 196616 | tf_op jit(solution)/shard_map/ppermute | solution.py:35
  7.2 0.9 %copy-start.2 = (bf16[16,2048]{1,0:T(8,128)(2,1)S(1)}, bf16[16,2048]{1,0:T(8,128)(2,1)}, u32[]{:S(2)}) copy-start(bf16[16,2048]{1,0:T(8,128)(2,1)} %from_ref.1) | copy-start | bytes 196612
  10.0 6.6 %collective-permute-start.1 = (bf16[32,2048]{1,0:T(8,128)(2,1)S(1)}, bf16[32,2048]{1,0:T(8,128)(2,1)S(1)}, u32[]{:S(2)}, u32[]{:S(2)}) collective-permute-start(bf16[32,2048]{1,0:T(8,128)(2,1)S(1)} %pad_maximum_fusion.3), channel_id=1, source_target_pairs={{0,4},{1,5},{2,6},{3,7},{4,0},{5,1},{6,2},{7,3},{8,12},{9,13},{10,... | collective-permute-start | bytes 393224 | tf_op jit(solution)/shard_map/ppermute | solution.py:35
  16.5 9.1 %collective-permute-start.2 = (bf16[64,2048]{1,0:T(8,128)(2,1)S(1)}, bf16[64,2048]{1,0:T(8,128)(2,1)S(1)}, u32[]{:S(2)}, u32[]{:S(2)}) collective-permute-start(bf16[64,2048]{1,0:T(8,128)(2,1)S(1)} %pad_maximum_fusion.2), channel_id=1, source_target_pairs={{0,8},{1,33},{2,10},{3,35},{4,12},{5,37},{6,14},{7,39},{8,16},{9,4... | collective-permute-start | bytes 786440 | tf_op jit(solution)/shard_map/ppermute | solution.py:35
  18.2 8.0 %collective-permute-start.4 = (bf16[64,2048]{1,0:T(8,128)(2,1)S(1)}, bf16[64,2048]{1,0:T(8,128)(2,1)S(1)}, u32[]{:S(2)}, u32[]{:S(2)}) collective-permute-start(bf16[64,2048]{1,0:T(8,128)(2,1)S(1)} %pad_maximum_fusion.2), channel_id=1, source_target_pairs={{0,16},{1,65},{2,18},{3,67},{4,20},{5,69},{6,22},{7,71},{8,24},{9,... | collective-permute-start | bytes 786440 | tf_op jit(solution)/shard_map/ppermute | solution.py:35
  19.4 9.2 %collective-permute-start.3 = (bf16[64,2048]{1,0:T(8,128)(2,1)S(1)}, bf16[64,2048]{1,0:T(8,128)(2,1)S(1)}, u32[]{:S(2)}, u32[]{:S(2)}) collective-permute-start(bf16[64,2048]{1,0:T(8,128)(2,1)S(1)} %pad_maximum_fusion.2), channel_id=1, source_target_pairs={{0,24},{1,225},{2,26},{3,227},{4,28},{5,229},{6,30},{7,231},{8,0},... | collective-permute-start | bytes 786440 | tf_op jit(solution)/shard_map/ppermute | solution.py:35
  21.6 2.2 %copy-start.1 = (bf16[1024,2048]{1,0:T(8,128)(2,1)S(1)}, bf16[1024,2048]{1,0:T(8,128)(2,1)}, u32[]{:S(2)}) copy-start(bf16[1024,2048]{1,0:T(8,128)(2,1)} %train_ref) | copy-start | bytes 12582916
  28.6 11.3 %collective-permute-start.5 = (bf16[128,2048]{1,0:T(8,128)(2,1)S(1)}, bf16[128,2048]{1,0:T(8,128)(2,1)S(1)}, u32[]{:S(2)}, u32[]{:S(2)}) collective-permute-start(bf16[128,2048]{1,0:T(8,128)(2,1)S(1)} %pad_maximum_fusion.low), channel_id=1, source_target_pairs={{0,32},{1,9},{2,34},{3,11},{4,36},{5,13},{6,38},{7,15},{8,40},{9,1... | collective-permute-start | bytes 1572872 | tf_op jit(solution)/shard_map/ppermute | solution.py:35
  30.2 9.7 %collective-permute-start.6 = (bf16[128,2048]{1,0:T(8,128)(2,1)S(1)}, bf16[128,2048]{1,0:T(8,128)(2,1)S(1)}, u32[]{:S(2)}, u32[]{:S(2)}) collective-permute-start(bf16[128,2048]{1,0:T(8,128)(2,1)S(1)} %pad_maximum_fusion.1.high), channel_id=1, source_target_pairs={{0,224},{1,25},{2,226},{3,27},{4,228},{5,29},{6,230},{7,31},{8,232... | collective-permute-start | bytes 1572872 | tf_op jit(solution)/shard_map/ppermute | solution.py:35
  32.9 12.7 %collective-permute-start.7 = (bf16[128,2048]{1,0:T(8,128)(2,1)S(1)}, bf16[128,2048]{1,0:T(8,128)(2,1)S(1)}, u32[]{:S(2)}, u32[]{:S(2)}) collective-permute-start(bf16[128,2048]{1,0:T(8,128)(2,1)S(1)} %pad_maximum_fusion.1.high), channel_id=1, source_target_pairs={{0,32},{1,9},{2,34},{3,11},{4,36},{5,13},{6,38},{7,15},{8,40},{9,1... | collective-permute-start | bytes 1572872 | tf_op jit(solution)/shard_map/ppermute | solution.py:35
  32.9 12.8 %collective-permute-start.8 = (bf16[128,2048]{1,0:T(8,128)(2,1)S(1)}, bf16[128,2048]{1,0:T(8,128)(2,1)S(1)}, u32[]{:S(2)}, u32[]{:S(2)}) collective-permute-start(bf16[128,2048]{1,0:T(8,128)(2,1)S(1)} %pad_maximum_fusion.low), channel_id=1, source_target_pairs={{0,224},{1,25},{2,226},{3,27},{4,228},{5,29},{6,230},{7,31},{8,232... | collective-permute-start | bytes 1572872 | tf_op jit(solution)/shard_map/ppermute | solution.py:35
  39.9 12.4 %collective-permute-start.14 = (bf16[128,2048]{1,0:T(8,128)(2,1)S(1)}, bf16[128,2048]{1,0:T(8,128)(2,1)S(1)}, u32[]{:S(2)}, u32[]{:S(2)}) collective-permute-start(bf16[128,2048]{1,0:T(8,128)(2,1)S(1)} %collective-permute-done.5.low), channel_id=1, source_target_pairs={{0,32},{1,9},{2,34},{3,11},{4,36},{5,13},{6,38},{7,15},{8,40},{9,1... | collective-permute-start | bytes 1572872 | tf_op jit(solution)/shard_map/ppermute | solution.py:35
  41.1 11.3 %collective-permute-start.15 = (bf16[128,2048]{1,0:T(8,128)(2,1)S(1)}, bf16[128,2048]{1,0:T(8,128)(2,1)S(1)}, u32[]{:S(2)}, u32[]{:S(2)}) collective-permute-start(bf16[128,2048]{1,0:T(8,128)(2,1)S(1)} %collective-permute-done.6.high), channel_id=1, source_target_pairs={{0,224},{1,25},{2,226},{3,27},{4,228},{5,29},{6,230},{7,31},{8,232... | collective-permute-start | bytes 1572872 | tf_op jit(solution)/shard_map/ppermute | solution.py:35
  45.1 1.6 %collective-permute-start.9 = (bf16[256,512]{1,0:T(8,128)(2,1)S(1)}, bf16[256,512]{1,0:T(8,128)(2,1)S(1)}, u32[]{:S(2)}, u32[]{:S(2)}) collective-permute-start(bf16[256,512]{1,0:T(8,128)(2,1)S(1)} %get-tuple-element.60), channel_id=1, source_target_pairs={{0,1},{1,0},{2,3},{3,2},{4,5},{5,4},{6,7},{7,6},{8,9},{9,8},{10,11... | collective-permute-start | bytes 786440 | tf_op jit(solution)/shard_map/ppermute | solution.py:39
  45.5 3.3 %collective-permute-start.10 = (bf16[256,512]{1,0:T(8,128)(2,1)S(1)}, bf16[256,512]{1,0:T(8,128)(2,1)S(1)}, u32[]{:S(2)}, u32[]{:S(2)}) collective-permute-start(bf16[256,512]{1,0:T(8,128)(2,1)S(1)} %get-tuple-element.56), channel_id=1, source_target_pairs={{0,1},{1,0},{2,3},{3,2},{4,5},{5,4},{6,7},{7,6},{8,9},{9,8},{10,11... | collective-permute-start | bytes 786440 | tf_op jit(solution)/shard_map/ppermute | solution.py:39
  48.3 1.4 %collective-permute-start.11 = (bf16[128,512]{1,0:T(8,128)(2,1)S(1)}, bf16[128,512]{1,0:T(8,128)(2,1)S(1)}, u32[]{:S(2)}, u32[]{:S(2)}) collective-permute-start(bf16[128,512]{1,0:T(8,128)(2,1)S(1)} %get-tuple-element.64), channel_id=1, source_target_pairs={{0,1},{1,0},{2,3},{3,2},{4,5},{5,4},{6,7},{7,6},{8,9},{9,8},{10,11... | collective-permute-start | bytes 393224 | tf_op jit(solution)/shard_map/ppermute | solution.py:39
  48.5 1.4 %collective-permute-start.12 = (bf16[128,512]{1,0:T(8,128)(2,1)S(1)}, bf16[128,512]{1,0:T(8,128)(2,1)S(1)}, u32[]{:S(2)}, u32[]{:S(2)}) collective-permute-start(bf16[128,512]{1,0:T(8,128)(2,1)S(1)} %get-tuple-element.65), channel_id=1, source_target_pairs={{0,1},{1,0},{2,3},{3,2},{4,5},{5,4},{6,7},{7,6},{8,9},{9,8},{10,11... | collective-permute-start | bytes 393224 | tf_op jit(solution)/shard_map/ppermute | solution.py:39
  50.6 9.9 %collective-permute-start.13 = (bf16[576,256]{1,0:T(8,128)(2,1)S(1)}, bf16[576,256]{1,0:T(8,128)(2,1)S(1)}, u32[]{:S(2)}, u32[]{:S(2)}) collective-permute-start(bf16[576,256]{1,0:T(8,128)(2,1)S(1)} %get-tuple-element.67), channel_id=1, source_target_pairs={{0,2},{1,3},{2,0},{3,1},{4,6},{5,7},{6,4},{7,5},{8,10},{9,11},{10,... | collective-permute-start | bytes 884744 | tf_op jit(solution)/shard_map/ppermute | solution.py:39
  53.9 1.6 %collective-permute-start.17 = (bf16[144,512]{1,0:T(8,128)(2,1)S(1)}, bf16[144,512]{1,0:T(8,128)(2,1)S(1)}, u32[]{:S(2)}, u32[]{:S(2)}) collective-permute-start(bf16[144,512]{1,0:T(8,128)(2,1)S(1)} %get-tuple-element.76), channel_id=1, source_target_pairs={{0,1},{1,0},{2,3},{3,2},{4,5},{5,4},{6,7},{7,6},{8,9},{9,8},{10,11... | collective-permute-start | bytes 442376 | tf_op jit(solution)/shard_map/ppermute | solution.py:39
  54.0 1.5 %collective-permute-start.16 = (bf16[128,512]{1,0:T(8,128)(2,1)S(1)}, bf16[128,512]{1,0:T(8,128)(2,1)S(1)}, u32[]{:S(2)}, u32[]{:S(2)}) collective-permute-start(bf16[128,512]{1,0:T(8,128)(2,1)S(1)} %get-tuple-element.75), channel_id=1, source_target_pairs={{0,1},{1,0},{2,3},{3,2},{4,5},{5,4},{6,7},{7,6},{8,9},{9,8},{10,11... | collective-permute-start | bytes 393224 | tf_op jit(solution)/shard_map/ppermute | solution.py:39
  56.2 8.8 %collective-permute-start.18 = (bf16[256,256]{1,0:T(8,128)(2,1)S(1)}, bf16[256,256]{1,0:T(8,128)(2,1)S(1)}, u32[]{:S(2)}, u32[]{:S(2)}) collective-permute-start(bf16[256,256]{1,0:T(8,128)(2,1)S(1)} %get-tuple-element.79), channel_id=1, source_target_pairs={{0,2},{1,3},{2,0},{3,1},{4,6},{5,7},{6,4},{7,5},{8,10},{9,11},{10,... | collective-permute-start | bytes 393224 | tf_op jit(solution)/shard_map/ppermute | solution.py:39
  56.7 8.3 %collective-permute-start.19 = (bf16[208,256]{1,0:T(8,128)(2,1)S(1)}, bf16[208,256]{1,0:T(8,128)(2,1)S(1)}, u32[]{:S(2)}, u32[]{:S(2)}) collective-permute-start(bf16[208,256]{1,0:T(8,128)(2,1)S(1)} %get-tuple-element.80), channel_id=1, source_target_pairs={{0,2},{1,3},{2,0},{3,1},{4,6},{5,7},{6,4},{7,5},{8,10},{9,11},{10,... | collective-permute-start | bytes 319496 | tf_op jit(solution)/shard_map/ppermute | solution.py:39

commit v4 on v3

--- a/solution.py
+++ b/solution.py
@@ -14,7 +14,6 @@
 BLOCK = 4 * SHARD
 NEAR = (0, -1, 1, -2)
 VMEM = pl.BlockSpec(memory_space=pltpu.VMEM)
-SMEM = pl.BlockSpec(memory_space=pltpu.SMEM)
 MIB = 1 << 20
 
 
@@ -84,10 +83,6 @@
     return -2 if step == 2 else step
 
 
-EARLY = [block for block in ORDER if 2 not in map(abs, block)]
-LATE = [block for block in ORDER if 2 in map(abs, block)]
-
-
 def slot(block):
     at = ORDER.index(block) * BLOCK
     for stage, rows in enumerate(STAGE_ROWS):
@@ -99,6 +94,20 @@
 def twin(block):
     other = (wrap(block[1]), wrap(block[0]))
     return next(b for b in ORDER if (wrap(b[0]), wrap(b[1])) == other)
+
+
+def stage_of(block):
+    return max(slot(block)[0], slot(twin(block))[0])
+
+
+EARLY = sorted((block for block in ORDER if stage_of(block) < 3), key=lambda block: stage_of(block) > 1)
+LATE = [block for block in ORDER if stage_of(block) == 3]
+FIRST = 3
+
+
+def place_here():
+    row = lax.axis_index("rows")
+    return row // (NY * NX), (row // NX) & (NY - 1), row & (NX - 1), lax.axis_index("feat")
 
 
 def depth(core, block):
@@ -136,8 +145,8 @@
     to_ref[...] = from_ref[...]
 
 
-def prepare_kernel(place, train_ref, turned_ref, sums_ref):
-    me = place[3]
+def prepare_kernel(train_ref, turned_ref, sums_ref):
+    me = lax.axis_index("feat")
     for k, mask in enumerate((0, 2, 1, 3)):
         start = pl.multiple_of((me ^ mask) * 256, 256)
         for j in range(0, 2048, 512):
@@ -182,16 +191,22 @@
     multiply(rounded_ref, turned_ref, [keep_ref], 0)
 
 
-def last_kept_kernel(turned_ref, rounded_ref, keep_ref):
+def sent_kernel(turned_ref, precond_ref, low, high, rounded_ref, send_low, send_high, sums_ref):
+    condition((low, high), precond_ref, sums_ref, rounded_ref)
+    multiply(rounded_ref, turned_ref, [send_low, send_high], 2)
+
+
+def kept_kernel(turned_ref, rounded_ref, keep_ref):
     multiply(rounded_ref, turned_ref, [keep_ref], 0)
 
 
 def last_sent_kernel(
-    place, turned_ref, precond_ref, low, high, sums0, sums1, sums2, train_ref, rounded_ref, send_low, send_high, lanes_ref, sums3, all_sums
+    turned_ref, precond_ref, low, high, sums0, sums1, sums2, train_ref, rounded_ref, send_low, send_high, lanes_ref, sums3, all_sums
 ):
     condition((low, high), precond_ref, sums3, rounded_ref)
     multiply(rounded_ref, turned_ref, [send_low, send_high], 2)
     sums = (sums0, sums1, sums2, sums3)
+    place = place_here()
     for block in ORDER:
         stage, at = slot(block)
         for part, row in enumerate(first_rows(place, block)):
@@ -205,8 +220,9 @@
     send_high[low.shape[0] :, :] = jnp.concatenate(extra, axis=0)
 
 
-def add_blocks(place, blocks, keeps, gots, mine_ref, send_ref, at=0):
+def add_blocks(blocks, keeps, gots, mine_ref, send_ref, at=0):
     first = at
+    place = place_here()
     for block in blocks:
         stage, base = slot(block)
         there, rows = twin_rows(place, block)
@@ -218,17 +234,21 @@
             at += SHARD
 
 
-def early_kernel(place, *refs):
+def first_kernel(keep0, keep1, got0, got1, mine_ref, send_ref):
+    add_blocks(EARLY[:FIRST], (keep0, keep1), (got0, got1), mine_ref, send_ref)
+
+
+def early_kernel(*refs):
     keeps, gots = refs[: len(STAGES) - 1], refs[len(STAGES) - 1 : -2]
-    add_blocks(place, EARLY, keeps, gots, *refs[-2:])
-
-
-def late_kernel(place, *refs):
+    add_blocks(EARLY[FIRST:], keeps, gots, *refs[-2:])
+
+
+def late_kernel(*refs):
     first, last = len(STAGES), len(STAGES) + sum(SENDS)
     keeps, gots, rest = refs[:first], refs[first:last], refs[last:]
     lanes_ref, train_ref, mine_ref, send_low, send_high, lanes2_ref, train2_ref = rest
-    add_blocks(place, LATE[:4], keeps, gots, mine_ref, send_low)
-    add_blocks(place, LATE[4:], keeps, gots, mine_ref, send_high, 4 * BLOCK)
+    add_blocks(LATE[:4], keeps, gots, mine_ref, send_low)
+    add_blocks(LATE[4:], keeps, gots, mine_ref, send_high, 4 * BLOCK)
     got = gots[-1][keeps[-1].shape[0] // 2 :, :].astype(jnp.float32)
     extra = []
     for j in range(2):
@@ -247,11 +267,13 @@
     return rows[at : at + 1] + (rows[at + 1 : at + 2] + rows[at + 2 : at + 3])
 
 
-def merge_kernel(mine0, got0, all_ref):
-    all_ref[...] = mine0[...] + got0[...].astype(jnp.float32)
-
-
-def finish_kernel(place, early_ref, mine1, got1, got2, lanes_ref, train_ref, out_ref, scale_ref, sums_ref, sem):
+def merge_kernel(mine0, mine1, got0, got1, all_ref):
+    rows = FIRST * BLOCK
+    all_ref[:rows, :] = mine0[...] + got0[...].astype(jnp.float32)
+    all_ref[rows:, :] = mine1[...] + got1[...].astype(jnp.float32)
+
+
+def finish_kernel(early_ref, mine1, got1, got2, lanes_ref, train_ref, out_ref, scale_ref, sums_ref, sem):
     split = got1.shape[0]
     late = mine1.shape[0]
     got = got2[late - split :, :].astype(jnp.float32)
@@ -261,6 +283,7 @@
         scale_ref[i : i + 128, :] = jnp.broadcast_to(query[:, i : i + 128], (128, 128)).T
     train = (1.0 / jnp.sqrt(train_ref[...] + sum3(got, 12) + EPS)) * math.sqrt(F)
     at = 0
+    place = place_here()
     for block in EARLY + LATE:
         for row in first_rows(place, block):
             base = at - len(EARLY) * BLOCK
@@ -278,11 +301,11 @@
     pltpu.make_async_copy(sums_ref, out_ref, sem).wait()
 
 
-def call(kernel, outs, inputs, scratch=(), smem=0, out_spec=VMEM):
+def call(kernel, outs, inputs, scratch=(), out_spec=VMEM):
     return pl.pallas_call(
         kernel,
         out_shape=[jax.ShapeDtypeStruct(s, d) for s, d in outs],
-        in_specs=[SMEM] * smem + [VMEM] * (len(inputs) - smem),
+        in_specs=[VMEM] * len(inputs),
         out_specs=[out_spec] * len(outs),
         scratch_shapes=list(scratch),
         compiler_params=pltpu.CompilerParams(vmem_limit_bytes=24 * MIB),
@@ -292,17 +315,14 @@
 
 def on_device(query_grads, train_grads, precond):
     f32, bf16 = jnp.float32, jnp.bfloat16
-    row = lax.axis_index("rows")
-    place = jnp.stack([row // (NY * NX), row // NX % NY, row % NX, lax.axis_index("feat")]).astype(jnp.int32)
 
     def prepare(four):
         train, _ = together(train_grads, four)
         return call(
             prepare_kernel,
             [((4, 2048, 256), bf16), ((4, 256), f32)],
-            [place, train],
-            smem=1,
-        )
+            [train],
+            )
 
     def product(pieces, prepared, sends=1):
         rows = sum(piece.shape[0] for piece in pieces)
@@ -317,16 +337,29 @@
     turned, train_sums = prepared
     keep, send, squares = done
     keeps, gots, sums = [keep], [across(send, 1)], [squares]
-    for n, pieces in enumerate(stages):
-        *pieces, _ = together(*pieces, gots[-1] if n else send)
-        keep, *sends, squares = product(pieces, prepared, SENDS[n + 1])
-        keeps.append(keep)
-        gots += [across(send, 1) for send in sends]
-        sums.append(squares)
+    *pieces, _ = together(*stages[0], squares)
+    keep, send, squares = product(pieces, prepared)
+    keeps.append(keep)
+    gots.append(across(send, 1))
+    sums.append(squares)
+    rows = STAGE_ROWS[2]
+    *pieces, _, _ = together(*stages[1], squares, gots[0])
+    rounded, send_low, send_high, squares = call(
+        sent_kernel,
+        [((rows, 2048), bf16), *[((rows // 2, 512), bf16)] * 2, ((rows, 128), f32)],
+        [turned, precond, *pieces],
+    )
+    sums.append(squares)
+    first = FIRST * BLOCK
     early = len(EARLY) * BLOCK
     late = len(LATE) * BLOCK
+    mine_first, send = call(first_kernel, [((first, 256), f32), ((first, 256), bf16)], [*keeps, *gots])
+    got_first = across(send, 2)
+    rounded, _ = together(rounded, send)
+    keeps.append(call(kept_kernel, [((rows, 512), f32)], [turned, rounded])[0])
+    gots += [across(send_low, 1), across(send_high, 1)]
     mine0, send = call(
-        early_kernel, [((early, 256), f32), ((early, 256), bf16)], [place, *keeps, *gots], smem=1
+        early_kernel, [((early - first, 256), f32), ((early - first, 256), bf16)], [*keeps, *gots]
     )
     got0 = across(send, 2)
     low, high, _ = together(*last, send)
@@ -334,11 +367,12 @@
     rounded, send_low, send_high, lanes = call(
         last_sent_kernel,
         [((rows, 2048), bf16), ((rows // 2, 512), bf16), ((rows // 2 + SHARD, 512), bf16), ((1, 1024), f32)],
-        [place, turned, precond, low, high, *sums, train_sums],
+        [turned, precond, low, high, *sums, train_sums],
         scratch=[pltpu.VMEM((rows, 128), f32), pltpu.VMEM((1024, 128), f32)],
-        smem=1,
     )
-    keep = call(last_kept_kernel, [((rows, 512), f32)], [turned, rounded])[0]
+    keeps.append(call(kept_kernel, [((rows, 512), f32)], [turned, rounded])[0])
+    send_low, send_high, got_first = together(send_low, send_high, got_first)
+    gots += [across(send_low, 1), across(send_high, 1)]
     mine1, send_low, send_high, lanes, train = call(
         late_kernel,
         [
@@ -348,17 +382,16 @@
             ((1, 1024), f32),
             ((1, 256), f32),
         ],
-        [place, *keeps, keep, *gots, across(send_low, 1), across(send_high, 1), lanes, train_sums],
-        smem=1,
+        [*keeps, *gots, lanes, train_sums],
     )
+    send_high, got0 = together(send_high, got0)
     got1, got2 = across(send_low, 2), across(send_high, 2)
-    merged = call(merge_kernel, [((early, 256), f32)], [mine0, got0])[0]
+    merged = call(merge_kernel, [((early, 256), f32)], [mine_first, mine0, got_first, got0])[0]
     return call(
         finish_kernel,
         [((1024, 256), f32)],
-        [place, merged, mine1, got1, got2, lanes, train],
+        [merged, mine1, got1, got2, lanes, train],
         scratch=[pltpu.VMEM((1024, 128), f32), pltpu.VMEM((1024, 256), f32), pltpu.SemaphoreType.DMA],
-        smem=1,
         out_spec=pl.BlockSpec(memory_space=pl.ANY),
     )[0]
 

time: 67.2 us -> 65.7 us (0.978)
  Pallas kernels: 11.9 us -> 9.3 us
  starting transfers between devices: 32 us -> 34.4 us
  waiting for transfers between devices: 19.5 us -> 18.1 us
    ppermute x9 -> x10, waiting for transfers between devices: 8.95 us -> 5.1 us  [across(): return lax.ppermute(value, 'feat', [(f, f ^ mask) for f in range(4)])]
    ppermute x9 -> x10, starting transfers between devices: 5.3 us -> 7.91 us  [across(): return lax.ppermute(value, 'feat', [(f, f ^ mask) for f in range(4)])]
    pallas_call x11 -> x13, Pallas kernels: 11.9 us -> 9.3 us  [call(): pl.pallas_call(kernel, out_shape=[jax.ShapeDtypeStruct(s, d) for s, d in...]
    ppermute x11, waiting for transfers between devices: 10.6 us -> 13 us  [shift(): return lax.ppermute(value, ('rows', 'feat'), pairs)]
  transfers between devices with their start and end apart: 20 -> 21, of which waited for: 12 -> 11; matrix products, arithmetic and copies ran while one was open for 0% -> 0% of each run, Pallas kernels for 15% -> 12%
where the time goes in v4:
time: 65.7 us; the launch traced here: 65.3 us
  starting transfers between devices  34.4 us (52%)
  waiting for transfers between devices  18.1 us (28%)
  Pallas kernels  9.3 us (14%)
  local copies, waits for them, and re-layouts  3.06 us (5%)
    ppermute x11, starting transfers between devices, shift(): return lax.ppermute(value, ('rows', 'feat'), pairs)  26.5 us
    ppermute x11, waiting for transfers between devices, shift(): return lax.ppermute(value, ('rows', 'feat'), pairs)  13 us
    pallas_call x13, Pallas kernels, call(): pl.pallas_call(kernel, out_shape=[jax.ShapeDtypeStruct(s, d) for s, d in...  9.3 us
    ppermute x10, starting transfers between devices, across(): return lax.ppermute(value, 'feat', [(f, f ^ mask) for f in range(4)])  7.91 us
    ppermute x10, waiting for transfers between devices, across(): return lax.ppermute(value, 'feat', [(f, f ^ mask) for f in range(4)])  5.1 us
    unnamed x6, local copies, waits for them, and re-layouts  3.06 us
  transfers between devices with their start and end apart: 21, of which 11 were waited for; matrix products, arithmetic and copies ran while one was open for 0% of the time, Pallas kernels for 12%

profile of v4, /device:TPU:8, one launch (start us, length us, event | category | flops | bytes accessed | tf_op | source)
XLA Modules:
  0.0 65.3 jit_solution(2728452733422666610)
XLA Ops:
  0.0 7.2 %collective-permute-start = (bf16[16,2048]{1,0:T(8,128)(2,1)}, bf16[16,2048]{1,0:T(8,128)(2,1)S(1)}, u32[]{:S(2)}, u32[]{:S(2)}) collective-permute-start(bf16[16,2048]{1,0:T(8,128)(2,1)} %from_ref.1), channel_id=1, source_target_pairs={{0,128},{1,129},{2,130},{3,131},{4,132},{5,133},{6,134},{7,135},{8... | collective-permute-start | bytes 196616 | tf_op jit(solution)/shard_map/ppermute | solution.py:34
  7.2 0.9 %copy-done.2 = bf16[16,2048]{1,0:T(8,128)(2,1)S(1)} copy-done((bf16[16,2048]{1,0:T(8,128)(2,1)S(1)}, bf16[16,2048]{1,0:T(8,128)(2,1)}, u32[]{:S(2)}) %copy-start.2) | copy-done | bytes 65560
  8.1 1.9 %collective-permute-done = bf16[16,2048]{1,0:T(8,128)(2,1)S(1)} collective-permute-done((bf16[16,2048]{1,0:T(8,128)(2,1)}, bf16[16,2048]{1,0:T(8,128)(2,1)S(1)}, u32[]{:S(2)}, u32[]{:S(2)}) %collective-permute-start) | collective-permute-done | bytes 65568 | tf_op jit(solution)/shard_map/ppermute | solution.py:34
  10.0 3.1 %collective-permute-start.1 = (bf16[32,2048]{1,0:T(8,128)(2,1)S(1)}, bf16[32,2048]{1,0:T(8,128)(2,1)S(1)}, u32[]{:S(2)}, u32[]{:S(2)}) collective-permute-start(bf16[32,2048]{1,0:T(8,128)(2,1)S(1)} %pad_maximum_fusion.3), channel_id=1, source_target_pairs={{0,4},{1,5},{2,6},{3,7},{4,0},{5,1},{6,2},{7,3},{8,12},{9,13},{10,... | collective-permute-start | bytes 393224 | tf_op jit(solution)/shard_map/ppermute | solution.py:34
  13.1 3.4 %collective-permute-done.1 = bf16[32,2048]{1,0:T(8,128)(2,1)S(1)} collective-permute-done((bf16[32,2048]{1,0:T(8,128)(2,1)S(1)}, bf16[32,2048]{1,0:T(8,128)(2,1)S(1)}, u32[]{:S(2)}, u32[]{:S(2)}) %collective-permute-start.1) | collective-permute-done | bytes 131104 | tf_op jit(solution)/shard_map/ppermute | solution.py:34
  16.5 1.7 %collective-permute-start.2 = (bf16[64,2048]{1,0:T(8,128)(2,1)S(1)}, bf16[64,2048]{1,0:T(8,128)(2,1)S(1)}, u32[]{:S(2)}, u32[]{:S(2)}) collective-permute-start(bf16[64,2048]{1,0:T(8,128)(2,1)S(1)} %pad_maximum_fusion.2), channel_id=1, source_target_pairs={{0,8},{1,33},{2,10},{3,35},{4,12},{5,37},{6,14},{7,39},{8,16},{9,4... | collective-permute-start | bytes 786440 | tf_op jit(solution)/shard_map/ppermute | solution.py:34
  18.2 1.2 %collective-permute-start.4 = (bf16[64,2048]{1,0:T(8,128)(2,1)S(1)}, bf16[64,2048]{1,0:T(8,128)(2,1)S(1)}, u32[]{:S(2)}, u32[]{:S(2)}) collective-permute-start(bf16[64,2048]{1,0:T(8,128)(2,1)S(1)} %pad_maximum_fusion.2), channel_id=1, source_target_pairs={{0,16},{1,65},{2,18},{3,67},{4,20},{5,69},{6,22},{7,71},{8,24},{9,... | collective-permute-start | bytes 786440 | tf_op jit(solution)/shard_map/ppermute | solution.py:34
  19.4 2.1 %collective-permute-start.3 = (bf16[64,2048]{1,0:T(8,128)(2,1)S(1)}, bf16[64,2048]{1,0:T(8,128)(2,1)S(1)}, u32[]{:S(2)}, u32[]{:S(2)}) collective-permute-start(bf16[64,2048]{1,0:T(8,128)(2,1)S(1)} %pad_maximum_fusion.2), channel_id=1, source_target_pairs={{0,24},{1,225},{2,26},{3,227},{4,28},{5,229},{6,30},{7,231},{8,0},... | collective-permute-start | bytes 786440 | tf_op jit(solution)/shard_map/ppermute | solution.py:34
  21.5 2.2 %copy-done.1 = bf16[1024,2048]{1,0:T(8,128)(2,1)S(1)} copy-done((bf16[1024,2048]{1,0:T(8,128)(2,1)S(1)}, bf16[1024,2048]{1,0:T(8,128)(2,1)}, u32[]{:S(2)}) %copy-start.1) | copy-done | bytes 4194328
  23.7 1.2 %shard_map.38 = (bf16[4,2048,256]{2,1,0:T(8,128)(2,1)S(1)}, f32[4,256]{1,0:T(4,128)S(1)}) custom-call(bf16[1024,2048]{1,0:T(8,128)(2,1)S(1)} %copy-done.1), custom_call_target="tpu_custom_call" | custom-call | flops 1 | bytes 1 | tf_op jit(solution)/shard_map/pallas_call | solution.py:305
  25.0 0.0 collective-permute-done.2
  25.0 1.1 %collective-permute-done.4 = bf16[64,2048]{1,0:T(8,128)(2,1)S(1)} collective-permute-done((bf16[64,2048]{1,0:T(8,128)(2,1)S(1)}, bf16[64,2048]{1,0:T(8,128)(2,1)S(1)}, u32[]{:S(2)}, u32[]{:S(2)}) %collective-permute-start.4) | collective-permute-done | bytes 262176 | tf_op jit(solution)/shard_map/ppermute | solution.py:34
  26.2 2.4 %collective-permute-done.3 = bf16[64,2048]{1,0:T(8,128)(2,1)S(1)} collective-permute-done((bf16[64,2048]{1,0:T(8,128)(2,1)S(1)}, bf16[64,2048]{1,0:T(8,128)(2,1)S(1)}, u32[]{:S(2)}, u32[]{:S(2)}) %collective-permute-start.3) | collective-permute-done | bytes 262176 | tf_op jit(solution)/shard_map/ppermute | solution.py:34
  28.6 1.6 %collective-permute-start.5 = (bf16[128,2048]{1,0:T(8,128)(2,1)S(1)}, bf16[128,2048]{1,0:T(8,128)(2,1)S(1)}, u32[]{:S(2)}, u32[]{:S(2)}) collective-permute-start(bf16[128,2048]{1,0:T(8,128)(2,1)S(1)} %pad_maximum_fusion.low), channel_id=1, source_target_pairs={{0,32},{1,9},{2,34},{3,11},{4,36},{5,13},{6,38},{7,15},{8,40},{9,1... | collective-permute-start | bytes 1572872 | tf_op jit(solution)/shard_map/ppermute | solution.py:34
  30.2 2.6 %collective-permute-start.6 = (bf16[128,2048]{1,0:T(8,128)(2,1)S(1)}, bf16[128,2048]{1,0:T(8,128)(2,1)S(1)}, u32[]{:S(2)}, u32[]{:S(2)}) collective-permute-start(bf16[128,2048]{1,0:T(8,128)(2,1)S(1)} %pad_maximum_fusion.1.high), channel_id=1, source_target_pairs={{0,224},{1,25},{2,226},{3,27},{4,228},{5,29},{6,230},{7,31},{8,232... | collective-permute-start | bytes 1572872 | tf_op jit(solution)/shard_map/ppermute | solution.py:34
  32.9 3.5 %collective-permute-start.10 = (bf16[128,2048]{1,0:T(8,128)(2,1)S(1)}, bf16[128,2048]{1,0:T(8,128)(2,1)S(1)}, u32[]{:S(2)}, u32[]{:S(2)}) collective-permute-start(bf16[128,2048]{1,0:T(8,128)(2,1)S(1)} %pad_maximum_fusion.low), channel_id=1, source_target_pairs={{0,224},{1,25},{2,226},{3,27},{4,228},{5,29},{6,230},{7,31},{8,232... | collective-permute-start | bytes 1572872 | tf_op jit(solution)/shard_map/ppermute | solution.py:34
  36.4 1.5 %shard_map.39 = (f32[256,512]{1,0:T(8,128)S(1)}, bf16[256,512]{1,0:T(8,128)(2,1)S(1)}, f32[256,128]{1,0:T(8,128)S(1)}) custom-call(bf16[4,2048,256]{2,1,0:T(8,128)(2,1)S(1)} %get-tuple-element.57.turned_ref, bf16[8,256,256]{2,1,0:T(8,128)(2,1)S(1)} %copy-done, bf16[128,2048]{1,0:T(8,128)(2,1)S(1)} %pad_maximum_fusion.low, ...), custom_call_target="tpu_custom_call" | custom-call | flops 1 | bytes 1 | tf_op jit(solution)/shard_map/pallas_call | solution.py:305
  37.9 2.0 %collective-permute-done.5.low = bf16[128,2048]{1,0:T(8,128)(2,1)S(1)} collective-permute-done((bf16[128,2048]{1,0:T(8,128)(2,1)S(1)}, bf16[128,2048]{1,0:T(8,128)(2,1)S(1)}, u32[]{:S(2)}, u32[]{:S(2)}) %collective-permute-start.5) | collective-permute-done | bytes 524320 | tf_op jit(solution)/shard_map/ppermute | solution.py:34
  39.9 0.0 collective-permute-done.6.high
  39.9 1.1 %collective-permute-start.13 = (bf16[128,2048]{1,0:T(8,128)(2,1)S(1)}, bf16[128,2048]{1,0:T(8,128)(2,1)S(1)}, u32[]{:S(2)}, u32[]{:S(2)}) collective-permute-start(bf16[128,2048]{1,0:T(8,128)(2,1)S(1)} %collective-permute-done.5.low), channel_id=1, source_target_pairs={{0,32},{1,9},{2,34},{3,11},{4,36},{5,13},{6,38},{7,15},{8,40},{9,1... | collective-permute-start | bytes 1572872 | tf_op jit(solution)/shard_map/ppermute | solution.py:34
  41.1 2.4 %collective-permute-start.14 = (bf16[128,2048]{1,0:T(8,128)(2,1)S(1)}, bf16[128,2048]{1,0:T(8,128)(2,1)S(1)}, u32[]{:S(2)}, u32[]{:S(2)}) collective-permute-start(bf16[128,2048]{1,0:T(8,128)(2,1)S(1)} %collective-permute-done.6.high), channel_id=1, source_target_pairs={{0,224},{1,25},{2,226},{3,27},{4,228},{5,29},{6,230},{7,31},{8,232... | collective-permute-start | bytes 1572872 | tf_op jit(solution)/shard_map/ppermute | solution.py:34
  43.4 0.0 collective-permute-start.7
  43.4 1.5 %shard_map.40 = (f32[256,512]{1,0:T(8,128)S(1)}, bf16[256,512]{1,0:T(8,128)(2,1)S(1)}, f32[256,128]{1,0:T(8,128)S(1)}) custom-call(bf16[4,2048,256]{2,1,0:T(8,128)(2,1)S(1)} %get-tuple-element.57.turned_ref, bf16[8,256,256]{2,1,0:T(8,128)(2,1)S(1)} %copy-done, bf16[128,2048]{1,0:T(8,128)(2,1)S(1)} %collective-permute-done.5.low, ...), custom_call_target="tpu_custom_call" | custom-call | flops 1 | bytes 1 | tf_op jit(solution)/shard_map/pallas_call | solution.py:305
  45.0 0.2 collective-permute-done.10.high
  45.2 0.6 collective-permute-start.8
  45.8 1.0 %collective-permute-done.9.low = bf16[128,2048]{1,0:T(8,128)(2,1)S(1)} collective-permute-done((bf16[128,2048]{1,0:T(8,128)(2,1)S(1)}, bf16[128,2048]{1,0:T(8,128)(2,1)S(1)}, u32[]{:S(2)}, u32[]{:S(2)}) %collective-permute-start.9) | collective-permute-done | bytes 524320 | tf_op jit(solution)/shard_map/ppermute | solution.py:34
  46.7 1.0 %shard_map.42 = (bf16[256,2048]{1,0:T(8,128)(2,1)S(1)}, bf16[128,512]{1,0:T(8,128)(2,1)S(1)}, bf16[128,512]{1,0:T(8,128)(2,1)S(1)}, f32[256,128]{1,0:T(8,128)S(1)}) custom-call(bf16[4,2048,256]{2,1,0:T(8,128)(2,1)S(1)} %get-tuple-element.57.turned_ref, bf16[8,256,256]{2,1,0:T(8,128)(2,1)S(1)} %copy-done, bf16[128,2048]{1,0:T(8,128)(2,1)S(1)} %collective-permute-done.9.low, ...), custom_call_target="tpu_custom_call" | custom-call | flops 1 | bytes 1 | tf_op jit(solution)/shard_map/pallas_call | solution.py:305
  47.8 0.1 collective-permute-start.11
  47.9 0.5 collective-permute-start.12
  48.4 0.0 collective-permute-done.8.got1.refs_4_.refs_5_
  48.4 1.9 %collective-permute-start.15 = (bf16[192,256]{1,0:T(8,128)(2,1)S(1)}, bf16[192,256]{1,0:T(8,128)(2,1)S(1)}, u32[]{:S(2)}, u32[]{:S(2)}) collective-permute-start(bf16[192,256]{1,0:T(8,128)(2,1)S(1)} %get-tuple-element.75), channel_id=1, source_target_pairs={{0,2},{1,3},{2,0},{3,1},{4,6},{5,7},{6,4},{7,5},{8,10},{9,11},{10,... | collective-permute-start | bytes 294920 | tf_op jit(solution)/shard_map/ppermute | solution.py:38
  50.3 0.7 %shard_map.43.refs_2_ = f32[256,512]{1,0:T(8,128)S(1)} custom-call(bf16[4,2048,256]{2,1,0:T(8,128)(2,1)S(1)} %get-tuple-element.57.turned_ref, bf16[256,2048]{1,0:T(8,128)(2,1)S(1)} %get-tuple-element.76.rounded_ref), custom_call_target="tpu_custom_call" | custom-call | flops 1 | bytes 1 | tf_op jit(solution)/shard_map/pallas_call | solution.py:305
  51.0 0.1 shard_map.44
  51.1 0.3 collective-permute-start.18
  51.4 0.9 %collective-permute-done.13.low = bf16[128,2048]{1,0:T(8,128)(2,1)S(1)} collective-permute-done((bf16[128,2048]{1,0:T(8,128)(2,1)S(1)}, bf16[128,2048]{1,0:T(8,128)(2,1)S(1)}, u32[]{:S(2)}, u32[]{:S(2)}) %collective-permute-start.13) | collective-permute-done | bytes 524320 | tf_op jit(solution)/shard_map/ppermute | solution.py:34
  52.4 1.0 %shard_map.45 = (bf16[256,2048]{1,0:T(8,128)(2,1)S(1)}, bf16[128,512]{1,0:T(8,128)(2,1)S(1)}, bf16[144,512]{1,0:T(8,128)(2,1)S(1)}, f32[1,1024]{1,0:T(1,128)S(1)}) custom-call(bf16[4,2048,256]{2,1,0:T(8,128)(2,1)S(1)} %get-tuple-element.57.turned_ref, bf16[8,256,256]{2,1,0:T(8,128)(2,1)S(1)} %copy-done, bf16[128,2048]{1,0:T(8,128)(2,1)S(1)} %collective-permute-done.13.low, ...), custom_call_target="tpu_custom_call" | custom-call | flops 1 | bytes 1 | tf_op jit(solution)/shard_map/pallas_call | solution.py:305
  53.4 0.0 collective-permute-done.15.got0
  53.4 0.1 collective-permute-start.17
  53.5 0.5 collective-permute-start.16
  54.0 0.7 %shard_map.46.refs_3_ = f32[256,512]{1,0:T(8,128)S(1)} custom-call(bf16[4,2048,256]{2,1,0:T(8,128)(2,1)S(1)} %get-tuple-element.57.turned_ref, bf16[256,2048]{1,0:T(8,128)(2,1)S(1)} %get-tuple-element.88.rounded_ref), custom_call_target="tpu_custom_call" | custom-call | flops 1 | bytes 1 | tf_op jit(solution)/shard_map/pallas_call | solution.py:305
  54.7 0.3 collective-permute-done.16.refs_8_
  55.0 0.1 shard_map.47
  55.2 2.5 %collective-permute-start.19 = (bf16[256,256]{1,0:T(8,128)(2,1)S(1)}, bf16[256,256]{1,0:T(8,128)(2,1)S(1)}, u32[]{:S(2)}, u32[]{:S(2)}) collective-permute-start(bf16[256,256]{1,0:T(8,128)(2,1)S(1)} %get-tuple-element.95), channel_id=1, source_target_pairs={{0,2},{1,3},{2,0},{3,1},{4,6},{5,7},{6,4},{7,5},{8,10},{9,11},{10,... | collective-permute-start | bytes 393224 | tf_op jit(solution)/shard_map/ppermute | solution.py:38
  57.7 0.1 collective-permute-done.18.got1
  57.8 1.5 %collective-permute-start.20 = (bf16[208,256]{1,0:T(8,128)(2,1)S(1)}, bf16[208,256]{1,0:T(8,128)(2,1)S(1)}, u32[]{:S(2)}, u32[]{:S(2)}) collective-permute-start(bf16[208,256]{1,0:T(8,128)(2,1)S(1)} %get-tuple-element.96), channel_id=1, source_target_pairs={{0,2},{1,3},{2,0},{3,1},{4,6},{5,7},{6,4},{7,5},{8,10},{9,11},{10,... | collective-permute-start | bytes 319496 | tf_op jit(solution)/shard_map/ppermute | solution.py:38
  59.3 0.1 shard_map.48.early_ref
  59.3 4.6 %collective-permute-done.20.got2 = bf16[208,256]{1,0:T(8,128)(2,1)S(1)} collective-permute-done((bf16[208,256]{1,0:T(8,128)(2,1)S(1)}, bf16[208,256]{1,0:T(8,128)(2,1)S(1)}, u32[]{:S(2)}, u32[]{:S(2)}) %collective-permute-start.20) | collective-permute-done | bytes 106528 | tf_op jit(solution)/shard_map/ppermute | solution.py:38
  63.9 1.2 %shard_map.49 = f32[1024,256]{1,0:T(8,128)} custom-call(f32[576,256]{1,0:T(8,128)S(1)} %shard_map.48.early_ref, f32[448,256]{1,0:T(8,128)S(1)} %get-tuple-element.94.mine1, bf16[256,256]{1,0:T(8,128)(2,1)S(1)} %collective-permute-done.19.got1, bf16[208,256]{1,0:T(8,128)(2,1)S(1)} %collective-permute-done.20.got2, f32[1,1024]{1,0:T(1,128)S(1)} %get-tuple-element.97.lanes_ref, ...), custom_call_target="tpu_custom_call" | custom-call | flops 1 | bytes 1 | tf_op jit(solution)/shard_map/pallas_call | solution.py:305
  (17 shorter events, 0.2 us)
Async XLA Ops:
  0.0 36.4 %copy-start = (bf16[8,256,256]{2,1,0:T(8,128)(2,1)S(1)}, bf16[8,256,256]{2,1,0:T(8,128)(2,1)}, u32[]{:S(2)}) copy-start(bf16[8,256,256]{2,1,0:T(8,128)(2,1)} %precond_ref.7) | copy-start | bytes 3145732
  0.0 9.9 %collective-permute-start = (bf16[16,2048]{1,0:T(8,128)(2,1)}, bf16[16,2048]{1,0:T(8,128)(2,1)S(1)}, u32[]{:S(2)}, u32[]{:S(2)}) collective-permute-start(bf16[16,2048]{1,0:T(8,128)(2,1)} %from_ref.1), channel_id=1, source_target_pairs={{0,128},{1,129},{2,130},{3,131},{4,132},{5,133},{6,134},{7,135},{8... | collective-permute-start | bytes 196616 | tf_op jit(solution)/shard_map/ppermute | solution.py:34
  7.2 0.9 %copy-start.2 = (bf16[16,2048]{1,0:T(8,128)(2,1)S(1)}, bf16[16,2048]{1,0:T(8,128)(2,1)}, u32[]{:S(2)}) copy-start(bf16[16,2048]{1,0:T(8,128)(2,1)} %from_ref.1) | copy-start | bytes 196612
  10.0 6.6 %collective-permute-start.1 = (bf16[32,2048]{1,0:T(8,128)(2,1)S(1)}, bf16[32,2048]{1,0:T(8,128)(2,1)S(1)}, u32[]{:S(2)}, u32[]{:S(2)}) collective-permute-start(bf16[32,2048]{1,0:T(8,128)(2,1)S(1)} %pad_maximum_fusion.3), channel_id=1, source_target_pairs={{0,4},{1,5},{2,6},{3,7},{4,0},{5,1},{6,2},{7,3},{8,12},{9,13},{10,... | collective-permute-start | bytes 393224 | tf_op jit(solution)/shard_map/ppermute | solution.py:34
  16.5 8.4 %collective-permute-start.2 = (bf16[64,2048]{1,0:T(8,128)(2,1)S(1)}, bf16[64,2048]{1,0:T(8,128)(2,1)S(1)}, u32[]{:S(2)}, u32[]{:S(2)}) collective-permute-start(bf16[64,2048]{1,0:T(8,128)(2,1)S(1)} %pad_maximum_fusion.2), channel_id=1, source_target_pairs={{0,8},{1,33},{2,10},{3,35},{4,12},{5,37},{6,14},{7,39},{8,16},{9,4... | collective-permute-start | bytes 786440 | tf_op jit(solution)/shard_map/ppermute | solution.py:34
  18.2 8.0 %collective-permute-start.4 = (bf16[64,2048]{1,0:T(8,128)(2,1)S(1)}, bf16[64,2048]{1,0:T(8,128)(2,1)S(1)}, u32[]{:S(2)}, u32[]{:S(2)}) collective-permute-start(bf16[64,2048]{1,0:T(8,128)(2,1)S(1)} %pad_maximum_fusion.2), channel_id=1, source_target_pairs={{0,16},{1,65},{2,18},{3,67},{4,20},{5,69},{6,22},{7,71},{8,24},{9,... | collective-permute-start | bytes 786440 | tf_op jit(solution)/shard_map/ppermute | solution.py:34
  19.4 9.2 %collective-permute-start.3 = (bf16[64,2048]{1,0:T(8,128)(2,1)S(1)}, bf16[64,2048]{1,0:T(8,128)(2,1)S(1)}, u32[]{:S(2)}, u32[]{:S(2)}) collective-permute-start(bf16[64,2048]{1,0:T(8,128)(2,1)S(1)} %pad_maximum_fusion.2), channel_id=1, source_target_pairs={{0,24},{1,225},{2,26},{3,227},{4,28},{5,229},{6,30},{7,231},{8,0},... | collective-permute-start | bytes 786440 | tf_op jit(solution)/shard_map/ppermute | solution.py:34
  21.5 2.2 %copy-start.1 = (bf16[1024,2048]{1,0:T(8,128)(2,1)S(1)}, bf16[1024,2048]{1,0:T(8,128)(2,1)}, u32[]{:S(2)}) copy-start(bf16[1024,2048]{1,0:T(8,128)(2,1)} %train_ref) | copy-start | bytes 12582916
  28.6 11.3 %collective-permute-start.5 = (bf16[128,2048]{1,0:T(8,128)(2,1)S(1)}, bf16[128,2048]{1,0:T(8,128)(2,1)S(1)}, u32[]{:S(2)}, u32[]{:S(2)}) collective-permute-start(bf16[128,2048]{1,0:T(8,128)(2,1)S(1)} %pad_maximum_fusion.low), channel_id=1, source_target_pairs={{0,32},{1,9},{2,34},{3,11},{4,36},{5,13},{6,38},{7,15},{8,40},{9,1... | collective-permute-start | bytes 1572872 | tf_op jit(solution)/shard_map/ppermute | solution.py:34
  30.2 9.7 %collective-permute-start.6 = (bf16[128,2048]{1,0:T(8,128)(2,1)S(1)}, bf16[128,2048]{1,0:T(8,128)(2,1)S(1)}, u32[]{:S(2)}, u32[]{:S(2)}) collective-permute-start(bf16[128,2048]{1,0:T(8,128)(2,1)S(1)} %pad_maximum_fusion.1.high), channel_id=1, source_target_pairs={{0,224},{1,25},{2,226},{3,27},{4,228},{5,29},{6,230},{7,31},{8,232... | collective-permute-start | bytes 1572872 | tf_op jit(solution)/shard_map/ppermute | solution.py:34
  32.9 12.3 %collective-permute-start.10 = (bf16[128,2048]{1,0:T(8,128)(2,1)S(1)}, bf16[128,2048]{1,0:T(8,128)(2,1)S(1)}, u32[]{:S(2)}, u32[]{:S(2)}) collective-permute-start(bf16[128,2048]{1,0:T(8,128)(2,1)S(1)} %pad_maximum_fusion.low), channel_id=1, source_target_pairs={{0,224},{1,25},{2,226},{3,27},{4,228},{5,29},{6,230},{7,31},{8,232... | collective-permute-start | bytes 1572872 | tf_op jit(solution)/shard_map/ppermute | solution.py:34
  36.3 10.4 %collective-permute-start.9 = (bf16[128,2048]{1,0:T(8,128)(2,1)S(1)}, bf16[128,2048]{1,0:T(8,128)(2,1)S(1)}, u32[]{:S(2)}, u32[]{:S(2)}) collective-permute-start(bf16[128,2048]{1,0:T(8,128)(2,1)S(1)} %pad_maximum_fusion.1.high), channel_id=1, source_target_pairs={{0,32},{1,9},{2,34},{3,11},{4,36},{5,13},{6,38},{7,15},{8,40},{9,1... | collective-permute-start | bytes 1572872 | tf_op jit(solution)/shard_map/ppermute | solution.py:34
  39.9 12.4 %collective-permute-start.13 = (bf16[128,2048]{1,0:T(8,128)(2,1)S(1)}, bf16[128,2048]{1,0:T(8,128)(2,1)S(1)}, u32[]{:S(2)}, u32[]{:S(2)}) collective-permute-start(bf16[128,2048]{1,0:T(8,128)(2,1)S(1)} %collective-permute-done.5.low), channel_id=1, source_target_pairs={{0,32},{1,9},{2,34},{3,11},{4,36},{5,13},{6,38},{7,15},{8,40},{9,1... | collective-permute-start | bytes 1572872 | tf_op jit(solution)/shard_map/ppermute | solution.py:34
  41.1 11.3 %collective-permute-start.14 = (bf16[128,2048]{1,0:T(8,128)(2,1)S(1)}, bf16[128,2048]{1,0:T(8,128)(2,1)S(1)}, u32[]{:S(2)}, u32[]{:S(2)}) collective-permute-start(bf16[128,2048]{1,0:T(8,128)(2,1)S(1)} %collective-permute-done.6.high), channel_id=1, source_target_pairs={{0,224},{1,25},{2,226},{3,27},{4,228},{5,29},{6,230},{7,31},{8,232... | collective-permute-start | bytes 1572872 | tf_op jit(solution)/shard_map/ppermute | solution.py:34
  43.4 3.3 %collective-permute-start.7 = (bf16[256,512]{1,0:T(8,128)(2,1)S(1)}, bf16[256,512]{1,0:T(8,128)(2,1)S(1)}, u32[]{:S(2)}, u32[]{:S(2)}) collective-permute-start(bf16[256,512]{1,0:T(8,128)(2,1)S(1)} %get-tuple-element.68), channel_id=1, source_target_pairs={{0,1},{1,0},{2,3},{3,2},{4,5},{5,4},{6,7},{7,6},{8,9},{9,8},{10,11... | collective-permute-start | bytes 786440 | tf_op jit(solution)/shard_map/ppermute | solution.py:38
  45.2 3.2 %collective-permute-start.8 = (bf16[256,512]{1,0:T(8,128)(2,1)S(1)}, bf16[256,512]{1,0:T(8,128)(2,1)S(1)}, u32[]{:S(2)}, u32[]{:S(2)}) collective-permute-start(bf16[256,512]{1,0:T(8,128)(2,1)S(1)} %get-tuple-element.69), channel_id=1, source_target_pairs={{0,1},{1,0},{2,3},{3,2},{4,5},{5,4},{6,7},{7,6},{8,9},{9,8},{10,11... | collective-permute-start | bytes 786440 | tf_op jit(solution)/shard_map/ppermute | solution.py:38
  47.8 3.2 %collective-permute-start.11 = (bf16[128,512]{1,0:T(8,128)(2,1)S(1)}, bf16[128,512]{1,0:T(8,128)(2,1)S(1)}, u32[]{:S(2)}, u32[]{:S(2)}) collective-permute-start(bf16[128,512]{1,0:T(8,128)(2,1)S(1)} %get-tuple-element.77), channel_id=1, source_target_pairs={{0,1},{1,0},{2,3},{3,2},{4,5},{5,4},{6,7},{7,6},{8,9},{9,8},{10,11... | collective-permute-start | bytes 393224 | tf_op jit(solution)/shard_map/ppermute | solution.py:38
  47.9 3.1 %collective-permute-start.12 = (bf16[128,512]{1,0:T(8,128)(2,1)S(1)}, bf16[128,512]{1,0:T(8,128)(2,1)S(1)}, u32[]{:S(2)}, u32[]{:S(2)}) collective-permute-start(bf16[128,512]{1,0:T(8,128)(2,1)S(1)} %get-tuple-element.78), channel_id=1, source_target_pairs={{0,1},{1,0},{2,3},{3,2},{4,5},{5,4},{6,7},{7,6},{8,9},{9,8},{10,11... | collective-permute-start | bytes 393224 | tf_op jit(solution)/shard_map/ppermute | solution.py:38
  48.4 5.0 %collective-permute-start.15 = (bf16[192,256]{1,0:T(8,128)(2,1)S(1)}, bf16[192,256]{1,0:T(8,128)(2,1)S(1)}, u32[]{:S(2)}, u32[]{:S(2)}) collective-permute-start(bf16[192,256]{1,0:T(8,128)(2,1)S(1)} %get-tuple-element.75), channel_id=1, source_target_pairs={{0,2},{1,3},{2,0},{3,1},{4,6},{5,7},{6,4},{7,5},{8,10},{9,11},{10,... | collective-permute-start | bytes 294920 | tf_op jit(solution)/shard_map/ppermute | solution.py:38
  51.1 6.7 %collective-permute-start.18 = (bf16[384,256]{1,0:T(8,128)(2,1)S(1)}, bf16[384,256]{1,0:T(8,128)(2,1)S(1)}, u32[]{:S(2)}, u32[]{:S(2)}) collective-permute-start(bf16[384,256]{1,0:T(8,128)(2,1)S(1)} %get-tuple-element.80), channel_id=1, source_target_pairs={{0,2},{1,3},{2,0},{3,1},{4,6},{5,7},{6,4},{7,5},{8,10},{9,11},{10,... | collective-permute-start | bytes 589832 | tf_op jit(solution)/shard_map/ppermute | solution.py:38
  53.4 1.6 %collective-permute-start.17 = (bf16[144,512]{1,0:T(8,128)(2,1)S(1)}, bf16[144,512]{1,0:T(8,128)(2,1)S(1)}, u32[]{:S(2)}, u32[]{:S(2)}) collective-permute-start(bf16[144,512]{1,0:T(8,128)(2,1)S(1)} %get-tuple-element.90), channel_id=1, source_target_pairs={{0,1},{1,0},{2,3},{3,2},{4,5},{5,4},{6,7},{7,6},{8,9},{9,8},{10,11... | collective-permute-start | bytes 442376 | tf_op jit(solution)/shard_map/ppermute | solution.py:38
  53.5 1.5 %collective-permute-start.16 = (bf16[128,512]{1,0:T(8,128)(2,1)S(1)}, bf16[128,512]{1,0:T(8,128)(2,1)S(1)}, u32[]{:S(2)}, u32[]{:S(2)}) collective-permute-start(bf16[128,512]{1,0:T(8,128)(2,1)S(1)} %get-tuple-element.89), channel_id=1, source_target_pairs={{0,1},{1,0},{2,3},{3,2},{4,5},{5,4},{6,7},{7,6},{8,9},{9,8},{10,11... | collective-permute-start | bytes 393224 | tf_op jit(solution)/shard_map/ppermute | solution.py:38
  55.2 8.8 %collective-permute-start.19 = (bf16[256,256]{1,0:T(8,128)(2,1)S(1)}, bf16[256,256]{1,0:T(8,128)(2,1)S(1)}, u32[]{:S(2)}, u32[]{:S(2)}) collective-permute-start(bf16[256,256]{1,0:T(8,128)(2,1)S(1)} %get-tuple-element.95), channel_id=1, source_target_pairs={{0,2},{1,3},{2,0},{3,1},{4,6},{5,7},{6,4},{7,5},{8,10},{9,11},{10,... | collective-permute-start | bytes 393224 | tf_op jit(solution)/shard_map/ppermute | solution.py:38
  57.8 6.1 %collective-permute-start.20 = (bf16[208,256]{1,0:T(8,128)(2,1)S(1)}, bf16[208,256]{1,0:T(8,128)(2,1)S(1)}, u32[]{:S(2)}, u32[]{:S(2)}) collective-permute-start(bf16[208,256]{1,0:T(8,128)(2,1)S(1)} %get-tuple-element.96), channel_id=1, source_target_pairs={{0,2},{1,3},{2,0},{3,1},{4,6},{5,7},{6,4},{7,5},{8,10},{9,11},{10,... | collective-permute-start | bytes 319496 | tf_op jit(solution)/shard_map/ppermute | solution.py:38

commit v5 on v4

--- a/solution.py
+++ b/solution.py
@@ -102,7 +102,6 @@
 
 EARLY = sorted((block for block in ORDER if stage_of(block) < 3), key=lambda block: stage_of(block) > 1)
 LATE = [block for block in ORDER if stage_of(block) == 3]
-FIRST = 3
 
 
 def place_here():
@@ -234,13 +233,9 @@
             at += SHARD
 
 
-def first_kernel(keep0, keep1, got0, got1, mine_ref, send_ref):
-    add_blocks(EARLY[:FIRST], (keep0, keep1), (got0, got1), mine_ref, send_ref)
-
-
 def early_kernel(*refs):
     keeps, gots = refs[: len(STAGES) - 1], refs[len(STAGES) - 1 : -2]
-    add_blocks(EARLY[FIRST:], keeps, gots, *refs[-2:])
+    add_blocks(EARLY, keeps, gots, *refs[-2:])
 
 
 def late_kernel(*refs):
@@ -267,10 +262,8 @@
     return rows[at : at + 1] + (rows[at + 1 : at + 2] + rows[at + 2 : at + 3])
 
 
-def merge_kernel(mine0, mine1, got0, got1, all_ref):
-    rows = FIRST * BLOCK
-    all_ref[:rows, :] = mine0[...] + got0[...].astype(jnp.float32)
-    all_ref[rows:, :] = mine1[...] + got1[...].astype(jnp.float32)
+def merge_kernel(mine0, got0, all_ref):
+    all_ref[...] = mine0[...] + got0[...].astype(jnp.float32)
 
 
 def finish_kernel(early_ref, mine1, got1, got2, lanes_ref, train_ref, out_ref, scale_ref, sums_ref, sem):
@@ -350,17 +343,11 @@
         [turned, precond, *pieces],
     )
     sums.append(squares)
-    first = FIRST * BLOCK
     early = len(EARLY) * BLOCK
     late = len(LATE) * BLOCK
-    mine_first, send = call(first_kernel, [((first, 256), f32), ((first, 256), bf16)], [*keeps, *gots])
-    got_first = across(send, 2)
-    rounded, _ = together(rounded, send)
     keeps.append(call(kept_kernel, [((rows, 512), f32)], [turned, rounded])[0])
     gots += [across(send_low, 1), across(send_high, 1)]
-    mine0, send = call(
-        early_kernel, [((early - first, 256), f32), ((early - first, 256), bf16)], [*keeps, *gots]
-    )
+    mine0, send = call(early_kernel, [((early, 256), f32), ((early, 256), bf16)], [*keeps, *gots])
     got0 = across(send, 2)
     low, high, _ = together(*last, send)
     rows = STAGE_ROWS[-1]
@@ -371,7 +358,6 @@
         scratch=[pltpu.VMEM((rows, 128), f32), pltpu.VMEM((1024, 128), f32)],
     )
     keeps.append(call(kept_kernel, [((rows, 512), f32)], [turned, rounded])[0])
-    send_low, send_high, got_first = together(send_low, send_high, got_first)
     gots += [across(send_low, 1), across(send_high, 1)]
     mine1, send_low, send_high, lanes, train = call(
         late_kernel,
@@ -384,9 +370,8 @@
         ],
         [*keeps, *gots, lanes, train_sums],
     )
-    send_high, got0 = together(send_high, got0)
     got1, got2 = across(send_low, 2), across(send_high, 2)
-    merged = call(merge_kernel, [((early, 256), f32)], [mine_first, mine0, got_first, got0])[0]
+    merged = call(merge_kernel, [((early, 256), f32)], [mine0, got0])[0]
     return call(
         finish_kernel,
         [((1024, 256), f32)],

time: 65.7 us -> 65.4 us (level)
  starting transfers between devices: 34.4 us -> 31.8 us
  waiting for transfers between devices: 18.1 us -> 19.8 us
    ppermute x10 -> x9, starting transfers between devices: 7.91 us -> 5.27 us  [across(): return lax.ppermute(value, 'feat', [(f, f ^ mask) for f in range(4)])]
    ppermute x10 -> x9, waiting for transfers between devices: 5.1 us -> 7.56 us  [across(): return lax.ppermute(value, 'feat', [(f, f ^ mask) for f in range(4)])]
    ppermute x11, waiting for transfers between devices: 13 us -> 12.3 us  [shift(): return lax.ppermute(value, ('rows', 'feat'), pairs)]
    pallas_call x13 -> x12, Pallas kernels: 9.3 us -> 9.3 us  [call(): pl.pallas_call(kernel, out_shape=[jax.ShapeDtypeStruct(s, d) for s, d in...]
  transfers between devices with their start and end apart: 21 -> 20, of which waited for: 11 -> 12; matrix products, arithmetic and copies ran while one was open for 0% -> 0% of each run, Pallas kernels for 12% -> 13%
where the time goes in v5:
time: 65.4 us; the launch traced here: 64.4 us
  starting transfers between devices  31.8 us (49%)
  waiting for transfers between devices  19.8 us (30%)
  Pallas kernels  9.3 us (14%)
  local copies, waits for them, and re-layouts  3.06 us (5%)
    ppermute x11, starting transfers between devices, shift(): return lax.ppermute(value, ('rows', 'feat'), pairs)  26.5 us
    ppermute x11, waiting for transfers between devices, shift(): return lax.ppermute(value, ('rows', 'feat'), pairs)  12.3 us
    pallas_call x12, Pallas kernels, call(): pl.pallas_call(kernel, out_shape=[jax.ShapeDtypeStruct(s, d) for s, d in...  9.3 us
    ppermute x9, waiting for transfers between devices, across(): return lax.ppermute(value, 'feat', [(f, f ^ mask) for f in range(4)])  7.56 us
    ppermute x9, starting transfers between devices, across(): return lax.ppermute(value, 'feat', [(f, f ^ mask) for f in range(4)])  5.27 us
    unnamed x6, local copies, waits for them, and re-layouts  3.06 us
  transfers between devices with their start and end apart: 20, of which 12 were waited for; matrix products, arithmetic and copies ran while one was open for 0% of the time, Pallas kernels for 13%

profile of v5, /device:TPU:8, one launch (start us, length us, event | category | flops | bytes accessed | tf_op | source)
XLA Modules:
  0.0 64.4 jit_solution(2217931129997461508)
XLA Ops:
  0.0 7.2 %collective-permute-start = (bf16[16,2048]{1,0:T(8,128)(2,1)}, bf16[16,2048]{1,0:T(8,128)(2,1)S(1)}, u32[]{:S(2)}, u32[]{:S(2)}) collective-permute-start(bf16[16,2048]{1,0:T(8,128)(2,1)} %from_ref.1), channel_id=1, source_target_pairs={{0,128},{1,129},{2,130},{3,131},{4,132},{5,133},{6,134},{7,135},{8... | collective-permute-start | bytes 196616 | tf_op jit(solution)/shard_map/ppermute | solution.py:34
  7.2 0.9 %copy-done.2 = bf16[16,2048]{1,0:T(8,128)(2,1)S(1)} copy-done((bf16[16,2048]{1,0:T(8,128)(2,1)S(1)}, bf16[16,2048]{1,0:T(8,128)(2,1)}, u32[]{:S(2)}) %copy-start.2) | copy-done | bytes 65560
  8.1 1.9 %collective-permute-done = bf16[16,2048]{1,0:T(8,128)(2,1)S(1)} collective-permute-done((bf16[16,2048]{1,0:T(8,128)(2,1)}, bf16[16,2048]{1,0:T(8,128)(2,1)S(1)}, u32[]{:S(2)}, u32[]{:S(2)}) %collective-permute-start) | collective-permute-done | bytes 65568 | tf_op jit(solution)/shard_map/ppermute | solution.py:34
  10.0 3.1 %collective-permute-start.1 = (bf16[32,2048]{1,0:T(8,128)(2,1)S(1)}, bf16[32,2048]{1,0:T(8,128)(2,1)S(1)}, u32[]{:S(2)}, u32[]{:S(2)}) collective-permute-start(bf16[32,2048]{1,0:T(8,128)(2,1)S(1)} %pad_maximum_fusion.3), channel_id=1, source_target_pairs={{0,4},{1,5},{2,6},{3,7},{4,0},{5,1},{6,2},{7,3},{8,12},{9,13},{10,... | collective-permute-start | bytes 393224 | tf_op jit(solution)/shard_map/ppermute | solution.py:34
  13.1 3.4 %collective-permute-done.1 = bf16[32,2048]{1,0:T(8,128)(2,1)S(1)} collective-permute-done((bf16[32,2048]{1,0:T(8,128)(2,1)S(1)}, bf16[32,2048]{1,0:T(8,128)(2,1)S(1)}, u32[]{:S(2)}, u32[]{:S(2)}) %collective-permute-start.1) | collective-permute-done | bytes 131104 | tf_op jit(solution)/shard_map/ppermute | solution.py:34
  16.5 1.7 %collective-permute-start.2 = (bf16[64,2048]{1,0:T(8,128)(2,1)S(1)}, bf16[64,2048]{1,0:T(8,128)(2,1)S(1)}, u32[]{:S(2)}, u32[]{:S(2)}) collective-permute-start(bf16[64,2048]{1,0:T(8,128)(2,1)S(1)} %pad_maximum_fusion.2), channel_id=1, source_target_pairs={{0,8},{1,33},{2,10},{3,35},{4,12},{5,37},{6,14},{7,39},{8,16},{9,4... | collective-permute-start | bytes 786440 | tf_op jit(solution)/shard_map/ppermute | solution.py:34
  18.2 1.2 %collective-permute-start.4 = (bf16[64,2048]{1,0:T(8,128)(2,1)S(1)}, bf16[64,2048]{1,0:T(8,128)(2,1)S(1)}, u32[]{:S(2)}, u32[]{:S(2)}) collective-permute-start(bf16[64,2048]{1,0:T(8,128)(2,1)S(1)} %pad_maximum_fusion.2), channel_id=1, source_target_pairs={{0,16},{1,65},{2,18},{3,67},{4,20},{5,69},{6,22},{7,71},{8,24},{9,... | collective-permute-start | bytes 786440 | tf_op jit(solution)/shard_map/ppermute | solution.py:34
  19.4 2.1 %collective-permute-start.3 = (bf16[64,2048]{1,0:T(8,128)(2,1)S(1)}, bf16[64,2048]{1,0:T(8,128)(2,1)S(1)}, u32[]{:S(2)}, u32[]{:S(2)}) collective-permute-start(bf16[64,2048]{1,0:T(8,128)(2,1)S(1)} %pad_maximum_fusion.2), channel_id=1, source_target_pairs={{0,24},{1,225},{2,26},{3,227},{4,28},{5,229},{6,30},{7,231},{8,0},... | collective-permute-start | bytes 786440 | tf_op jit(solution)/shard_map/ppermute | solution.py:34
  21.5 2.2 %copy-done.1 = bf16[1024,2048]{1,0:T(8,128)(2,1)S(1)} copy-done((bf16[1024,2048]{1,0:T(8,128)(2,1)S(1)}, bf16[1024,2048]{1,0:T(8,128)(2,1)}, u32[]{:S(2)}) %copy-start.1) | copy-done | bytes 4194328
  23.7 1.2 %shard_map.38 = (bf16[4,2048,256]{2,1,0:T(8,128)(2,1)S(1)}, f32[4,256]{1,0:T(4,128)S(1)}) custom-call(bf16[1024,2048]{1,0:T(8,128)(2,1)S(1)} %copy-done.1), custom_call_target="tpu_custom_call" | custom-call | flops 1 | bytes 1 | tf_op jit(solution)/shard_map/pallas_call | solution.py:298
  25.0 1.1 %collective-permute-done.4 = bf16[64,2048]{1,0:T(8,128)(2,1)S(1)} collective-permute-done((bf16[64,2048]{1,0:T(8,128)(2,1)S(1)}, bf16[64,2048]{1,0:T(8,128)(2,1)S(1)}, u32[]{:S(2)}, u32[]{:S(2)}) %collective-permute-start.4) | collective-permute-done | bytes 262176 | tf_op jit(solution)/shard_map/ppermute | solution.py:34
  26.2 2.4 %collective-permute-done.3 = bf16[64,2048]{1,0:T(8,128)(2,1)S(1)} collective-permute-done((bf16[64,2048]{1,0:T(8,128)(2,1)S(1)}, bf16[64,2048]{1,0:T(8,128)(2,1)S(1)}, u32[]{:S(2)}, u32[]{:S(2)}) %collective-permute-start.3) | collective-permute-done | bytes 262176 | tf_op jit(solution)/shard_map/ppermute | solution.py:34
  28.6 1.6 %collective-permute-start.5 = (bf16[128,2048]{1,0:T(8,128)(2,1)S(1)}, bf16[128,2048]{1,0:T(8,128)(2,1)S(1)}, u32[]{:S(2)}, u32[]{:S(2)}) collective-permute-start(bf16[128,2048]{1,0:T(8,128)(2,1)S(1)} %pad_maximum_fusion.low), channel_id=1, source_target_pairs={{0,32},{1,9},{2,34},{3,11},{4,36},{5,13},{6,38},{7,15},{8,40},{9,1... | collective-permute-start | bytes 1572872 | tf_op jit(solution)/shard_map/ppermute | solution.py:34
  30.2 2.6 %collective-permute-start.6 = (bf16[128,2048]{1,0:T(8,128)(2,1)S(1)}, bf16[128,2048]{1,0:T(8,128)(2,1)S(1)}, u32[]{:S(2)}, u32[]{:S(2)}) collective-permute-start(bf16[128,2048]{1,0:T(8,128)(2,1)S(1)} %pad_maximum_fusion.1.high), channel_id=1, source_target_pairs={{0,224},{1,25},{2,226},{3,27},{4,228},{5,29},{6,230},{7,31},{8,232... | collective-permute-start | bytes 1572872 | tf_op jit(solution)/shard_map/ppermute | solution.py:34
  32.9 3.5 %collective-permute-start.8 = (bf16[128,2048]{1,0:T(8,128)(2,1)S(1)}, bf16[128,2048]{1,0:T(8,128)(2,1)S(1)}, u32[]{:S(2)}, u32[]{:S(2)}) collective-permute-start(bf16[128,2048]{1,0:T(8,128)(2,1)S(1)} %pad_maximum_fusion.low), channel_id=1, source_target_pairs={{0,224},{1,25},{2,226},{3,27},{4,228},{5,29},{6,230},{7,31},{8,232... | collective-permute-start | bytes 1572872 | tf_op jit(solution)/shard_map/ppermute | solution.py:34
  36.4 1.5 %shard_map.39 = (f32[256,512]{1,0:T(8,128)S(1)}, bf16[256,512]{1,0:T(8,128)(2,1)S(1)}, f32[256,128]{1,0:T(8,128)S(1)}) custom-call(bf16[4,2048,256]{2,1,0:T(8,128)(2,1)S(1)} %get-tuple-element.49.turned_ref, bf16[8,256,256]{2,1,0:T(8,128)(2,1)S(1)} %copy-done, bf16[128,2048]{1,0:T(8,128)(2,1)S(1)} %pad_maximum_fusion.low, ...), custom_call_target="tpu_custom_call" | custom-call | flops 1 | bytes 1 | tf_op jit(solution)/shard_map/pallas_call | solution.py:298
  37.9 2.0 %collective-permute-done.5.low = bf16[128,2048]{1,0:T(8,128)(2,1)S(1)} collective-permute-done((bf16[128,2048]{1,0:T(8,128)(2,1)S(1)}, bf16[128,2048]{1,0:T(8,128)(2,1)S(1)}, u32[]{:S(2)}, u32[]{:S(2)}) %collective-permute-start.5) | collective-permute-done | bytes 524320 | tf_op jit(solution)/shard_map/ppermute | solution.py:34
  39.9 0.0 collective-permute-done.6.high
  39.9 1.1 %collective-permute-start.14 = (bf16[128,2048]{1,0:T(8,128)(2,1)S(1)}, bf16[128,2048]{1,0:T(8,128)(2,1)S(1)}, u32[]{:S(2)}, u32[]{:S(2)}) collective-permute-start(bf16[128,2048]{1,0:T(8,128)(2,1)S(1)} %collective-permute-done.5.low), channel_id=1, source_target_pairs={{0,32},{1,9},{2,34},{3,11},{4,36},{5,13},{6,38},{7,15},{8,40},{9,1... | collective-permute-start | bytes 1572872 | tf_op jit(solution)/shard_map/ppermute | solution.py:34
  41.1 2.4 %collective-permute-start.15 = (bf16[128,2048]{1,0:T(8,128)(2,1)S(1)}, bf16[128,2048]{1,0:T(8,128)(2,1)S(1)}, u32[]{:S(2)}, u32[]{:S(2)}) collective-permute-start(bf16[128,2048]{1,0:T(8,128)(2,1)S(1)} %collective-permute-done.6.high), channel_id=1, source_target_pairs={{0,224},{1,25},{2,226},{3,27},{4,228},{5,29},{6,230},{7,31},{8,232... | collective-permute-start | bytes 1572872 | tf_op jit(solution)/shard_map/ppermute | solution.py:34
  43.4 0.0 collective-permute-start.9
  43.4 1.5 %shard_map.40 = (f32[256,512]{1,0:T(8,128)S(1)}, bf16[256,512]{1,0:T(8,128)(2,1)S(1)}, f32[256,128]{1,0:T(8,128)S(1)}) custom-call(bf16[4,2048,256]{2,1,0:T(8,128)(2,1)S(1)} %get-tuple-element.49.turned_ref, bf16[8,256,256]{2,1,0:T(8,128)(2,1)S(1)} %copy-done, bf16[128,2048]{1,0:T(8,128)(2,1)S(1)} %collective-permute-done.5.low, ...), custom_call_target="tpu_custom_call" | custom-call | flops 1 | bytes 1 | tf_op jit(solution)/shard_map/pallas_call | solution.py:298
  45.0 0.6 collective-permute-done.7.low
  45.5 0.2 collective-permute-start.10
  45.8 0.0 collective-permute-done.9.refs_3_.refs_4_
  45.8 1.0 %shard_map.41 = (bf16[256,2048]{1,0:T(8,128)(2,1)S(1)}, bf16[128,512]{1,0:T(8,128)(2,1)S(1)}, bf16[128,512]{1,0:T(8,128)(2,1)S(1)}, f32[256,128]{1,0:T(8,128)S(1)}) custom-call(bf16[4,2048,256]{2,1,0:T(8,128)(2,1)S(1)} %get-tuple-element.49.turned_ref, bf16[8,256,256]{2,1,0:T(8,128)(2,1)S(1)} %copy-done, bf16[128,2048]{1,0:T(8,128)(2,1)S(1)} %collective-permute-done.7.low, ...), custom_call_target="tpu_custom_call" | custom-call | flops 1 | bytes 1 | tf_op jit(solution)/shard_map/pallas_call | solution.py:298
  46.8 0.4 collective-permute-start.11
  47.2 0.2 collective-permute-start.12
  47.4 0.7 %shard_map.42.refs_2_ = f32[256,512]{1,0:T(8,128)S(1)} custom-call(bf16[4,2048,256]{2,1,0:T(8,128)(2,1)S(1)} %get-tuple-element.49.turned_ref, bf16[256,2048]{1,0:T(8,128)(2,1)S(1)} %get-tuple-element.64.rounded_ref), custom_call_target="tpu_custom_call" | custom-call | flops 1 | bytes 1 | tf_op jit(solution)/shard_map/pallas_call | solution.py:298
  48.1 0.0 collective-permute-done.10.refs_4_.refs_5_
  48.1 0.1 collective-permute-done.11.refs_5_.refs_6_
  48.2 0.3 collective-permute-done.12.refs_6_.refs_7_
  48.5 0.1 shard_map.43
  48.6 1.7 %collective-permute-start.13 = (bf16[576,256]{1,0:T(8,128)(2,1)S(1)}, bf16[576,256]{1,0:T(8,128)(2,1)S(1)}, u32[]{:S(2)}, u32[]{:S(2)}) collective-permute-start(bf16[576,256]{1,0:T(8,128)(2,1)S(1)} %get-tuple-element.69), channel_id=1, source_target_pairs={{0,2},{1,3},{2,0},{3,1},{4,6},{5,7},{6,4},{7,5},{8,10},{9,11},{10,... | collective-permute-start | bytes 884744 | tf_op jit(solution)/shard_map/ppermute | solution.py:38
  50.4 0.8 %collective-permute-done.14.low = bf16[128,2048]{1,0:T(8,128)(2,1)S(1)} collective-permute-done((bf16[128,2048]{1,0:T(8,128)(2,1)S(1)}, bf16[128,2048]{1,0:T(8,128)(2,1)S(1)}, u32[]{:S(2)}, u32[]{:S(2)}) %collective-permute-start.14) | collective-permute-done | bytes 524320 | tf_op jit(solution)/shard_map/ppermute | solution.py:34
  51.2 1.0 %shard_map.45 = (bf16[256,2048]{1,0:T(8,128)(2,1)S(1)}, bf16[128,512]{1,0:T(8,128)(2,1)S(1)}, bf16[144,512]{1,0:T(8,128)(2,1)S(1)}, f32[1,1024]{1,0:T(1,128)S(1)}) custom-call(bf16[4,2048,256]{2,1,0:T(8,128)(2,1)S(1)} %get-tuple-element.49.turned_ref, bf16[8,256,256]{2,1,0:T(8,128)(2,1)S(1)} %copy-done, bf16[128,2048]{1,0:T(8,128)(2,1)S(1)} %collective-permute-done.14.low, ...), custom_call_target="tpu_custom_call" | custom-call | flops 1 | bytes 1 | tf_op jit(solution)/shard_map/pallas_call | solution.py:298
  52.2 0.1 collective-permute-start.17
  52.3 0.5 collective-permute-start.16
  52.8 0.7 %shard_map.46.refs_3_ = f32[256,512]{1,0:T(8,128)S(1)} custom-call(bf16[4,2048,256]{2,1,0:T(8,128)(2,1)S(1)} %get-tuple-element.49.turned_ref, bf16[256,2048]{1,0:T(8,128)(2,1)S(1)} %get-tuple-element.74.rounded_ref), custom_call_target="tpu_custom_call" | custom-call | flops 1 | bytes 1 | tf_op jit(solution)/shard_map/pallas_call | solution.py:298
  53.5 0.3 collective-permute-done.16.refs_8_
  53.8 0.0 collective-permute-done.17.refs_9_
  53.8 0.1 shard_map.47
  54.0 1.6 %collective-permute-start.18 = (bf16[256,256]{1,0:T(8,128)(2,1)S(1)}, bf16[256,256]{1,0:T(8,128)(2,1)S(1)}, u32[]{:S(2)}, u32[]{:S(2)}) collective-permute-start(bf16[256,256]{1,0:T(8,128)(2,1)S(1)} %get-tuple-element.79), channel_id=1, source_target_pairs={{0,2},{1,3},{2,0},{3,1},{4,6},{5,7},{6,4},{7,5},{8,10},{9,11},{10,... | collective-permute-start | bytes 393224 | tf_op jit(solution)/shard_map/ppermute | solution.py:38
  55.5 0.5 collective-permute-start.19
  56.1 2.5 %collective-permute-done.13.got0 = bf16[576,256]{1,0:T(8,128)(2,1)S(1)} collective-permute-done((bf16[576,256]{1,0:T(8,128)(2,1)S(1)}, bf16[576,256]{1,0:T(8,128)(2,1)S(1)}, u32[]{:S(2)}, u32[]{:S(2)}) %collective-permute-start.13) | collective-permute-done | bytes 294944 | tf_op jit(solution)/shard_map/ppermute | solution.py:38
  58.6 0.1 shard_map.44.early_ref
  58.6 4.3 %collective-permute-done.19.got2 = bf16[208,256]{1,0:T(8,128)(2,1)S(1)} collective-permute-done((bf16[208,256]{1,0:T(8,128)(2,1)S(1)}, bf16[208,256]{1,0:T(8,128)(2,1)S(1)}, u32[]{:S(2)}, u32[]{:S(2)}) %collective-permute-start.19) | collective-permute-done | bytes 106528 | tf_op jit(solution)/shard_map/ppermute | solution.py:38
  63.0 1.2 %shard_map.48 = f32[1024,256]{1,0:T(8,128)} custom-call(f32[576,256]{1,0:T(8,128)S(1)} %shard_map.44.early_ref, f32[448,256]{1,0:T(8,128)S(1)} %get-tuple-element.78.mine1, bf16[256,256]{1,0:T(8,128)(2,1)S(1)} %collective-permute-done.18.got1, bf16[208,256]{1,0:T(8,128)(2,1)S(1)} %collective-permute-done.19.got2, f32[1,1024]{1,0:T(1,128)S(1)} %get-tuple-element.81.lanes_ref, ...), custom_call_target="tpu_custom_call" | custom-call | flops 1 | bytes 1 | tf_op jit(solution)/shard_map/pallas_call | solution.py:298
  (14 shorter events, 0.1 us)
Async XLA Ops:
  0.0 36.4 %copy-start = (bf16[8,256,256]{2,1,0:T(8,128)(2,1)S(1)}, bf16[8,256,256]{2,1,0:T(8,128)(2,1)}, u32[]{:S(2)}) copy-start(bf16[8,256,256]{2,1,0:T(8,128)(2,1)} %precond_ref.7) | copy-start | bytes 3145732
  0.0 9.9 %collective-permute-start = (bf16[16,2048]{1,0:T(8,128)(2,1)}, bf16[16,2048]{1,0:T(8,128)(2,1)S(1)}, u32[]{:S(2)}, u32[]{:S(2)}) collective-permute-start(bf16[16,2048]{1,0:T(8,128)(2,1)} %from_ref.1), channel_id=1, source_target_pairs={{0,128},{1,129},{2,130},{3,131},{4,132},{5,133},{6,134},{7,135},{8... | collective-permute-start | bytes 196616 | tf_op jit(solution)/shard_map/ppermute | solution.py:34
  7.2 0.9 %copy-start.2 = (bf16[16,2048]{1,0:T(8,128)(2,1)S(1)}, bf16[16,2048]{1,0:T(8,128)(2,1)}, u32[]{:S(2)}) copy-start(bf16[16,2048]{1,0:T(8,128)(2,1)} %from_ref.1) | copy-start | bytes 196612
  10.0 6.6 %collective-permute-start.1 = (bf16[32,2048]{1,0:T(8,128)(2,1)S(1)}, bf16[32,2048]{1,0:T(8,128)(2,1)S(1)}, u32[]{:S(2)}, u32[]{:S(2)}) collective-permute-start(bf16[32,2048]{1,0:T(8,128)(2,1)S(1)} %pad_maximum_fusion.3), channel_id=1, source_target_pairs={{0,4},{1,5},{2,6},{3,7},{4,0},{5,1},{6,2},{7,3},{8,12},{9,13},{10,... | collective-permute-start | bytes 393224 | tf_op jit(solution)/shard_map/ppermute | solution.py:34
  16.5 8.4 %collective-permute-start.2 = (bf16[64,2048]{1,0:T(8,128)(2,1)S(1)}, bf16[64,2048]{1,0:T(8,128)(2,1)S(1)}, u32[]{:S(2)}, u32[]{:S(2)}) collective-permute-start(bf16[64,2048]{1,0:T(8,128)(2,1)S(1)} %pad_maximum_fusion.2), channel_id=1, source_target_pairs={{0,8},{1,33},{2,10},{3,35},{4,12},{5,37},{6,14},{7,39},{8,16},{9,4... | collective-permute-start | bytes 786440 | tf_op jit(solution)/shard_map/ppermute | solution.py:34
  18.2 8.0 %collective-permute-start.4 = (bf16[64,2048]{1,0:T(8,128)(2,1)S(1)}, bf16[64,2048]{1,0:T(8,128)(2,1)S(1)}, u32[]{:S(2)}, u32[]{:S(2)}) collective-permute-start(bf16[64,2048]{1,0:T(8,128)(2,1)S(1)} %pad_maximum_fusion.2), channel_id=1, source_target_pairs={{0,16},{1,65},{2,18},{3,67},{4,20},{5,69},{6,22},{7,71},{8,24},{9,... | collective-permute-start | bytes 786440 | tf_op jit(solution)/shard_map/ppermute | solution.py:34
  19.4 9.2 %collective-permute-start.3 = (bf16[64,2048]{1,0:T(8,128)(2,1)S(1)}, bf16[64,2048]{1,0:T(8,128)(2,1)S(1)}, u32[]{:S(2)}, u32[]{:S(2)}) collective-permute-start(bf16[64,2048]{1,0:T(8,128)(2,1)S(1)} %pad_maximum_fusion.2), channel_id=1, source_target_pairs={{0,24},{1,225},{2,26},{3,227},{4,28},{5,229},{6,30},{7,231},{8,0},... | collective-permute-start | bytes 786440 | tf_op jit(solution)/shard_map/ppermute | solution.py:34
  21.5 2.2 %copy-start.1 = (bf16[1024,2048]{1,0:T(8,128)(2,1)S(1)}, bf16[1024,2048]{1,0:T(8,128)(2,1)}, u32[]{:S(2)}) copy-start(bf16[1024,2048]{1,0:T(8,128)(2,1)} %train_ref) | copy-start | bytes 12582916
  28.6 11.3 %collective-permute-start.5 = (bf16[128,2048]{1,0:T(8,128)(2,1)S(1)}, bf16[128,2048]{1,0:T(8,128)(2,1)S(1)}, u32[]{:S(2)}, u32[]{:S(2)}) collective-permute-start(bf16[128,2048]{1,0:T(8,128)(2,1)S(1)} %pad_maximum_fusion.low), channel_id=1, source_target_pairs={{0,32},{1,9},{2,34},{3,11},{4,36},{5,13},{6,38},{7,15},{8,40},{9,1... | collective-permute-start | bytes 1572872 | tf_op jit(solution)/shard_map/ppermute | solution.py:34
  30.2 9.7 %collective-permute-start.6 = (bf16[128,2048]{1,0:T(8,128)(2,1)S(1)}, bf16[128,2048]{1,0:T(8,128)(2,1)S(1)}, u32[]{:S(2)}, u32[]{:S(2)}) collective-permute-start(bf16[128,2048]{1,0:T(8,128)(2,1)S(1)} %pad_maximum_fusion.1.high), channel_id=1, source_target_pairs={{0,224},{1,25},{2,226},{3,27},{4,228},{5,29},{6,230},{7,31},{8,232... | collective-permute-start | bytes 1572872 | tf_op jit(solution)/shard_map/ppermute | solution.py:34
  32.9 12.7 %collective-permute-start.7 = (bf16[128,2048]{1,0:T(8,128)(2,1)S(1)}, bf16[128,2048]{1,0:T(8,128)(2,1)S(1)}, u32[]{:S(2)}, u32[]{:S(2)}) collective-permute-start(bf16[128,2048]{1,0:T(8,128)(2,1)S(1)} %pad_maximum_fusion.1.high), channel_id=1, source_target_pairs={{0,32},{1,9},{2,34},{3,11},{4,36},{5,13},{6,38},{7,15},{8,40},{9,1... | collective-permute-start | bytes 1572872 | tf_op jit(solution)/shard_map/ppermute | solution.py:34
  32.9 12.9 %collective-permute-start.8 = (bf16[128,2048]{1,0:T(8,128)(2,1)S(1)}, bf16[128,2048]{1,0:T(8,128)(2,1)S(1)}, u32[]{:S(2)}, u32[]{:S(2)}) collective-permute-start(bf16[128,2048]{1,0:T(8,128)(2,1)S(1)} %pad_maximum_fusion.low), channel_id=1, source_target_pairs={{0,224},{1,25},{2,226},{3,27},{4,228},{5,29},{6,230},{7,31},{8,232... | collective-permute-start | bytes 1572872 | tf_op jit(solution)/shard_map/ppermute | solution.py:34
  39.9 11.2 %collective-permute-start.14 = (bf16[128,2048]{1,0:T(8,128)(2,1)S(1)}, bf16[128,2048]{1,0:T(8,128)(2,1)S(1)}, u32[]{:S(2)}, u32[]{:S(2)}) collective-permute-start(bf16[128,2048]{1,0:T(8,128)(2,1)S(1)} %collective-permute-done.5.low), channel_id=1, source_target_pairs={{0,32},{1,9},{2,34},{3,11},{4,36},{5,13},{6,38},{7,15},{8,40},{9,1... | collective-permute-start | bytes 1572872 | tf_op jit(solution)/shard_map/ppermute | solution.py:34
  41.1 10.1 %collective-permute-start.15 = (bf16[128,2048]{1,0:T(8,128)(2,1)S(1)}, bf16[128,2048]{1,0:T(8,128)(2,1)S(1)}, u32[]{:S(2)}, u32[]{:S(2)}) collective-permute-start(bf16[128,2048]{1,0:T(8,128)(2,1)S(1)} %collective-permute-done.6.high), channel_id=1, source_target_pairs={{0,224},{1,25},{2,226},{3,27},{4,228},{5,29},{6,230},{7,31},{8,232... | collective-permute-start | bytes 1572872 | tf_op jit(solution)/shard_map/ppermute | solution.py:34
  43.4 2.3 %collective-permute-start.9 = (bf16[256,512]{1,0:T(8,128)(2,1)S(1)}, bf16[256,512]{1,0:T(8,128)(2,1)S(1)}, u32[]{:S(2)}, u32[]{:S(2)}) collective-permute-start(bf16[256,512]{1,0:T(8,128)(2,1)S(1)} %get-tuple-element.61), channel_id=1, source_target_pairs={{0,1},{1,0},{2,3},{3,2},{4,5},{5,4},{6,7},{7,6},{8,9},{9,8},{10,11... | collective-permute-start | bytes 786440 | tf_op jit(solution)/shard_map/ppermute | solution.py:38
  45.5 2.6 %collective-permute-start.10 = (bf16[256,512]{1,0:T(8,128)(2,1)S(1)}, bf16[256,512]{1,0:T(8,128)(2,1)S(1)}, u32[]{:S(2)}, u32[]{:S(2)}) collective-permute-start(bf16[256,512]{1,0:T(8,128)(2,1)S(1)} %get-tuple-element.65), channel_id=1, source_target_pairs={{0,1},{1,0},{2,3},{3,2},{4,5},{5,4},{6,7},{7,6},{8,9},{9,8},{10,11... | collective-permute-start | bytes 786440 | tf_op jit(solution)/shard_map/ppermute | solution.py:38
  46.8 1.4 %collective-permute-start.11 = (bf16[128,512]{1,0:T(8,128)(2,1)S(1)}, bf16[128,512]{1,0:T(8,128)(2,1)S(1)}, u32[]{:S(2)}, u32[]{:S(2)}) collective-permute-start(bf16[128,512]{1,0:T(8,128)(2,1)S(1)} %get-tuple-element.66), channel_id=1, source_target_pairs={{0,1},{1,0},{2,3},{3,2},{4,5},{5,4},{6,7},{7,6},{8,9},{9,8},{10,11... | collective-permute-start | bytes 393224 | tf_op jit(solution)/shard_map/ppermute | solution.py:38
  47.2 1.3 %collective-permute-start.12 = (bf16[128,512]{1,0:T(8,128)(2,1)S(1)}, bf16[128,512]{1,0:T(8,128)(2,1)S(1)}, u32[]{:S(2)}, u32[]{:S(2)}) collective-permute-start(bf16[128,512]{1,0:T(8,128)(2,1)S(1)} %get-tuple-element.67), channel_id=1, source_target_pairs={{0,1},{1,0},{2,3},{3,2},{4,5},{5,4},{6,7},{7,6},{8,9},{9,8},{10,11... | collective-permute-start | bytes 393224 | tf_op jit(solution)/shard_map/ppermute | solution.py:38
  48.6 9.9 %collective-permute-start.13 = (bf16[576,256]{1,0:T(8,128)(2,1)S(1)}, bf16[576,256]{1,0:T(8,128)(2,1)S(1)}, u32[]{:S(2)}, u32[]{:S(2)}) collective-permute-start(bf16[576,256]{1,0:T(8,128)(2,1)S(1)} %get-tuple-element.69), channel_id=1, source_target_pairs={{0,2},{1,3},{2,0},{3,1},{4,6},{5,7},{6,4},{7,5},{8,10},{9,11},{10,... | collective-permute-start | bytes 884744 | tf_op jit(solution)/shard_map/ppermute | solution.py:38
  52.2 1.6 %collective-permute-start.17 = (bf16[144,512]{1,0:T(8,128)(2,1)S(1)}, bf16[144,512]{1,0:T(8,128)(2,1)S(1)}, u32[]{:S(2)}, u32[]{:S(2)}) collective-permute-start(bf16[144,512]{1,0:T(8,128)(2,1)S(1)} %get-tuple-element.76), channel_id=1, source_target_pairs={{0,1},{1,0},{2,3},{3,2},{4,5},{5,4},{6,7},{7,6},{8,9},{9,8},{10,11... | collective-permute-start | bytes 442376 | tf_op jit(solution)/shard_map/ppermute | solution.py:38
  52.3 1.5 %collective-permute-start.16 = (bf16[128,512]{1,0:T(8,128)(2,1)S(1)}, bf16[128,512]{1,0:T(8,128)(2,1)S(1)}, u32[]{:S(2)}, u32[]{:S(2)}) collective-permute-start(bf16[128,512]{1,0:T(8,128)(2,1)S(1)} %get-tuple-element.75), channel_id=1, source_target_pairs={{0,1},{1,0},{2,3},{3,2},{4,5},{5,4},{6,7},{7,6},{8,9},{9,8},{10,11... | collective-permute-start | bytes 393224 | tf_op jit(solution)/shard_map/ppermute | solution.py:38
  54.0 9.0 %collective-permute-start.18 = (bf16[256,256]{1,0:T(8,128)(2,1)S(1)}, bf16[256,256]{1,0:T(8,128)(2,1)S(1)}, u32[]{:S(2)}, u32[]{:S(2)}) collective-permute-start(bf16[256,256]{1,0:T(8,128)(2,1)S(1)} %get-tuple-element.79), channel_id=1, source_target_pairs={{0,2},{1,3},{2,0},{3,1},{4,6},{5,7},{6,4},{7,5},{8,10},{9,11},{10,... | collective-permute-start | bytes 393224 | tf_op jit(solution)/shard_map/ppermute | solution.py:38
  55.5 7.4 %collective-permute-start.19 = (bf16[208,256]{1,0:T(8,128)(2,1)S(1)}, bf16[208,256]{1,0:T(8,128)(2,1)S(1)}, u32[]{:S(2)}, u32[]{:S(2)}) collective-permute-start(bf16[208,256]{1,0:T(8,128)(2,1)S(1)} %get-tuple-element.80), channel_id=1, source_target_pairs={{0,2},{1,3},{2,0},{3,1},{4,6},{5,7},{6,4},{7,5},{8,10},{9,11},{10,... | collective-permute-start | bytes 319496 | tf_op jit(solution)/shard_map/ppermute | solution.py:38

commit v6 on v5

--- a/solution.py
+++ b/solution.py
@@ -329,12 +329,13 @@
     prepared, done, *stages, last = gather(query_grads, prepare, product)
     turned, train_sums = prepared
     keep, send, squares = done
-    keeps, gots, sums = [keep], [across(send, 1)], [squares]
+    keeps, sums = [keep], [squares]
     *pieces, _ = together(*stages[0], squares)
-    keep, send, squares = product(pieces, prepared)
+    keep, send1, squares = product(pieces, prepared)
     keeps.append(keep)
-    gots.append(across(send, 1))
     sums.append(squares)
+    send, _ = together(send, squares)
+    gots = [across(send, 1), across(send1, 1)]
     rows = STAGE_ROWS[2]
     *pieces, _, _ = together(*stages[1], squares, gots[0])
     rounded, send_low, send_high, squares = call(

time: 65.4 us -> 65.6 us (level)
  waiting for transfers between devices: 19.8 us -> 20.7 us
    ppermute x9, waiting for transfers between devices: 7.56 us -> 9.26 us  [across(): return lax.ppermute(value, 'feat', [(f, f ^ mask) for f in range(4)])]
    ppermute x11, waiting for transfers between devices: 12.3 us -> 11.4 us  [shift(): return lax.ppermute(value, ('rows', 'feat'), pairs)]
  transfers between devices with their start and end apart: 20 -> 20, of which waited for: 12 -> 12; matrix products, arithmetic and copies ran while one was open for 0% -> 0% of each run, Pallas kernels for 13% -> 12%
where the time goes in v6:
time: 65.6 us; the launch traced here: 65.2 us
  starting transfers between devices  31.8 us (48%)
  waiting for transfers between devices  20.7 us (32%)
  Pallas kernels  9.31 us (14%)
  local copies, waits for them, and re-layouts  3.06 us (5%)
    ppermute x11, starting transfers between devices, shift(): return lax.ppermute(value, ('rows', 'feat'), pairs)  26.5 us
    ppermute x11, waiting for transfers between devices, shift(): return lax.ppermute(value, ('rows', 'feat'), pairs)  11.4 us
    pallas_call x12, Pallas kernels, call(): pl.pallas_call(kernel, out_shape=[jax.ShapeDtypeStruct(s, d) for s, d in...  9.31 us
    ppermute x9, waiting for transfers between devices, across(): return lax.ppermute(value, 'feat', [(f, f ^ mask) for f in range(4)])  9.26 us
    ppermute x9, starting transfers between devices, across(): return lax.ppermute(value, 'feat', [(f, f ^ mask) for f in range(4)])  5.28 us
    unnamed x6, local copies, waits for them, and re-layouts  3.06 us
  transfers between devices with their start and end apart: 20, of which 12 were waited for; matrix products, arithmetic and copies ran while one was open for 0% of the time, Pallas kernels for 12%

profile of v6, /device:TPU:8, one launch (start us, length us, event | category | flops | bytes accessed | tf_op | source)
XLA Modules:
  0.0 65.2 jit_solution(9254313503174956552)
XLA Ops:
  0.0 7.2 %collective-permute-start = (bf16[16,2048]{1,0:T(8,128)(2,1)}, bf16[16,2048]{1,0:T(8,128)(2,1)S(1)}, u32[]{:S(2)}, u32[]{:S(2)}) collective-permute-start(bf16[16,2048]{1,0:T(8,128)(2,1)} %from_ref.1), channel_id=1, source_target_pairs={{0,128},{1,129},{2,130},{3,131},{4,132},{5,133},{6,134},{7,135},{8... | collective-permute-start | bytes 196616 | tf_op jit(solution)/shard_map/ppermute | solution.py:34
  7.2 0.9 %copy-done.2 = bf16[16,2048]{1,0:T(8,128)(2,1)S(1)} copy-done((bf16[16,2048]{1,0:T(8,128)(2,1)S(1)}, bf16[16,2048]{1,0:T(8,128)(2,1)}, u32[]{:S(2)}) %copy-start.2) | copy-done | bytes 65560
  8.1 1.9 %collective-permute-done = bf16[16,2048]{1,0:T(8,128)(2,1)S(1)} collective-permute-done((bf16[16,2048]{1,0:T(8,128)(2,1)}, bf16[16,2048]{1,0:T(8,128)(2,1)S(1)}, u32[]{:S(2)}, u32[]{:S(2)}) %collective-permute-start) | collective-permute-done | bytes 65568 | tf_op jit(solution)/shard_map/ppermute | solution.py:34
  10.0 3.1 %collective-permute-start.1 = (bf16[32,2048]{1,0:T(8,128)(2,1)S(1)}, bf16[32,2048]{1,0:T(8,128)(2,1)S(1)}, u32[]{:S(2)}, u32[]{:S(2)}) collective-permute-start(bf16[32,2048]{1,0:T(8,128)(2,1)S(1)} %pad_maximum_fusion.3), channel_id=1, source_target_pairs={{0,4},{1,5},{2,6},{3,7},{4,0},{5,1},{6,2},{7,3},{8,12},{9,13},{10,... | collective-permute-start | bytes 393224 | tf_op jit(solution)/shard_map/ppermute | solution.py:34
  13.1 3.4 %collective-permute-done.1 = bf16[32,2048]{1,0:T(8,128)(2,1)S(1)} collective-permute-done((bf16[32,2048]{1,0:T(8,128)(2,1)S(1)}, bf16[32,2048]{1,0:T(8,128)(2,1)S(1)}, u32[]{:S(2)}, u32[]{:S(2)}) %collective-permute-start.1) | collective-permute-done | bytes 131104 | tf_op jit(solution)/shard_map/ppermute | solution.py:34
  16.5 1.7 %collective-permute-start.2 = (bf16[64,2048]{1,0:T(8,128)(2,1)S(1)}, bf16[64,2048]{1,0:T(8,128)(2,1)S(1)}, u32[]{:S(2)}, u32[]{:S(2)}) collective-permute-start(bf16[64,2048]{1,0:T(8,128)(2,1)S(1)} %pad_maximum_fusion.2), channel_id=1, source_target_pairs={{0,8},{1,33},{2,10},{3,35},{4,12},{5,37},{6,14},{7,39},{8,16},{9,4... | collective-permute-start | bytes 786440 | tf_op jit(solution)/shard_map/ppermute | solution.py:34
  18.2 1.2 %collective-permute-start.4 = (bf16[64,2048]{1,0:T(8,128)(2,1)S(1)}, bf16[64,2048]{1,0:T(8,128)(2,1)S(1)}, u32[]{:S(2)}, u32[]{:S(2)}) collective-permute-start(bf16[64,2048]{1,0:T(8,128)(2,1)S(1)} %pad_maximum_fusion.2), channel_id=1, source_target_pairs={{0,16},{1,65},{2,18},{3,67},{4,20},{5,69},{6,22},{7,71},{8,24},{9,... | collective-permute-start | bytes 786440 | tf_op jit(solution)/shard_map/ppermute | solution.py:34
  19.4 2.1 %collective-permute-start.3 = (bf16[64,2048]{1,0:T(8,128)(2,1)S(1)}, bf16[64,2048]{1,0:T(8,128)(2,1)S(1)}, u32[]{:S(2)}, u32[]{:S(2)}) collective-permute-start(bf16[64,2048]{1,0:T(8,128)(2,1)S(1)} %pad_maximum_fusion.2), channel_id=1, source_target_pairs={{0,24},{1,225},{2,26},{3,227},{4,28},{5,229},{6,30},{7,231},{8,0},... | collective-permute-start | bytes 786440 | tf_op jit(solution)/shard_map/ppermute | solution.py:34
  21.5 2.2 %copy-done.1 = bf16[1024,2048]{1,0:T(8,128)(2,1)S(1)} copy-done((bf16[1024,2048]{1,0:T(8,128)(2,1)S(1)}, bf16[1024,2048]{1,0:T(8,128)(2,1)}, u32[]{:S(2)}) %copy-start.1) | copy-done | bytes 4194328
  23.7 1.2 %shard_map.38 = (bf16[4,2048,256]{2,1,0:T(8,128)(2,1)S(1)}, f32[4,256]{1,0:T(4,128)S(1)}) custom-call(bf16[1024,2048]{1,0:T(8,128)(2,1)S(1)} %copy-done.1), custom_call_target="tpu_custom_call" | custom-call | flops 1 | bytes 1 | tf_op jit(solution)/shard_map/pallas_call | solution.py:298
  25.0 0.0 collective-permute-done.2
  25.0 1.1 %collective-permute-done.4 = bf16[64,2048]{1,0:T(8,128)(2,1)S(1)} collective-permute-done((bf16[64,2048]{1,0:T(8,128)(2,1)S(1)}, bf16[64,2048]{1,0:T(8,128)(2,1)S(1)}, u32[]{:S(2)}, u32[]{:S(2)}) %collective-permute-start.4) | collective-permute-done | bytes 262176 | tf_op jit(solution)/shard_map/ppermute | solution.py:34
  26.2 2.4 %collective-permute-done.3 = bf16[64,2048]{1,0:T(8,128)(2,1)S(1)} collective-permute-done((bf16[64,2048]{1,0:T(8,128)(2,1)S(1)}, bf16[64,2048]{1,0:T(8,128)(2,1)S(1)}, u32[]{:S(2)}, u32[]{:S(2)}) %collective-permute-start.3) | collective-permute-done | bytes 262176 | tf_op jit(solution)/shard_map/ppermute | solution.py:34
  28.6 1.6 %collective-permute-start.5 = (bf16[128,2048]{1,0:T(8,128)(2,1)S(1)}, bf16[128,2048]{1,0:T(8,128)(2,1)S(1)}, u32[]{:S(2)}, u32[]{:S(2)}) collective-permute-start(bf16[128,2048]{1,0:T(8,128)(2,1)S(1)} %pad_maximum_fusion.low), channel_id=1, source_target_pairs={{0,32},{1,9},{2,34},{3,11},{4,36},{5,13},{6,38},{7,15},{8,40},{9,1... | collective-permute-start | bytes 1572872 | tf_op jit(solution)/shard_map/ppermute | solution.py:34
  30.2 2.6 %collective-permute-start.6 = (bf16[128,2048]{1,0:T(8,128)(2,1)S(1)}, bf16[128,2048]{1,0:T(8,128)(2,1)S(1)}, u32[]{:S(2)}, u32[]{:S(2)}) collective-permute-start(bf16[128,2048]{1,0:T(8,128)(2,1)S(1)} %pad_maximum_fusion.1.high), channel_id=1, source_target_pairs={{0,224},{1,25},{2,226},{3,27},{4,228},{5,29},{6,230},{7,31},{8,232... | collective-permute-start | bytes 1572872 | tf_op jit(solution)/shard_map/ppermute | solution.py:34
  32.9 0.0 collective-permute-start.7
  32.9 3.5 %collective-permute-start.8 = (bf16[128,2048]{1,0:T(8,128)(2,1)S(1)}, bf16[128,2048]{1,0:T(8,128)(2,1)S(1)}, u32[]{:S(2)}, u32[]{:S(2)}) collective-permute-start(bf16[128,2048]{1,0:T(8,128)(2,1)S(1)} %pad_maximum_fusion.low), channel_id=1, source_target_pairs={{0,224},{1,25},{2,226},{3,27},{4,228},{5,29},{6,230},{7,31},{8,232... | collective-permute-start | bytes 1572872 | tf_op jit(solution)/shard_map/ppermute | solution.py:34
  36.4 1.5 %shard_map.39 = (f32[256,512]{1,0:T(8,128)S(1)}, bf16[256,512]{1,0:T(8,128)(2,1)S(1)}, f32[256,128]{1,0:T(8,128)S(1)}) custom-call(bf16[4,2048,256]{2,1,0:T(8,128)(2,1)S(1)} %get-tuple-element.50.turned_ref, bf16[8,256,256]{2,1,0:T(8,128)(2,1)S(1)} %copy-done, bf16[128,2048]{1,0:T(8,128)(2,1)S(1)} %pad_maximum_fusion.low, ...), custom_call_target="tpu_custom_call" | custom-call | flops 1 | bytes 1 | tf_op jit(solution)/shard_map/pallas_call | solution.py:298
  37.9 2.0 %collective-permute-done.5.low = bf16[128,2048]{1,0:T(8,128)(2,1)S(1)} collective-permute-done((bf16[128,2048]{1,0:T(8,128)(2,1)S(1)}, bf16[128,2048]{1,0:T(8,128)(2,1)S(1)}, u32[]{:S(2)}, u32[]{:S(2)}) %collective-permute-start.5) | collective-permute-done | bytes 524320 | tf_op jit(solution)/shard_map/ppermute | solution.py:34
  39.9 1.1 %collective-permute-start.14 = (bf16[128,2048]{1,0:T(8,128)(2,1)S(1)}, bf16[128,2048]{1,0:T(8,128)(2,1)S(1)}, u32[]{:S(2)}, u32[]{:S(2)}) collective-permute-start(bf16[128,2048]{1,0:T(8,128)(2,1)S(1)} %collective-permute-done.5.low), channel_id=1, source_target_pairs={{0,32},{1,9},{2,34},{3,11},{4,36},{5,13},{6,38},{7,15},{8,40},{9,1... | collective-permute-start | bytes 1572872 | tf_op jit(solution)/shard_map/ppermute | solution.py:34
  41.1 2.4 %collective-permute-start.15 = (bf16[128,2048]{1,0:T(8,128)(2,1)S(1)}, bf16[128,2048]{1,0:T(8,128)(2,1)S(1)}, u32[]{:S(2)}, u32[]{:S(2)}) collective-permute-start(bf16[128,2048]{1,0:T(8,128)(2,1)S(1)} %collective-permute-done.6.high), channel_id=1, source_target_pairs={{0,224},{1,25},{2,226},{3,27},{4,228},{5,29},{6,230},{7,31},{8,232... | collective-permute-start | bytes 1572872 | tf_op jit(solution)/shard_map/ppermute | solution.py:34
  43.4 1.5 %shard_map.40 = (f32[256,512]{1,0:T(8,128)S(1)}, bf16[256,512]{1,0:T(8,128)(2,1)S(1)}, f32[256,128]{1,0:T(8,128)S(1)}) custom-call(bf16[4,2048,256]{2,1,0:T(8,128)(2,1)S(1)} %get-tuple-element.50.turned_ref, bf16[8,256,256]{2,1,0:T(8,128)(2,1)S(1)} %copy-done, bf16[128,2048]{1,0:T(8,128)(2,1)S(1)} %collective-permute-done.5.low, ...), custom_call_target="tpu_custom_call" | custom-call | flops 1 | bytes 1 | tf_op jit(solution)/shard_map/pallas_call | solution.py:298
  45.0 0.1 collective-permute-start.9
  45.1 0.5 collective-permute-done.7.low
  45.5 0.0 collective-permute-start.10
  45.6 1.0 %collective-permute-done.9.refs_3_.refs_4_ = bf16[256,512]{1,0:T(8,128)(2,1)S(1)} collective-permute-done((bf16[256,512]{1,0:T(8,128)(2,1)S(1)}, bf16[256,512]{1,0:T(8,128)(2,1)S(1)}, u32[]{:S(2)}, u32[]{:S(2)}) %collective-permute-start.9) | collective-permute-done | bytes 262176 | tf_op jit(solution)/shard_map/ppermute | solution.py:38
  46.6 1.0 %shard_map.41 = (bf16[256,2048]{1,0:T(8,128)(2,1)S(1)}, bf16[128,512]{1,0:T(8,128)(2,1)S(1)}, bf16[128,512]{1,0:T(8,128)(2,1)S(1)}, f32[256,128]{1,0:T(8,128)S(1)}) custom-call(bf16[4,2048,256]{2,1,0:T(8,128)(2,1)S(1)} %get-tuple-element.50.turned_ref, bf16[8,256,256]{2,1,0:T(8,128)(2,1)S(1)} %copy-done, bf16[128,2048]{1,0:T(8,128)(2,1)S(1)} %collective-permute-done.7.low, ...), custom_call_target="tpu_custom_call" | custom-call | flops 1 | bytes 1 | tf_op jit(solution)/shard_map/pallas_call | solution.py:298
  47.6 0.2 collective-permute-start.11
  47.8 0.4 collective-permute-start.12
  48.2 0.7 %shard_map.42.refs_2_ = f32[256,512]{1,0:T(8,128)S(1)} custom-call(bf16[4,2048,256]{2,1,0:T(8,128)(2,1)S(1)} %get-tuple-element.50.turned_ref, bf16[256,2048]{1,0:T(8,128)(2,1)S(1)} %get-tuple-element.66.rounded_ref), custom_call_target="tpu_custom_call" | custom-call | flops 1 | bytes 1 | tf_op jit(solution)/shard_map/pallas_call | solution.py:298
  48.9 0.0 collective-permute-done.10.refs_4_.refs_5_
  48.9 0.1 collective-permute-done.11.refs_5_.refs_6_
  49.0 0.2 collective-permute-done.12.refs_6_.refs_7_
  49.2 0.1 shard_map.43
  49.3 1.8 %collective-permute-start.13 = (bf16[576,256]{1,0:T(8,128)(2,1)S(1)}, bf16[576,256]{1,0:T(8,128)(2,1)S(1)}, u32[]{:S(2)}, u32[]{:S(2)}) collective-permute-start(bf16[576,256]{1,0:T(8,128)(2,1)S(1)} %get-tuple-element.71), channel_id=1, source_target_pairs={{0,2},{1,3},{2,0},{3,1},{4,6},{5,7},{6,4},{7,5},{8,10},{9,11},{10,... | collective-permute-start | bytes 884744 | tf_op jit(solution)/shard_map/ppermute | solution.py:38
  51.2 0.0 collective-permute-done.15.high
  51.2 1.0 %shard_map.45 = (bf16[256,2048]{1,0:T(8,128)(2,1)S(1)}, bf16[128,512]{1,0:T(8,128)(2,1)S(1)}, bf16[144,512]{1,0:T(8,128)(2,1)S(1)}, f32[1,1024]{1,0:T(1,128)S(1)}) custom-call(bf16[4,2048,256]{2,1,0:T(8,128)(2,1)S(1)} %get-tuple-element.50.turned_ref, bf16[8,256,256]{2,1,0:T(8,128)(2,1)S(1)} %copy-done, bf16[128,2048]{1,0:T(8,128)(2,1)S(1)} %collective-permute-done.14.low, ...), custom_call_target="tpu_custom_call" | custom-call | flops 1 | bytes 1 | tf_op jit(solution)/shard_map/pallas_call | solution.py:298
  52.2 0.1 collective-permute-start.17
  52.3 0.5 collective-permute-start.16
  52.8 0.7 %shard_map.46.refs_3_ = f32[256,512]{1,0:T(8,128)S(1)} custom-call(bf16[4,2048,256]{2,1,0:T(8,128)(2,1)S(1)} %get-tuple-element.50.turned_ref, bf16[256,2048]{1,0:T(8,128)(2,1)S(1)} %get-tuple-element.76.rounded_ref), custom_call_target="tpu_custom_call" | custom-call | flops 1 | bytes 1 | tf_op jit(solution)/shard_map/pallas_call | solution.py:298
  53.5 0.3 collective-permute-done.16.refs_8_
  53.9 0.1 shard_map.47
  54.0 1.5 %collective-permute-start.18 = (bf16[256,256]{1,0:T(8,128)(2,1)S(1)}, bf16[256,256]{1,0:T(8,128)(2,1)S(1)}, u32[]{:S(2)}, u32[]{:S(2)}) collective-permute-start(bf16[256,256]{1,0:T(8,128)(2,1)S(1)} %get-tuple-element.81), channel_id=1, source_target_pairs={{0,2},{1,3},{2,0},{3,1},{4,6},{5,7},{6,4},{7,5},{8,10},{9,11},{10,... | collective-permute-start | bytes 393224 | tf_op jit(solution)/shard_map/ppermute | solution.py:38
  55.5 0.6 collective-permute-start.19
  56.1 3.1 %collective-permute-done.13.got0 = bf16[576,256]{1,0:T(8,128)(2,1)S(1)} collective-permute-done((bf16[576,256]{1,0:T(8,128)(2,1)S(1)}, bf16[576,256]{1,0:T(8,128)(2,1)S(1)}, u32[]{:S(2)}, u32[]{:S(2)}) %collective-permute-start.13) | collective-permute-done | bytes 294944 | tf_op jit(solution)/shard_map/ppermute | solution.py:38
  59.3 0.1 shard_map.44.early_ref
  59.3 4.5 %collective-permute-done.19.got2 = bf16[208,256]{1,0:T(8,128)(2,1)S(1)} collective-permute-done((bf16[208,256]{1,0:T(8,128)(2,1)S(1)}, bf16[208,256]{1,0:T(8,128)(2,1)S(1)}, u32[]{:S(2)}, u32[]{:S(2)}) %collective-permute-start.19) | collective-permute-done | bytes 106528 | tf_op jit(solution)/shard_map/ppermute | solution.py:38
  63.8 1.2 %shard_map.48 = f32[1024,256]{1,0:T(8,128)} custom-call(f32[576,256]{1,0:T(8,128)S(1)} %shard_map.44.early_ref, f32[448,256]{1,0:T(8,128)S(1)} %get-tuple-element.80.mine1, bf16[256,256]{1,0:T(8,128)(2,1)S(1)} %collective-permute-done.18.got1, bf16[208,256]{1,0:T(8,128)(2,1)S(1)} %collective-permute-done.19.got2, f32[1,1024]{1,0:T(1,128)S(1)} %get-tuple-element.83.lanes_ref, ...), custom_call_target="tpu_custom_call" | custom-call | flops 1 | bytes 1 | tf_op jit(solution)/shard_map/pallas_call | solution.py:298
  (14 shorter events, 0.1 us)
Async XLA Ops:
  0.0 36.4 %copy-start = (bf16[8,256,256]{2,1,0:T(8,128)(2,1)S(1)}, bf16[8,256,256]{2,1,0:T(8,128)(2,1)}, u32[]{:S(2)}) copy-start(bf16[8,256,256]{2,1,0:T(8,128)(2,1)} %precond_ref.7) | copy-start | bytes 3145732
  0.0 9.9 %collective-permute-start = (bf16[16,2048]{1,0:T(8,128)(2,1)}, bf16[16,2048]{1,0:T(8,128)(2,1)S(1)}, u32[]{:S(2)}, u32[]{:S(2)}) collective-permute-start(bf16[16,2048]{1,0:T(8,128)(2,1)} %from_ref.1), channel_id=1, source_target_pairs={{0,128},{1,129},{2,130},{3,131},{4,132},{5,133},{6,134},{7,135},{8... | collective-permute-start | bytes 196616 | tf_op jit(solution)/shard_map/ppermute | solution.py:34
  7.2 0.9 %copy-start.2 = (bf16[16,2048]{1,0:T(8,128)(2,1)S(1)}, bf16[16,2048]{1,0:T(8,128)(2,1)}, u32[]{:S(2)}) copy-start(bf16[16,2048]{1,0:T(8,128)(2,1)} %from_ref.1) | copy-start | bytes 196612
  10.0 6.6 %collective-permute-start.1 = (bf16[32,2048]{1,0:T(8,128)(2,1)S(1)}, bf16[32,2048]{1,0:T(8,128)(2,1)S(1)}, u32[]{:S(2)}, u32[]{:S(2)}) collective-permute-start(bf16[32,2048]{1,0:T(8,128)(2,1)S(1)} %pad_maximum_fusion.3), channel_id=1, source_target_pairs={{0,4},{1,5},{2,6},{3,7},{4,0},{5,1},{6,2},{7,3},{8,12},{9,13},{10,... | collective-permute-start | bytes 393224 | tf_op jit(solution)/shard_map/ppermute | solution.py:34
  16.5 8.4 %collective-permute-start.2 = (bf16[64,2048]{1,0:T(8,128)(2,1)S(1)}, bf16[64,2048]{1,0:T(8,128)(2,1)S(1)}, u32[]{:S(2)}, u32[]{:S(2)}) collective-permute-start(bf16[64,2048]{1,0:T(8,128)(2,1)S(1)} %pad_maximum_fusion.2), channel_id=1, source_target_pairs={{0,8},{1,33},{2,10},{3,35},{4,12},{5,37},{6,14},{7,39},{8,16},{9,4... | collective-permute-start | bytes 786440 | tf_op jit(solution)/shard_map/ppermute | solution.py:34
  18.2 8.0 %collective-permute-start.4 = (bf16[64,2048]{1,0:T(8,128)(2,1)S(1)}, bf16[64,2048]{1,0:T(8,128)(2,1)S(1)}, u32[]{:S(2)}, u32[]{:S(2)}) collective-permute-start(bf16[64,2048]{1,0:T(8,128)(2,1)S(1)} %pad_maximum_fusion.2), channel_id=1, source_target_pairs={{0,16},{1,65},{2,18},{3,67},{4,20},{5,69},{6,22},{7,71},{8,24},{9,... | collective-permute-start | bytes 786440 | tf_op jit(solution)/shard_map/ppermute | solution.py:34
  19.4 9.2 %collective-permute-start.3 = (bf16[64,2048]{1,0:T(8,128)(2,1)S(1)}, bf16[64,2048]{1,0:T(8,128)(2,1)S(1)}, u32[]{:S(2)}, u32[]{:S(2)}) collective-permute-start(bf16[64,2048]{1,0:T(8,128)(2,1)S(1)} %pad_maximum_fusion.2), channel_id=1, source_target_pairs={{0,24},{1,225},{2,26},{3,227},{4,28},{5,229},{6,30},{7,231},{8,0},... | collective-permute-start | bytes 786440 | tf_op jit(solution)/shard_map/ppermute | solution.py:34
  21.5 2.2 %copy-start.1 = (bf16[1024,2048]{1,0:T(8,128)(2,1)S(1)}, bf16[1024,2048]{1,0:T(8,128)(2,1)}, u32[]{:S(2)}) copy-start(bf16[1024,2048]{1,0:T(8,128)(2,1)} %train_ref) | copy-start | bytes 12582916
  28.6 11.3 %collective-permute-start.5 = (bf16[128,2048]{1,0:T(8,128)(2,1)S(1)}, bf16[128,2048]{1,0:T(8,128)(2,1)S(1)}, u32[]{:S(2)}, u32[]{:S(2)}) collective-permute-start(bf16[128,2048]{1,0:T(8,128)(2,1)S(1)} %pad_maximum_fusion.low), channel_id=1, source_target_pairs={{0,32},{1,9},{2,34},{3,11},{4,36},{5,13},{6,38},{7,15},{8,40},{9,1... | collective-permute-start | bytes 1572872 | tf_op jit(solution)/shard_map/ppermute | solution.py:34
  30.2 9.7 %collective-permute-start.6 = (bf16[128,2048]{1,0:T(8,128)(2,1)S(1)}, bf16[128,2048]{1,0:T(8,128)(2,1)S(1)}, u32[]{:S(2)}, u32[]{:S(2)}) collective-permute-start(bf16[128,2048]{1,0:T(8,128)(2,1)S(1)} %pad_maximum_fusion.1.high), channel_id=1, source_target_pairs={{0,224},{1,25},{2,226},{3,27},{4,228},{5,29},{6,230},{7,31},{8,232... | collective-permute-start | bytes 1572872 | tf_op jit(solution)/shard_map/ppermute | solution.py:34
  32.9 12.7 %collective-permute-start.7 = (bf16[128,2048]{1,0:T(8,128)(2,1)S(1)}, bf16[128,2048]{1,0:T(8,128)(2,1)S(1)}, u32[]{:S(2)}, u32[]{:S(2)}) collective-permute-start(bf16[128,2048]{1,0:T(8,128)(2,1)S(1)} %pad_maximum_fusion.1.high), channel_id=1, source_target_pairs={{0,32},{1,9},{2,34},{3,11},{4,36},{5,13},{6,38},{7,15},{8,40},{9,1... | collective-permute-start | bytes 1572872 | tf_op jit(solution)/shard_map/ppermute | solution.py:34
  32.9 12.7 %collective-permute-start.8 = (bf16[128,2048]{1,0:T(8,128)(2,1)S(1)}, bf16[128,2048]{1,0:T(8,128)(2,1)S(1)}, u32[]{:S(2)}, u32[]{:S(2)}) collective-permute-start(bf16[128,2048]{1,0:T(8,128)(2,1)S(1)} %pad_maximum_fusion.low), channel_id=1, source_target_pairs={{0,224},{1,25},{2,226},{3,27},{4,228},{5,29},{6,230},{7,31},{8,232... | collective-permute-start | bytes 1572872 | tf_op jit(solution)/shard_map/ppermute | solution.py:34
  39.9 11.3 %collective-permute-start.14 = (bf16[128,2048]{1,0:T(8,128)(2,1)S(1)}, bf16[128,2048]{1,0:T(8,128)(2,1)S(1)}, u32[]{:S(2)}, u32[]{:S(2)}) collective-permute-start(bf16[128,2048]{1,0:T(8,128)(2,1)S(1)} %collective-permute-done.5.low), channel_id=1, source_target_pairs={{0,32},{1,9},{2,34},{3,11},{4,36},{5,13},{6,38},{7,15},{8,40},{9,1... | collective-permute-start | bytes 1572872 | tf_op jit(solution)/shard_map/ppermute | solution.py:34
  41.1 10.1 %collective-permute-start.15 = (bf16[128,2048]{1,0:T(8,128)(2,1)S(1)}, bf16[128,2048]{1,0:T(8,128)(2,1)S(1)}, u32[]{:S(2)}, u32[]{:S(2)}) collective-permute-start(bf16[128,2048]{1,0:T(8,128)(2,1)S(1)} %collective-permute-done.6.high), channel_id=1, source_target_pairs={{0,224},{1,25},{2,226},{3,27},{4,228},{5,29},{6,230},{7,31},{8,232... | collective-permute-start | bytes 1572872 | tf_op jit(solution)/shard_map/ppermute | solution.py:34
  45.0 1.6 %collective-permute-start.9 = (bf16[256,512]{1,0:T(8,128)(2,1)S(1)}, bf16[256,512]{1,0:T(8,128)(2,1)S(1)}, u32[]{:S(2)}, u32[]{:S(2)}) collective-permute-start(bf16[256,512]{1,0:T(8,128)(2,1)S(1)} %get-tuple-element.63), channel_id=1, source_target_pairs={{0,1},{1,0},{2,3},{3,2},{4,5},{5,4},{6,7},{7,6},{8,9},{9,8},{10,11... | collective-permute-start | bytes 786440 | tf_op jit(solution)/shard_map/ppermute | solution.py:38
  45.5 3.4 %collective-permute-start.10 = (bf16[256,512]{1,0:T(8,128)(2,1)S(1)}, bf16[256,512]{1,0:T(8,128)(2,1)S(1)}, u32[]{:S(2)}, u32[]{:S(2)}) collective-permute-start(bf16[256,512]{1,0:T(8,128)(2,1)S(1)} %get-tuple-element.67), channel_id=1, source_target_pairs={{0,1},{1,0},{2,3},{3,2},{4,5},{5,4},{6,7},{7,6},{8,9},{9,8},{10,11... | collective-permute-start | bytes 786440 | tf_op jit(solution)/shard_map/ppermute | solution.py:38
  47.6 1.4 %collective-permute-start.11 = (bf16[128,512]{1,0:T(8,128)(2,1)S(1)}, bf16[128,512]{1,0:T(8,128)(2,1)S(1)}, u32[]{:S(2)}, u32[]{:S(2)}) collective-permute-start(bf16[128,512]{1,0:T(8,128)(2,1)S(1)} %get-tuple-element.68), channel_id=1, source_target_pairs={{0,1},{1,0},{2,3},{3,2},{4,5},{5,4},{6,7},{7,6},{8,9},{9,8},{10,11... | collective-permute-start | bytes 393224 | tf_op jit(solution)/shard_map/ppermute | solution.py:38
  47.8 1.4 %collective-permute-start.12 = (bf16[128,512]{1,0:T(8,128)(2,1)S(1)}, bf16[128,512]{1,0:T(8,128)(2,1)S(1)}, u32[]{:S(2)}, u32[]{:S(2)}) collective-permute-start(bf16[128,512]{1,0:T(8,128)(2,1)S(1)} %get-tuple-element.69), channel_id=1, source_target_pairs={{0,1},{1,0},{2,3},{3,2},{4,5},{5,4},{6,7},{7,6},{8,9},{9,8},{10,11... | collective-permute-start | bytes 393224 | tf_op jit(solution)/shard_map/ppermute | solution.py:38
  49.3 9.9 %collective-permute-start.13 = (bf16[576,256]{1,0:T(8,128)(2,1)S(1)}, bf16[576,256]{1,0:T(8,128)(2,1)S(1)}, u32[]{:S(2)}, u32[]{:S(2)}) collective-permute-start(bf16[576,256]{1,0:T(8,128)(2,1)S(1)} %get-tuple-element.71), channel_id=1, source_target_pairs={{0,2},{1,3},{2,0},{3,1},{4,6},{5,7},{6,4},{7,5},{8,10},{9,11},{10,... | collective-permute-start | bytes 884744 | tf_op jit(solution)/shard_map/ppermute | solution.py:38
  52.2 1.6 %collective-permute-start.17 = (bf16[144,512]{1,0:T(8,128)(2,1)S(1)}, bf16[144,512]{1,0:T(8,128)(2,1)S(1)}, u32[]{:S(2)}, u32[]{:S(2)}) collective-permute-start(bf16[144,512]{1,0:T(8,128)(2,1)S(1)} %get-tuple-element.78), channel_id=1, source_target_pairs={{0,1},{1,0},{2,3},{3,2},{4,5},{5,4},{6,7},{7,6},{8,9},{9,8},{10,11... | collective-permute-start | bytes 442376 | tf_op jit(solution)/shard_map/ppermute | solution.py:38
  52.3 1.5 %collective-permute-start.16 = (bf16[128,512]{1,0:T(8,128)(2,1)S(1)}, bf16[128,512]{1,0:T(8,128)(2,1)S(1)}, u32[]{:S(2)}, u32[]{:S(2)}) collective-permute-start(bf16[128,512]{1,0:T(8,128)(2,1)S(1)} %get-tuple-element.77), channel_id=1, source_target_pairs={{0,1},{1,0},{2,3},{3,2},{4,5},{5,4},{6,7},{7,6},{8,9},{9,8},{10,11... | collective-permute-start | bytes 393224 | tf_op jit(solution)/shard_map/ppermute | solution.py:38
  54.0 9.8 %collective-permute-start.18 = (bf16[256,256]{1,0:T(8,128)(2,1)S(1)}, bf16[256,256]{1,0:T(8,128)(2,1)S(1)}, u32[]{:S(2)}, u32[]{:S(2)}) collective-permute-start(bf16[256,256]{1,0:T(8,128)(2,1)S(1)} %get-tuple-element.81), channel_id=1, source_target_pairs={{0,2},{1,3},{2,0},{3,1},{4,6},{5,7},{6,4},{7,5},{8,10},{9,11},{10,... | collective-permute-start | bytes 393224 | tf_op jit(solution)/shard_map/ppermute | solution.py:38
  55.5 8.2 %collective-permute-start.19 = (bf16[208,256]{1,0:T(8,128)(2,1)S(1)}, bf16[208,256]{1,0:T(8,128)(2,1)S(1)}, u32[]{:S(2)}, u32[]{:S(2)}) collective-permute-start(bf16[208,256]{1,0:T(8,128)(2,1)S(1)} %get-tuple-element.82), channel_id=1, source_target_pairs={{0,2},{1,3},{2,0},{3,1},{4,6},{5,7},{6,4},{7,5},{8,10},{9,11},{10,... | collective-permute-start | bytes 319496 | tf_op jit(solution)/shard_map/ppermute | solution.py:38

commit v7 on v6

--- a/solution.py
+++ b/solution.py
@@ -29,7 +29,8 @@
             for x in range(NX):
                 for f in range(4):
                     dz, dy, dx = odd if f % 2 else even
-                    there = row_index(z + dz, y + dy, x + dx)
+                    way = -1 if f % 2 else 1
+                    there = row_index(z + way * dz, y + way * dy, x + dx)
                     pairs.append((row_index(z, y, x) * 4 + f, there * 4 + f))
     return lax.ppermute(value, ("rows", "feat"), pairs)
 
@@ -92,7 +93,7 @@
 
 
 def twin(block):
-    other = (wrap(block[1]), wrap(block[0]))
+    other = (wrap(-block[1]), wrap(-block[0]))
     return next(b for b in ORDER if (wrap(b[0]), wrap(b[1])) == other)
 
 
@@ -110,13 +111,13 @@
 
 
 def depth(core, block):
-    return block[1] if block[0] == block[1] else jnp.where(core == 0, block[1], block[0])
+    return jnp.where(core == 0, block[1], -block[0])
 
 
 def first_rows(place, block):
     z, y, x, core = place[0], place[1], place[2], place[3] & 1
     dz = depth(core, block)
-    dy = depth(1 - core, block)
+    dy = jnp.where(core == 0, block[0], -block[1])
     row = ((z + dz) & (NZ - 1)) * (NY * NX) + ((y + dy) & (NY - 1)) * NX + x
     return [pl.multiple_of((row ^ (NZ // 2 * NY * NX * (part % 2) + part // 2)) * SHARD, SHARD) for part in range(4)]
 
@@ -126,7 +127,7 @@
     stage, start = slot(twin(block))
     each = STAGE_ROWS[stage] // SENDS[stage]
     parts = [start % each + part * SHARD for part in range(4)]
-    if 2 in (block[1], twin(block)[1]):
+    if 2 in map(abs, block + twin(block)):
         away = (((depth(core, block) - depth(1 - core, twin(block))) >> 2) & 1) * SHARD
         parts = [pl.multiple_of(row ^ away, SHARD) for row in parts]
     return sum(SENDS[:stage]) + start // each, parts

time: 65.6 us -> 67.8 us (1.034)
  the two profiles are of different devices: /device:TPU:8 before, /device:TPU:114 now
where the time goes in v7:
time: 67.8 us; the launch traced here: 67.6 us
  waiting for transfers between devices  29.2 us (43%)
  starting transfers between devices  25.7 us (38%)
  Pallas kernels  9.29 us (14%)
  local copies, waits for them, and re-layouts  3.06 us (5%)
    ppermute x11, waiting for transfers between devices, shift(): return lax.ppermute(value, ('rows', 'feat'), pairs)  22.6 us
    ppermute x11, starting transfers between devices, shift(): return lax.ppermute(value, ('rows', 'feat'), pairs)  21.2 us
    pallas_call x12, Pallas kernels, call(): pl.pallas_call(kernel, out_shape=[jax.ShapeDtypeStruct(s, d) for s, d in...  9.29 us
    ppermute x9, waiting for transfers between devices, across(): return lax.ppermute(value, 'feat', [(f, f ^ mask) for f in range(4)])  6.53 us
    ppermute x9, starting transfers between devices, across(): return lax.ppermute(value, 'feat', [(f, f ^ mask) for f in range(4)])  4.49 us
    unnamed x6, local copies, waits for them, and re-layouts  3.06 us
  transfers between devices with their start and end apart: 20, of which 13 were waited for; matrix products, arithmetic and copies ran while one was open for 0% of the time, Pallas kernels for 12%

profile of v7, /device:TPU:114, one launch (start us, length us, event | category | flops | bytes accessed | tf_op | source)
XLA Modules:
  0.0 67.6 jit_solution(6174668701255283520)
XLA Ops:
  0.0 4.5 %collective-permute-start = (bf16[16,2048]{1,0:T(8,128)(2,1)}, bf16[16,2048]{1,0:T(8,128)(2,1)S(1)}, u32[]{:S(2)}, u32[]{:S(2)}) collective-permute-start(bf16[16,2048]{1,0:T(8,128)(2,1)} %from_ref.1), channel_id=1, source_target_pairs={{0,128},{1,129},{2,130},{3,131},{4,132},{5,133},{6,134},{7,135},{8... | collective-permute-start | bytes 196616 | tf_op jit(solution)/shard_map/ppermute | solution.py:35
  4.5 0.9 %copy-done.2 = bf16[16,2048]{1,0:T(8,128)(2,1)S(1)} copy-done((bf16[16,2048]{1,0:T(8,128)(2,1)S(1)}, bf16[16,2048]{1,0:T(8,128)(2,1)}, u32[]{:S(2)}) %copy-start.2) | copy-done | bytes 65560
  5.4 3.0 %collective-permute-done = bf16[16,2048]{1,0:T(8,128)(2,1)S(1)} collective-permute-done((bf16[16,2048]{1,0:T(8,128)(2,1)}, bf16[16,2048]{1,0:T(8,128)(2,1)S(1)}, u32[]{:S(2)}, u32[]{:S(2)}) %collective-permute-start) | collective-permute-done | bytes 65568 | tf_op jit(solution)/shard_map/ppermute | solution.py:35
  8.4 2.2 %collective-permute-start.1 = (bf16[32,2048]{1,0:T(8,128)(2,1)S(1)}, bf16[32,2048]{1,0:T(8,128)(2,1)S(1)}, u32[]{:S(2)}, u32[]{:S(2)}) collective-permute-start(bf16[32,2048]{1,0:T(8,128)(2,1)S(1)} %pad_maximum_fusion.3), channel_id=1, source_target_pairs={{0,4},{1,5},{2,6},{3,7},{4,0},{5,1},{6,2},{7,3},{8,12},{9,13},{10,... | collective-permute-start | bytes 393224 | tf_op jit(solution)/shard_map/ppermute | solution.py:35
  10.6 4.3 %collective-permute-done.1 = bf16[32,2048]{1,0:T(8,128)(2,1)S(1)} collective-permute-done((bf16[32,2048]{1,0:T(8,128)(2,1)S(1)}, bf16[32,2048]{1,0:T(8,128)(2,1)S(1)}, u32[]{:S(2)}, u32[]{:S(2)}) %collective-permute-start.1) | collective-permute-done | bytes 131104 | tf_op jit(solution)/shard_map/ppermute | solution.py:35
  15.0 1.4 %collective-permute-start.2 = (bf16[64,2048]{1,0:T(8,128)(2,1)S(1)}, bf16[64,2048]{1,0:T(8,128)(2,1)S(1)}, u32[]{:S(2)}, u32[]{:S(2)}) collective-permute-start(bf16[64,2048]{1,0:T(8,128)(2,1)S(1)} %pad_maximum_fusion.2), channel_id=1, source_target_pairs={{0,8},{1,225},{2,10},{3,227},{4,12},{5,229},{6,14},{7,231},{8,16},... | collective-permute-start | bytes 786440 | tf_op jit(solution)/shard_map/ppermute | solution.py:35
  16.3 0.6 collective-permute-start.4
  17.0 1.1 %collective-permute-start.3 = (bf16[64,2048]{1,0:T(8,128)(2,1)S(1)}, bf16[64,2048]{1,0:T(8,128)(2,1)S(1)}, u32[]{:S(2)}, u32[]{:S(2)}) collective-permute-start(bf16[64,2048]{1,0:T(8,128)(2,1)S(1)} %pad_maximum_fusion.2), channel_id=1, source_target_pairs={{0,24},{1,33},{2,26},{3,35},{4,28},{5,37},{6,30},{7,39},{8,0},{9,4... | collective-permute-start | bytes 786440 | tf_op jit(solution)/shard_map/ppermute | solution.py:35
  18.0 2.2 %copy-done.1 = bf16[1024,2048]{1,0:T(8,128)(2,1)S(1)} copy-done((bf16[1024,2048]{1,0:T(8,128)(2,1)S(1)}, bf16[1024,2048]{1,0:T(8,128)(2,1)}, u32[]{:S(2)}) %copy-start.1) | copy-done | bytes 4194328
  20.2 1.2 %shard_map.38 = (bf16[4,2048,256]{2,1,0:T(8,128)(2,1)S(1)}, f32[4,256]{1,0:T(4,128)S(1)}) custom-call(bf16[1024,2048]{1,0:T(8,128)(2,1)S(1)} %copy-done.1), custom_call_target="tpu_custom_call" | custom-call | flops 1 | bytes 1 | tf_op jit(solution)/shard_map/pallas_call | solution.py:299
  21.5 0.0 collective-permute-done.2
  21.5 2.7 %collective-permute-done.4 = bf16[64,2048]{1,0:T(8,128)(2,1)S(1)} collective-permute-done((bf16[64,2048]{1,0:T(8,128)(2,1)S(1)}, bf16[64,2048]{1,0:T(8,128)(2,1)S(1)}, u32[]{:S(2)}, u32[]{:S(2)}) %collective-permute-start.4) | collective-permute-done | bytes 262176 | tf_op jit(solution)/shard_map/ppermute | solution.py:35
  24.2 2.1 %collective-permute-done.3 = bf16[64,2048]{1,0:T(8,128)(2,1)S(1)} collective-permute-done((bf16[64,2048]{1,0:T(8,128)(2,1)S(1)}, bf16[64,2048]{1,0:T(8,128)(2,1)S(1)}, u32[]{:S(2)}, u32[]{:S(2)}) %collective-permute-start.3) | collective-permute-done | bytes 262176 | tf_op jit(solution)/shard_map/ppermute | solution.py:35
  26.4 3.8 %collective-permute-start.5 = (bf16[128,2048]{1,0:T(8,128)(2,1)S(1)}, bf16[128,2048]{1,0:T(8,128)(2,1)S(1)}, u32[]{:S(2)}, u32[]{:S(2)}) collective-permute-start(bf16[128,2048]{1,0:T(8,128)(2,1)S(1)} %pad_maximum_fusion.low), channel_id=1, source_target_pairs={{0,32},{1,25},{2,34},{3,27},{4,36},{5,29},{6,38},{7,31},{8,40},{9,... | collective-permute-start | bytes 1572872 | tf_op jit(solution)/shard_map/ppermute | solution.py:35
  30.2 0.0 collective-permute-start.6
  30.2 5.6 %collective-permute-start.7 = (bf16[128,2048]{1,0:T(8,128)(2,1)S(1)}, bf16[128,2048]{1,0:T(8,128)(2,1)S(1)}, u32[]{:S(2)}, u32[]{:S(2)}) collective-permute-start(bf16[128,2048]{1,0:T(8,128)(2,1)S(1)} %pad_maximum_fusion.1.high), channel_id=1, source_target_pairs={{0,32},{1,25},{2,34},{3,27},{4,36},{5,29},{6,38},{7,31},{8,40},{9,... | collective-permute-start | bytes 1572872 | tf_op jit(solution)/shard_map/ppermute | solution.py:35
  35.8 0.0 collective-permute-start.8
  35.8 1.5 %shard_map.39 = (f32[256,512]{1,0:T(8,128)S(1)}, bf16[256,512]{1,0:T(8,128)(2,1)S(1)}, f32[256,128]{1,0:T(8,128)S(1)}) custom-call(bf16[4,2048,256]{2,1,0:T(8,128)(2,1)S(1)} %get-tuple-element.50.turned_ref, bf16[8,256,256]{2,1,0:T(8,128)(2,1)S(1)} %copy-done, bf16[128,2048]{1,0:T(8,128)(2,1)S(1)} %pad_maximum_fusion.low, ...), custom_call_target="tpu_custom_call" | custom-call | flops 1 | bytes 1 | tf_op jit(solution)/shard_map/pallas_call | solution.py:299
  37.4 5.6 %collective-permute-done.6.high = bf16[128,2048]{1,0:T(8,128)(2,1)S(1)} collective-permute-done((bf16[128,2048]{1,0:T(8,128)(2,1)S(1)}, bf16[128,2048]{1,0:T(8,128)(2,1)S(1)}, u32[]{:S(2)}, u32[]{:S(2)}) %collective-permute-start.6) | collective-permute-done | bytes 524320 | tf_op jit(solution)/shard_map/ppermute | solution.py:35
  42.9 2.0 %collective-permute-start.14 = (bf16[128,2048]{1,0:T(8,128)(2,1)S(1)}, bf16[128,2048]{1,0:T(8,128)(2,1)S(1)}, u32[]{:S(2)}, u32[]{:S(2)}) collective-permute-start(bf16[128,2048]{1,0:T(8,128)(2,1)S(1)} %collective-permute-done.5.low), channel_id=1, source_target_pairs={{0,32},{1,25},{2,34},{3,27},{4,36},{5,29},{6,38},{7,31},{8,40},{9,... | collective-permute-start | bytes 1572872 | tf_op jit(solution)/shard_map/ppermute | solution.py:35
  45.0 0.0 collective-permute-start.15
  45.0 1.5 %shard_map.40 = (f32[256,512]{1,0:T(8,128)S(1)}, bf16[256,512]{1,0:T(8,128)(2,1)S(1)}, f32[256,128]{1,0:T(8,128)S(1)}) custom-call(bf16[4,2048,256]{2,1,0:T(8,128)(2,1)S(1)} %get-tuple-element.50.turned_ref, bf16[8,256,256]{2,1,0:T(8,128)(2,1)S(1)} %copy-done, bf16[128,2048]{1,0:T(8,128)(2,1)S(1)} %collective-permute-done.5.low, ...), custom_call_target="tpu_custom_call" | custom-call | flops 1 | bytes 1 | tf_op jit(solution)/shard_map/pallas_call | solution.py:299
  46.5 0.1 collective-permute-start.9
  46.6 0.0 collective-permute-done.7.low
  46.6 0.5 collective-permute-start.10
  47.1 1.4 %collective-permute-done.8.high = bf16[128,2048]{1,0:T(8,128)(2,1)S(1)} collective-permute-done((bf16[128,2048]{1,0:T(8,128)(2,1)S(1)}, bf16[128,2048]{1,0:T(8,128)(2,1)S(1)}, u32[]{:S(2)}, u32[]{:S(2)}) %collective-permute-start.8) | collective-permute-done | bytes 524320 | tf_op jit(solution)/shard_map/ppermute | solution.py:35
  48.6 1.0 %shard_map.41 = (bf16[256,2048]{1,0:T(8,128)(2,1)S(1)}, bf16[128,512]{1,0:T(8,128)(2,1)S(1)}, bf16[128,512]{1,0:T(8,128)(2,1)S(1)}, f32[256,128]{1,0:T(8,128)S(1)}) custom-call(bf16[4,2048,256]{2,1,0:T(8,128)(2,1)S(1)} %get-tuple-element.50.turned_ref, bf16[8,256,256]{2,1,0:T(8,128)(2,1)S(1)} %copy-done, bf16[128,2048]{1,0:T(8,128)(2,1)S(1)} %collective-permute-done.7.low, ...), custom_call_target="tpu_custom_call" | custom-call | flops 1 | bytes 1 | tf_op jit(solution)/shard_map/pallas_call | solution.py:299
  49.6 0.1 collective-permute-start.11
  49.7 0.5 collective-permute-start.12
  50.2 0.7 %shard_map.42.refs_2_ = f32[256,512]{1,0:T(8,128)S(1)} custom-call(bf16[4,2048,256]{2,1,0:T(8,128)(2,1)S(1)} %get-tuple-element.50.turned_ref, bf16[256,2048]{1,0:T(8,128)(2,1)S(1)} %get-tuple-element.66.rounded_ref), custom_call_target="tpu_custom_call" | custom-call | flops 1 | bytes 1 | tf_op jit(solution)/shard_map/pallas_call | solution.py:299
  50.9 0.1 collective-permute-done.11.refs_5_.refs_6_
  51.0 0.2 collective-permute-done.12.refs_6_.refs_7_
  51.2 0.1 shard_map.43
  51.3 0.6 collective-permute-start.13
  51.9 0.2 collective-permute-done.14.low
  52.1 3.2 %collective-permute-done.15.high = bf16[128,2048]{1,0:T(8,128)(2,1)S(1)} collective-permute-done((bf16[128,2048]{1,0:T(8,128)(2,1)S(1)}, bf16[128,2048]{1,0:T(8,128)(2,1)S(1)}, u32[]{:S(2)}, u32[]{:S(2)}) %collective-permute-start.15) | collective-permute-done | bytes 524320 | tf_op jit(solution)/shard_map/ppermute | solution.py:35
  55.4 1.0 %shard_map.45 = (bf16[256,2048]{1,0:T(8,128)(2,1)S(1)}, bf16[128,512]{1,0:T(8,128)(2,1)S(1)}, bf16[144,512]{1,0:T(8,128)(2,1)S(1)}, f32[1,1024]{1,0:T(1,128)S(1)}) custom-call(bf16[4,2048,256]{2,1,0:T(8,128)(2,1)S(1)} %get-tuple-element.50.turned_ref, bf16[8,256,256]{2,1,0:T(8,128)(2,1)S(1)} %copy-done, bf16[128,2048]{1,0:T(8,128)(2,1)S(1)} %collective-permute-done.14.low, ...), custom_call_target="tpu_custom_call" | custom-call | flops 1 | bytes 1 | tf_op jit(solution)/shard_map/pallas_call | solution.py:299
  56.4 0.1 collective-permute-start.17
  56.5 0.5 collective-permute-start.16
  57.0 0.7 %shard_map.46.refs_3_ = f32[256,512]{1,0:T(8,128)S(1)} custom-call(bf16[4,2048,256]{2,1,0:T(8,128)(2,1)S(1)} %get-tuple-element.50.turned_ref, bf16[256,2048]{1,0:T(8,128)(2,1)S(1)} %get-tuple-element.76.rounded_ref), custom_call_target="tpu_custom_call" | custom-call | flops 1 | bytes 1 | tf_op jit(solution)/shard_map/pallas_call | solution.py:299
  57.7 0.3 collective-permute-done.16.refs_8_
  58.0 0.1 shard_map.47
  58.1 0.6 collective-permute-start.18
  58.8 1.5 %collective-permute-start.19 = (bf16[208,256]{1,0:T(8,128)(2,1)S(1)}, bf16[208,256]{1,0:T(8,128)(2,1)S(1)}, u32[]{:S(2)}, u32[]{:S(2)}) collective-permute-start(bf16[208,256]{1,0:T(8,128)(2,1)S(1)} %get-tuple-element.82), channel_id=1, source_target_pairs={{0,2},{1,3},{2,0},{3,1},{4,6},{5,7},{6,4},{7,5},{8,10},{9,11},{10,... | collective-permute-start | bytes 319496 | tf_op jit(solution)/shard_map/ppermute | solution.py:39
  60.3 0.4 collective-permute-done.13.got0
  60.6 0.1 shard_map.44.early_ref
  60.7 5.5 %collective-permute-done.19.got2 = bf16[208,256]{1,0:T(8,128)(2,1)S(1)} collective-permute-done((bf16[208,256]{1,0:T(8,128)(2,1)S(1)}, bf16[208,256]{1,0:T(8,128)(2,1)S(1)}, u32[]{:S(2)}, u32[]{:S(2)}) %collective-permute-start.19) | collective-permute-done | bytes 106528 | tf_op jit(solution)/shard_map/ppermute | solution.py:39
  66.2 1.2 %shard_map.48 = f32[1024,256]{1,0:T(8,128)} custom-call(f32[576,256]{1,0:T(8,128)S(1)} %shard_map.44.early_ref, f32[448,256]{1,0:T(8,128)S(1)} %get-tuple-element.80.mine1, bf16[256,256]{1,0:T(8,128)(2,1)S(1)} %collective-permute-done.18.got1, bf16[208,256]{1,0:T(8,128)(2,1)S(1)} %collective-permute-done.19.got2, f32[1,1024]{1,0:T(1,128)S(1)} %get-tuple-element.83.lanes_ref, ...), custom_call_target="tpu_custom_call" | custom-call | flops 1 | bytes 1 | tf_op jit(solution)/shard_map/pallas_call | solution.py:299
  (14 shorter events, 0.1 us)
Async XLA Ops:
  0.0 35.8 %copy-start = (bf16[8,256,256]{2,1,0:T(8,128)(2,1)S(1)}, bf16[8,256,256]{2,1,0:T(8,128)(2,1)}, u32[]{:S(2)}) copy-start(bf16[8,256,256]{2,1,0:T(8,128)(2,1)} %precond_ref.7) | copy-start | bytes 3145732
  0.0 8.4 %collective-permute-start = (bf16[16,2048]{1,0:T(8,128)(2,1)}, bf16[16,2048]{1,0:T(8,128)(2,1)S(1)}, u32[]{:S(2)}, u32[]{:S(2)}) collective-permute-start(bf16[16,2048]{1,0:T(8,128)(2,1)} %from_ref.1), channel_id=1, source_target_pairs={{0,128},{1,129},{2,130},{3,131},{4,132},{5,133},{6,134},{7,135},{8... | collective-permute-start | bytes 196616 | tf_op jit(solution)/shard_map/ppermute | solution.py:35
  4.5 0.9 %copy-start.2 = (bf16[16,2048]{1,0:T(8,128)(2,1)S(1)}, bf16[16,2048]{1,0:T(8,128)(2,1)}, u32[]{:S(2)}) copy-start(bf16[16,2048]{1,0:T(8,128)(2,1)} %from_ref.1) | copy-start | bytes 196612
  8.4 6.6 %collective-permute-start.1 = (bf16[32,2048]{1,0:T(8,128)(2,1)S(1)}, bf16[32,2048]{1,0:T(8,128)(2,1)S(1)}, u32[]{:S(2)}, u32[]{:S(2)}) collective-permute-start(bf16[32,2048]{1,0:T(8,128)(2,1)S(1)} %pad_maximum_fusion.3), channel_id=1, source_target_pairs={{0,4},{1,5},{2,6},{3,7},{4,0},{5,1},{6,2},{7,3},{8,12},{9,13},{10,... | collective-permute-start | bytes 393224 | tf_op jit(solution)/shard_map/ppermute | solution.py:35
  15.0 6.5 %collective-permute-start.2 = (bf16[64,2048]{1,0:T(8,128)(2,1)S(1)}, bf16[64,2048]{1,0:T(8,128)(2,1)S(1)}, u32[]{:S(2)}, u32[]{:S(2)}) collective-permute-start(bf16[64,2048]{1,0:T(8,128)(2,1)S(1)} %pad_maximum_fusion.2), channel_id=1, source_target_pairs={{0,8},{1,225},{2,10},{3,227},{4,12},{5,229},{6,14},{7,231},{8,16},... | collective-permute-start | bytes 786440 | tf_op jit(solution)/shard_map/ppermute | solution.py:35
  16.3 7.9 %collective-permute-start.4 = (bf16[64,2048]{1,0:T(8,128)(2,1)S(1)}, bf16[64,2048]{1,0:T(8,128)(2,1)S(1)}, u32[]{:S(2)}, u32[]{:S(2)}) collective-permute-start(bf16[64,2048]{1,0:T(8,128)(2,1)S(1)} %pad_maximum_fusion.2), channel_id=1, source_target_pairs={{0,16},{1,193},{2,18},{3,195},{4,20},{5,197},{6,22},{7,199},{8,24}... | collective-permute-start | bytes 786440 | tf_op jit(solution)/shard_map/ppermute | solution.py:35
  17.0 9.4 %collective-permute-start.3 = (bf16[64,2048]{1,0:T(8,128)(2,1)S(1)}, bf16[64,2048]{1,0:T(8,128)(2,1)S(1)}, u32[]{:S(2)}, u32[]{:S(2)}) collective-permute-start(bf16[64,2048]{1,0:T(8,128)(2,1)S(1)} %pad_maximum_fusion.2), channel_id=1, source_target_pairs={{0,24},{1,33},{2,26},{3,35},{4,28},{5,37},{6,30},{7,39},{8,0},{9,4... | collective-permute-start | bytes 786440 | tf_op jit(solution)/shard_map/ppermute | solution.py:35
  18.0 2.2 %copy-start.1 = (bf16[1024,2048]{1,0:T(8,128)(2,1)S(1)}, bf16[1024,2048]{1,0:T(8,128)(2,1)}, u32[]{:S(2)}) copy-start(bf16[1024,2048]{1,0:T(8,128)(2,1)} %train_ref) | copy-start | bytes 12582916
  26.4 11.0 %collective-permute-start.5 = (bf16[128,2048]{1,0:T(8,128)(2,1)S(1)}, bf16[128,2048]{1,0:T(8,128)(2,1)S(1)}, u32[]{:S(2)}, u32[]{:S(2)}) collective-permute-start(bf16[128,2048]{1,0:T(8,128)(2,1)S(1)} %pad_maximum_fusion.low), channel_id=1, source_target_pairs={{0,32},{1,25},{2,34},{3,27},{4,36},{5,29},{6,38},{7,31},{8,40},{9,... | collective-permute-start | bytes 1572872 | tf_op jit(solution)/shard_map/ppermute | solution.py:35
  30.2 12.7 %collective-permute-start.6 = (bf16[128,2048]{1,0:T(8,128)(2,1)S(1)}, bf16[128,2048]{1,0:T(8,128)(2,1)S(1)}, u32[]{:S(2)}, u32[]{:S(2)}) collective-permute-start(bf16[128,2048]{1,0:T(8,128)(2,1)S(1)} %pad_maximum_fusion.1.high), channel_id=1, source_target_pairs={{0,224},{1,9},{2,226},{3,11},{4,228},{5,13},{6,230},{7,15},{8,232}... | collective-permute-start | bytes 1572872 | tf_op jit(solution)/shard_map/ppermute | solution.py:35
  30.2 16.4 %collective-permute-start.7 = (bf16[128,2048]{1,0:T(8,128)(2,1)S(1)}, bf16[128,2048]{1,0:T(8,128)(2,1)S(1)}, u32[]{:S(2)}, u32[]{:S(2)}) collective-permute-start(bf16[128,2048]{1,0:T(8,128)(2,1)S(1)} %pad_maximum_fusion.1.high), channel_id=1, source_target_pairs={{0,32},{1,25},{2,34},{3,27},{4,36},{5,29},{6,38},{7,31},{8,40},{9,... | collective-permute-start | bytes 1572872 | tf_op jit(solution)/shard_map/ppermute | solution.py:35
  35.8 12.8 %collective-permute-start.8 = (bf16[128,2048]{1,0:T(8,128)(2,1)S(1)}, bf16[128,2048]{1,0:T(8,128)(2,1)S(1)}, u32[]{:S(2)}, u32[]{:S(2)}) collective-permute-start(bf16[128,2048]{1,0:T(8,128)(2,1)S(1)} %pad_maximum_fusion.low), channel_id=1, source_target_pairs={{0,224},{1,9},{2,226},{3,11},{4,228},{5,13},{6,230},{7,15},{8,232}... | collective-permute-start | bytes 1572872 | tf_op jit(solution)/shard_map/ppermute | solution.py:35
  42.9 9.2 %collective-permute-start.14 = (bf16[128,2048]{1,0:T(8,128)(2,1)S(1)}, bf16[128,2048]{1,0:T(8,128)(2,1)S(1)}, u32[]{:S(2)}, u32[]{:S(2)}) collective-permute-start(bf16[128,2048]{1,0:T(8,128)(2,1)S(1)} %collective-permute-done.5.low), channel_id=1, source_target_pairs={{0,32},{1,25},{2,34},{3,27},{4,36},{5,29},{6,38},{7,31},{8,40},{9,... | collective-permute-start | bytes 1572872 | tf_op jit(solution)/shard_map/ppermute | solution.py:35
  45.0 10.4 %collective-permute-start.15 = (bf16[128,2048]{1,0:T(8,128)(2,1)S(1)}, bf16[128,2048]{1,0:T(8,128)(2,1)S(1)}, u32[]{:S(2)}, u32[]{:S(2)}) collective-permute-start(bf16[128,2048]{1,0:T(8,128)(2,1)S(1)} %collective-permute-done.6.high), channel_id=1, source_target_pairs={{0,224},{1,9},{2,226},{3,11},{4,228},{5,13},{6,230},{7,15},{8,232}... | collective-permute-start | bytes 1572872 | tf_op jit(solution)/shard_map/ppermute | solution.py:35
  46.5 2.0 %collective-permute-start.9 = (bf16[256,512]{1,0:T(8,128)(2,1)S(1)}, bf16[256,512]{1,0:T(8,128)(2,1)S(1)}, u32[]{:S(2)}, u32[]{:S(2)}) collective-permute-start(bf16[256,512]{1,0:T(8,128)(2,1)S(1)} %get-tuple-element.63), channel_id=1, source_target_pairs={{0,1},{1,0},{2,3},{3,2},{4,5},{5,4},{6,7},{7,6},{8,9},{9,8},{10,11... | collective-permute-start | bytes 786440 | tf_op jit(solution)/shard_map/ppermute | solution.py:39
  46.6 4.3 %collective-permute-start.10 = (bf16[256,512]{1,0:T(8,128)(2,1)S(1)}, bf16[256,512]{1,0:T(8,128)(2,1)S(1)}, u32[]{:S(2)}, u32[]{:S(2)}) collective-permute-start(bf16[256,512]{1,0:T(8,128)(2,1)S(1)} %get-tuple-element.67), channel_id=1, source_target_pairs={{0,1},{1,0},{2,3},{3,2},{4,5},{5,4},{6,7},{7,6},{8,9},{9,8},{10,11... | collective-permute-start | bytes 786440 | tf_op jit(solution)/shard_map/ppermute | solution.py:39
  49.6 1.4 %collective-permute-start.11 = (bf16[128,512]{1,0:T(8,128)(2,1)S(1)}, bf16[128,512]{1,0:T(8,128)(2,1)S(1)}, u32[]{:S(2)}, u32[]{:S(2)}) collective-permute-start(bf16[128,512]{1,0:T(8,128)(2,1)S(1)} %get-tuple-element.68), channel_id=1, source_target_pairs={{0,1},{1,0},{2,3},{3,2},{4,5},{5,4},{6,7},{7,6},{8,9},{9,8},{10,11... | collective-permute-start | bytes 393224 | tf_op jit(solution)/shard_map/ppermute | solution.py:39
  49.7 1.5 %collective-permute-start.12 = (bf16[128,512]{1,0:T(8,128)(2,1)S(1)}, bf16[128,512]{1,0:T(8,128)(2,1)S(1)}, u32[]{:S(2)}, u32[]{:S(2)}) collective-permute-start(bf16[128,512]{1,0:T(8,128)(2,1)S(1)} %get-tuple-element.69), channel_id=1, source_target_pairs={{0,1},{1,0},{2,3},{3,2},{4,5},{5,4},{6,7},{7,6},{8,9},{9,8},{10,11... | collective-permute-start | bytes 393224 | tf_op jit(solution)/shard_map/ppermute | solution.py:39
  51.3 9.3 %collective-permute-start.13 = (bf16[576,256]{1,0:T(8,128)(2,1)S(1)}, bf16[576,256]{1,0:T(8,128)(2,1)S(1)}, u32[]{:S(2)}, u32[]{:S(2)}) collective-permute-start(bf16[576,256]{1,0:T(8,128)(2,1)S(1)} %get-tuple-element.71), channel_id=1, source_target_pairs={{0,2},{1,3},{2,0},{3,1},{4,6},{5,7},{6,4},{7,5},{8,10},{9,11},{10,... | collective-permute-start | bytes 884744 | tf_op jit(solution)/shard_map/ppermute | solution.py:39
  56.4 1.6 %collective-permute-start.17 = (bf16[144,512]{1,0:T(8,128)(2,1)S(1)}, bf16[144,512]{1,0:T(8,128)(2,1)S(1)}, u32[]{:S(2)}, u32[]{:S(2)}) collective-permute-start(bf16[144,512]{1,0:T(8,128)(2,1)S(1)} %get-tuple-element.78), channel_id=1, source_target_pairs={{0,1},{1,0},{2,3},{3,2},{4,5},{5,4},{6,7},{7,6},{8,9},{9,8},{10,11... | collective-permute-start | bytes 442376 | tf_op jit(solution)/shard_map/ppermute | solution.py:39
  56.5 1.5 %collective-permute-start.16 = (bf16[128,512]{1,0:T(8,128)(2,1)S(1)}, bf16[128,512]{1,0:T(8,128)(2,1)S(1)}, u32[]{:S(2)}, u32[]{:S(2)}) collective-permute-start(bf16[128,512]{1,0:T(8,128)(2,1)S(1)} %get-tuple-element.77), channel_id=1, source_target_pairs={{0,1},{1,0},{2,3},{3,2},{4,5},{5,4},{6,7},{7,6},{8,9},{9,8},{10,11... | collective-permute-start | bytes 393224 | tf_op jit(solution)/shard_map/ppermute | solution.py:39
  58.1 8.1 %collective-permute-start.18 = (bf16[256,256]{1,0:T(8,128)(2,1)S(1)}, bf16[256,256]{1,0:T(8,128)(2,1)S(1)}, u32[]{:S(2)}, u32[]{:S(2)}) collective-permute-start(bf16[256,256]{1,0:T(8,128)(2,1)S(1)} %get-tuple-element.81), channel_id=1, source_target_pairs={{0,2},{1,3},{2,0},{3,1},{4,6},{5,7},{6,4},{7,5},{8,10},{9,11},{10,... | collective-permute-start | bytes 393224 | tf_op jit(solution)/shard_map/ppermute | solution.py:39
  58.8 7.5 %collective-permute-start.19 = (bf16[208,256]{1,0:T(8,128)(2,1)S(1)}, bf16[208,256]{1,0:T(8,128)(2,1)S(1)}, u32[]{:S(2)}, u32[]{:S(2)}) collective-permute-start(bf16[208,256]{1,0:T(8,128)(2,1)S(1)} %get-tuple-element.82), channel_id=1, source_target_pairs={{0,2},{1,3},{2,0},{3,1},{4,6},{5,7},{6,4},{7,5},{8,10},{9,11},{10,... | collective-permute-start | bytes 319496 | tf_op jit(solution)/shard_map/ppermute | solution.py:39
